TPU v7x, 32 devices: a whole 2x2x4 slice. The times are simulated.
32 devices in a mesh: dp: 2 (over x), expert: 16 (over z, y, core).
Axes of the slice: x: 2, y: 2, z: 4, core: 2. Of those that a mesh axis runs over, the one named last changes fastest.
Arguments:
- tokens: bfloat16 [4096, 2048], P(('dp', 'expert')), may hold values from -6 to 6
- out_grad: bfloat16 [4096, 2048], P(('dp', 'expert')), may hold values from -6 to 6
- route_gates: float32 [4096, 2], P(('dp', 'expert')), may hold values from 0.1 to 1
- route_slot: int32 [4096, 2], P(('dp', 'expert')), may hold values from 0 to 15, all different within a row; in each aligned block of 128 rows (0 to 127, 128 to 255, ...) at most 20 rows name the same one
- gate_weight: bfloat16 [16, 2048, 768], P('expert', 'dp'), may hold values from -0.125 to 0.125
- up_weight: bfloat16 [16, 2048, 768], P('expert', 'dp'), may hold values from -0.125 to 0.125
- down_weight: bfloat16 [16, 2048, 768], P('expert', 'dp'), may hold values from -0.21875 to 0.21875
Outputs:
- moe_out: bfloat16 [4096, 2048], P(('dp', 'expert'))
- token_grad: bfloat16 [4096, 2048], P(('dp', 'expert'))
- down_grad: bfloat16 [16, 2048, 768], P('expert', 'dp')
Inputs may be any that keep to these rules, and one draw needn't show every extreme that they name: `route_slot`: the 2 routes of a token name different slots. At most 20 routes of the tokens of one device name one slot, and in every draw some device sends exactly 20 routes to some slot.
All inputs are finite; a program needn't handle non-finite values.
Results may differ from a plain program's by a relative error of at most 0.014.
Values may be sent and summed in bfloat16 or wider, within the bound.
No kernel may reach another device: no remote copies, remote signals or barrier semaphores. Data moves between devices by JAX's collectives and lax.ppermute only.
A program may use at most 64 MiB of HBM per device.

v0:
```python
import jax
import jax.numpy as jnp
from jax import lax
from jax.sharding import PartitionSpec as P


def expert_forward(rows_in, w_gate, w_up, w_down):
    gate_proj = jnp.dot(rows_in, w_gate, preferred_element_type=jnp.float32)
    up_proj = jnp.dot(rows_in, w_up, preferred_element_type=jnp.float32)
    sigma_gate = jax.nn.sigmoid(gate_proj)
    activated = gate_proj * sigma_gate
    hidden = (activated * up_proj).astype(jnp.bfloat16)
    outputs = lax.dot_general(
        hidden, w_down, (((1,), (1,)), ((), ())), preferred_element_type=jnp.float32
    ).astype(jnp.bfloat16)
    return (outputs, gate_proj, up_proj, hidden)


def expert_backward(rows_grad, gate_proj, up_proj, w_gate, w_up, w_down):
    grad_hidden = jnp.dot(rows_grad, w_down, preferred_element_type=jnp.float32)
    sigma_gate = jax.nn.sigmoid(gate_proj)
    activated = gate_proj * sigma_gate
    grad_gate = (
        grad_hidden * up_proj * sigma_gate * (1.0 + gate_proj * (1.0 - sigma_gate))
    ).astype(jnp.bfloat16)
    grad_up = (grad_hidden * activated).astype(jnp.bfloat16)
    contract_dims = (((1,), (1,)), ((), ()))
    summed = lax.dot_general(
        grad_gate, w_gate, contract_dims, preferred_element_type=jnp.float32
    ) + lax.dot_general(grad_up, w_up, contract_dims, preferred_element_type=jnp.float32)
    return summed.astype(jnp.bfloat16)


def per_device(tokens, out_grad, route_gates, route_slot, gate_weight, up_weight, down_weight):
    tok_dev, model_width = tokens.shape
    route_count = route_slot.shape[1]
    peer_count = lax.axis_size("expert")
    capacity = max(2, (5 * tok_dev * route_count + 4 * peer_count - 1) // (4 * peer_count))
    route_total = tok_dev * route_count
    send_rows = peer_count * capacity
    flat_slot = route_slot.reshape(-1)
    onehot = (flat_slot[:, None] == jnp.arange(peer_count, dtype=jnp.int32)[None, :]).astype(
        jnp.int32
    )
    slot_rank = jnp.sum((jnp.cumsum(onehot, axis=0) - onehot) * onehot, axis=1)
    send_index = flat_slot * capacity + slot_rank
    route_of_row = (
        jnp.full((send_rows,), route_total, jnp.int32)
        .at[send_index]
        .set(jnp.arange(route_total, dtype=jnp.int32))
    )
    filled = route_of_row < route_total
    safe_route = jnp.where(filled, route_of_row, 0)
    token_row = safe_route // route_count
    gate_value = jnp.where(filled, route_gates.reshape(-1)[safe_route], 0.0)
    rows_in = jnp.where(filled[:, None], tokens[token_row], jnp.zeros((), tokens.dtype))
    rows_in = rows_in.reshape(peer_count, capacity, model_width)
    rows_grad = (gate_value[:, None] * out_grad[token_row].astype(jnp.float32)).astype(jnp.bfloat16)
    rows_grad = rows_grad.reshape(peer_count, capacity, model_width)
    full_gate, full_up, full_down = (
        lax.all_gather(gate_weight, "dp", axis=1, tiled=True),
        lax.all_gather(up_weight, "dp", axis=1, tiled=True),
        lax.all_gather(down_weight, "dp", axis=1, tiled=True),
    )
    w_gate = full_gate[0]
    w_up = full_up[0]
    w_down = full_down[0]
    item_shape = (peer_count, capacity, model_width)
    received = lax.all_to_all(rows_in, "expert", split_axis=0, concat_axis=0, tiled=True)
    outputs, gate_proj, up_proj, hidden_saved = expert_forward(
        received.reshape(-1, model_width), w_gate, w_up, w_down
    )
    out_back = lax.all_to_all(
        outputs.reshape(item_shape), "expert", split_axis=0, concat_axis=0, tiled=True
    )
    grad_in = lax.all_to_all(rows_grad, "expert", split_axis=0, concat_axis=0, tiled=True)
    grad_rows = expert_backward(
        grad_in.reshape(-1, model_width), gate_proj, up_proj, w_gate, w_up, w_down
    )
    grad_back = lax.all_to_all(
        grad_rows.reshape(item_shape), "expert", split_axis=0, concat_axis=0, tiled=True
    )
    grad_flat = grad_in.reshape(-1, model_width)
    down_share = lax.psum_scatter(
        lax.dot_general(
            grad_flat, hidden_saved, (((0,), (0,)), ((), ())), preferred_element_type=jnp.float32
        ).astype(jnp.bfloat16),
        "dp",
        scatter_dimension=0,
        tiled=True,
    )
    down_grad = down_share[None]
    out_routes = out_back.reshape(send_rows, model_width)[send_index].astype(jnp.float32)
    out_routes = out_routes.reshape(tok_dev, route_count, model_width)
    moe_out = jnp.sum(route_gates[:, :, None] * out_routes, axis=1).astype(jnp.bfloat16)
    grad_routes = grad_back.reshape(send_rows, model_width)[send_index].astype(jnp.float32)
    token_grad = jnp.sum(grad_routes.reshape(tok_dev, route_count, model_width), axis=1).astype(
        jnp.bfloat16
    )
    return (moe_out, token_grad, down_grad)


def solution(mesh):
    placed = (
        P(("dp", "expert"), None),
        P(("dp", "expert"), None),
        P(("dp", "expert"), None),
        P(("dp", "expert"), None),
        P("expert", "dp", None),
        P("expert", "dp", None),
        P("expert", "dp", None),
    )
    return jax.shard_map(
        per_device,
        mesh=mesh,
        in_specs=placed,
        out_specs=(P(("dp", "expert"), None), P(("dp", "expert"), None), P("expert", "dp", None)),
        check_vma=False,
    )
```

profile of v0, /device:TPU:17, one launch (start us, length us, event | category | flops | bytes accessed | tf_op | source)
XLA Modules:
  0.0 259.0 jit_solution(17634529206303139890)
XLA Ops:
  7.2 0.7 all-gather.4.cloned.1.call-update
  8.0 0.7 all-gather.6.cloned.1.call-update
  8.8 0.1 eq.29
  8.9 0.1 eq.25
  9.2 0.1 mul.63
  9.4 0.6 reduce-window.6
  9.9 0.2 slice_reduce_fusion
  10.3 1.4 scatter_custom_fusion
  11.8 2.4 gather_fusion
  14.3 0.3 gather.20
  14.6 1.3 broadcast_select_fusion
  15.9 6.6 %all-to-all-start = ((bf16[16,20,2048]{2,1,0:T(8,128)(2,1)}), bf16[16,20,2048]{2,1,0:T(8,128)(2,1)S(1)}, u32[]{:S(2)}, u32[]{:S(2)}) async-start(bf16[16,20,2048]{2,1,0:T(8,128)(2,1)} %broadcast_select_fusion), calls=%async_computation | async-start | bytes 3145728 | tf_op jit(solution)/shard_map/all_to_all | solution.py:69
  22.7 0.1 reshape.103
  22.8 2.5 gather_fusion.2
  25.4 3.0 %gather_fusion.3 = bf16[320,2048]{1,0:T(8,128)(2,1)} fusion(bf16[128,2048]{1,0:T(8,128)(2,1)S(1)} %copy-done.1, s32[1024]{0:T(1024)S(1)} %pad_clamp_fusion.2), kind=kCustom, calls=%fused_computation.3 | custom fusion | bytes 2622720 | tf_op jit(solution)/shard_map/gather | solution.py:58
  28.4 3.3 %reshape.108 = f32[16,20,2048]{2,1,0:T(8,128)} reshape(bf16[320,2048]{1,0:T(8,128)(2,1)} %gather_fusion.3) | data formatting | bytes 3932160 | tf_op jit(solution)/shard_map/convert_element_type | solution.py:58
  31.7 3.3 %multiply_convert_fusion = bf16[16,20,2048]{2,1,0:T(8,128)(2,1)} fusion(f32[16,20,2048]{2,1,0:T(8,128)} %reshape.108, f32[16,20]{1,0:T(8,128)S(1)} %mul.68), kind=kLoop, calls=%fused_computation.19 | loop fusion | flops 1310720 | bytes 3933440 | tf_op jit(solution)/shard_map/convert_element_type | solution.py:58
  35.0 23.4 %all-to-all-done = bf16[16,20,2048]{2,1,0:T(8,128)(2,1)S(1)} async-done(((bf16[16,20,2048]{2,1,0:T(8,128)(2,1)}), bf16[16,20,2048]{2,1,0:T(8,128)(2,1)S(1)}, u32[]{:S(2)}, u32[]{:S(2)}) %all-to-all-start) | async-done | bytes 1310752 | tf_op jit(solution)/shard_map/all_to_all | solution.py:69
  58.5 5.2 %all-to-all-start.2 = ((bf16[16,20,2048]{2,1,0:T(8,128)(2,1)}), bf16[16,20,2048]{2,1,0:T(8,128)(2,1)}, u32[]{:S(2)}, u32[]{:S(2)}) async-start(bf16[16,20,2048]{2,1,0:T(8,128)(2,1)} %multiply_convert_fusion), calls=%async_computation.2 | async-start | bytes 3145728 | tf_op jit(solution)/shard_map/all_to_all | solution.py:76
  63.7 0.7 all-gather.8.cloned.1.call-update
  64.4 1.2 reshape.100
  65.6 34.0 %all-to-all-done.2 = bf16[16,20,2048]{2,1,0:T(8,128)(2,1)} async-done(((bf16[16,20,2048]{2,1,0:T(8,128)(2,1)}), bf16[16,20,2048]{2,1,0:T(8,128)(2,1)}, u32[]{:S(2)}, u32[]{:S(2)}) %all-to-all-start.2) | async-done | bytes 1310752 | tf_op jit(solution)/shard_map/all_to_all | solution.py:76
  99.7 2.3 reshape.104
  102.0 4.0 %fusion.10 = f32[320,768]{1,0:T(8,128)} fusion(bf16[320,2048]{1,0:T(8,128)(2,1)S(1)} %copy-done.3, bf16[1,2048,768]{2,1,0:T(8,128)(2,1)} %all-gather.4.cloned.1.call-done), kind=kOutput, calls=%fused_computation.17 | convolution fusion | flops 1006632960 | bytes 5439488 | tf_op jit(solution)/shard_map/dot_general | solution.py:8
  106.0 4.3 %multiply_convert_fusion.3 = (bf16[320,768]{1,0:T(8,128)(2,1)S(1)}, f32[320,768]{1,0:T(8,128)}) fusion(f32[320,768]{1,0:T(8,128)} %fusion.10, bf16[320,2048]{1,0:T(8,128)(2,1)S(1)} %copy-done.3, bf16[1,2048,768]{2,1,0:T(8,128)(2,1)} %all-gather.6.cloned.1.call-done), kind=kOutput, calls=%fused_computation.27 | convolution fusion | flops 1008107520 | bytes 6914048 | tf_op jit(solution)/shard_map/dot_general | solution.py:9
  110.3 0.8 copy-done.10
  111.1 3.5 %convolution_convert_fusion = bf16[2048,768]{1,0:T(8,128)(2,1)} fusion(bf16[320,2048]{1,0:T(8,128)(2,1)S(1)} %reshape.104, bf16[320,768]{1,0:T(8,128)(2,1)S(1)} %get-tuple-element.5), kind=kOutput, calls=%fused_computation.6 | convolution fusion | flops 1008205824 | bytes 4947968 | tf_op jit(solution)/shard_map/dot_general | solution.py:85
  114.7 34.0 %all-gather.8.cloned.1.call-done = bf16[1,2048,768]{2,1,0:T(8,128)(2,1)} async-done(((bf16[1,1024,768]{2,1,0:T(8,128)(2,1)}), bf16[1,2048,768]{2,1,0:T(8,128)(2,1)}) %all-gather.8.cloned.1.call-update) | async-done | bytes 3145744 | tf_op jit(solution)/shard_map/all_gather | solution.py:63
  148.6 3.3 %fusion.18 = bf16[320,2048]{1,0:T(8,128)(2,1)S(1)} fusion(bf16[320,768]{1,0:T(8,128)(2,1)} %copy-done.10, bf16[1,2048,768]{2,1,0:T(8,128)(2,1)} %all-gather.8.cloned.1.call-done), kind=kOutput, calls=%fused_computation.22 | convolution fusion | flops 1007288320 | bytes 4947968 | tf_op jit(solution)/shard_map/dot_general | solution.py:13
  151.9 1.3 reshape.101
  153.2 6.4 %all-to-all-start.1 = ((bf16[16,20,2048]{2,1,0:T(8,128)(2,1)}), bf16[16,20,2048]{2,1,0:T(8,128)(2,1)S(1)}, u32[]{:S(2)}, u32[]{:S(2)}) async-start(bf16[16,20,2048]{2,1,0:T(8,128)(2,1)} %reshape.101), calls=%async_computation.1 | async-start | bytes 3145728 | tf_op jit(solution)/shard_map/all_to_all | solution.py:73
  159.6 3.2 %fusion = f32[320,768]{1,0:T(8,128)S(1)} fusion(bf16[320,2048]{1,0:T(8,128)(2,1)S(1)} %reshape.104, bf16[1,2048,768]{2,1,0:T(8,128)(2,1)} %all-gather.8.cloned.1.call-done), kind=kOutput, calls=%fused_computation.7 | convolution fusion | flops 1006632960 | bytes 5439488 | tf_op jit(solution)/shard_map/dot_general | solution.py:20
  162.9 1.3 fusion.4
  164.1 0.6 copy-done.6
  164.7 0.3 copy-done.9
  165.0 1.3 fusion.15
  166.3 1.3 reshape.105
  167.6 27.8 %all-to-all-done.1 = bf16[16,20,2048]{2,1,0:T(8,128)(2,1)S(1)} async-done(((bf16[16,20,2048]{2,1,0:T(8,128)(2,1)}), bf16[16,20,2048]{2,1,0:T(8,128)(2,1)S(1)}, u32[]{:S(2)}, u32[]{:S(2)}) %all-to-all-start.1) | async-done | bytes 1310752 | tf_op jit(solution)/shard_map/all_to_all | solution.py:73
  195.5 5.2 %all-to-all-start.3 = ((bf16[16,20,2048]{2,1,0:T(8,128)(2,1)}), bf16[16,20,2048]{2,1,0:T(8,128)(2,1)}, u32[]{:S(2)}, u32[]{:S(2)}) async-start(bf16[16,20,2048]{2,1,0:T(8,128)(2,1)} %reshape.105), calls=%async_computation.3 | async-start | bytes 3145728 | tf_op jit(solution)/shard_map/all_to_all | solution.py:80
  200.7 0.3 reshape.102
  201.0 1.4 gather_fusion.1
  202.4 2.4 reshape.107
  204.7 32.0 %all-to-all-done.3 = bf16[16,20,2048]{2,1,0:T(8,128)(2,1)} async-done(((bf16[16,20,2048]{2,1,0:T(8,128)(2,1)}), bf16[16,20,2048]{2,1,0:T(8,128)(2,1)}, u32[]{:S(2)}, u32[]{:S(2)}) %all-to-all-start.3) | async-done | bytes 1310752 | tf_op jit(solution)/shard_map/all_to_all | solution.py:80
  236.7 2.3 reshape.106
  239.0 2.3 gather_fusion.4
  241.3 2.7 %gather.25 = bf16[128,2,2048]{2,1,0:T(2,128)(2,1)} reshape(bf16[256,2048]{1,0:T(8,128)(2,1)} %gather_fusion.4) | data formatting | bytes 2097152 | tf_op jit(solution)/shard_map/gather | solution.py:96
  244.0 4.6 %reduce_sum.35 = bf16[128,2048]{1,0:T(8,128)(2,1)} reduce(bf16[128,2,2048]{2,1,0:T(2,128)(2,1)} %gather.25, bf16[]{:T(256)} %constant.33.clone.1), dimensions={1}, to_apply=%region_5.6 | reduce | flops 262144 | bytes 1572866 | tf_op jit(solution)/shard_map/reduce_sum | solution.py:97
  248.6 3.9 %multiply_reduce_fusion = bf16[128,2048]{1,0:T(8,128)(2,1)} fusion(f32[128,2,2048]{2,1,0:T(2,128)S(1)} %copy-done.2, f32[128,2]{1,0:T(8,128)S(1)} %copy.11), kind=kLoop, calls=%fused_computation.23 | loop fusion | flops 786432 | bytes 2622464 | tf_op jit(solution)/shard_map/reduce_sum | solution.py:95
  (45 shorter events, 0.9 us)
Async XLA Ops:
  7.2 4.7 %copy-start = (bf16[128,2048]{1,0:T(8,128)(2,1)S(1)}, bf16[128,2048]{1,0:T(8,128)(2,1)}, u32[]{:S(2)}) copy-start(bf16[128,2048]{1,0:T(8,128)(2,1)} %param.7) | copy-start | bytes 1572868
  7.2 94.8 %all-gather.4.cloned.1.call-start = ((), (), s32[]{:S(2)}) async-start(), calls=%async_computation.5 | async-start | bytes 4718592 | tf_op jit(solution)/shard_map/all_gather | solution.py:61
  7.2 1.4 copy-start.4
  7.9 98.1 %all-gather.6.cloned.1.call-start = ((), (), s32[]{:S(2)}) async-start(), calls=%async_computation.6 | async-start | bytes 4718592 | tf_op jit(solution)/shard_map/all_gather | solution.py:62
  15.9 6.6 %copy-start.5 = (f32[128,2]{0,1:T(2,128)S(1)}, f32[128,2]{0,1:T(2,128)}, u32[]{:S(2)}) copy-start(f32[128,2]{0,1:T(2,128)} %param.9) | copy-start | bytes 3076
  15.9 42.5 %all-to-all-start = ((bf16[16,20,2048]{2,1,0:T(8,128)(2,1)}), bf16[16,20,2048]{2,1,0:T(8,128)(2,1)S(1)}, u32[]{:S(2)}, u32[]{:S(2)}) async-start(bf16[16,20,2048]{2,1,0:T(8,128)(2,1)} %broadcast_select_fusion), calls=%async_computation | async-start | bytes 3145728 | tf_op jit(solution)/shard_map/all_to_all | solution.py:69
  22.6 2.8 %copy-start.1 = (bf16[128,2048]{1,0:T(8,128)(2,1)S(1)}, bf16[128,2048]{1,0:T(8,128)(2,1)}, u32[]{:S(2)}) copy-start(bf16[128,2048]{1,0:T(8,128)(2,1)} %param.8) | copy-start | bytes 1572868
  58.5 41.2 %all-to-all-start.2 = ((bf16[16,20,2048]{2,1,0:T(8,128)(2,1)}), bf16[16,20,2048]{2,1,0:T(8,128)(2,1)}, u32[]{:S(2)}, u32[]{:S(2)}) async-start(bf16[16,20,2048]{2,1,0:T(8,128)(2,1)} %multiply_convert_fusion), calls=%async_computation.2 | async-start | bytes 3145728 | tf_op jit(solution)/shard_map/all_to_all | solution.py:76
  63.6 85.0 %all-gather.8.cloned.1.call-start = ((), (), s32[]{:S(2)}) async-start(), calls=%async_computation.7 | async-start | bytes 4718592 | tf_op jit(solution)/shard_map/all_gather | solution.py:63
  64.4 188.1 %reduce-scatter.2.cloned.1.call-start = ((), (), s32[]{:S(2)}) async-start(), calls=%async_computation.8 | async-start | bytes 4718592 | tf_op jit(solution)/shard_map/reduce_scatter | solution.py:84
  65.6 36.3 %copy-start.3 = (bf16[320,2048]{1,0:T(8,128)(2,1)S(1)}, bf16[320,2048]{1,0:T(8,128)(2,1)}, u32[]{:S(2)}) copy-start(bf16[320,2048]{1,0:T(8,128)(2,1)} %reshape.100) | copy-start | bytes 3932164
  110.3 0.8 copy-start.10
  153.2 42.3 %all-to-all-start.1 = ((bf16[16,20,2048]{2,1,0:T(8,128)(2,1)}), bf16[16,20,2048]{2,1,0:T(8,128)(2,1)S(1)}, u32[]{:S(2)}, u32[]{:S(2)}) async-start(bf16[16,20,2048]{2,1,0:T(8,128)(2,1)} %reshape.101), calls=%async_computation.1 | async-start | bytes 3145728 | tf_op jit(solution)/shard_map/all_to_all | solution.py:73
  159.6 3.2 %copy-start.7 = (bf16[1,2048,768]{2,1,0:T(8,128)(2,1)S(1)}, bf16[1,2048,768]{2,1,0:T(8,128)(2,1)}, u32[]{:S(2)}) copy-start(bf16[1,2048,768]{2,1,0:T(8,128)(2,1)} %all-gather.6.cloned.1.call-done) | copy-start | bytes 9437188
  159.6 3.2 %copy-start.8 = (f32[320,768]{1,0:T(8,128)S(1)}, f32[320,768]{1,0:T(8,128)}, u32[]{:S(2)}) copy-start(f32[320,768]{1,0:T(8,128)} %fusion.10) | copy-start | bytes 2949124
  162.8 1.9 copy-start.6
  162.8 2.1 copy-start.9
  195.5 41.2 %all-to-all-start.3 = ((bf16[16,20,2048]{2,1,0:T(8,128)(2,1)}), bf16[16,20,2048]{2,1,0:T(8,128)(2,1)}, u32[]{:S(2)}, u32[]{:S(2)}) async-start(bf16[16,20,2048]{2,1,0:T(8,128)(2,1)} %reshape.105), calls=%async_computation.3 | async-start | bytes 3145728 | tf_op jit(solution)/shard_map/all_to_all | solution.py:80
  241.3 7.3 %copy-start.2 = (f32[128,2,2048]{2,1,0:T(2,128)S(1)}, f32[128,2,2048]{2,1,0:T(2,128)}, u32[]{:S(2)}) copy-start(f32[128,2,2048]{2,1,0:T(2,128)} %reshape.107) | copy-start | bytes 6291460
Sparse Core Ops, SparseCore 0:
  9.6 45.9 all-gather.3
  57.1 44.9 all-gather.5
  103.7 44.9 all-gather.7
  151.3 43.3 reduce-scatter.1
where the time goes:
time: 260 us; the launch traced here: 259 us
  waiting for transfers between devices  153 us (59%)
  local copies, waits for them, and re-layouts  33.3 us (13%)
  starting transfers between devices  23.5 us (9%)
  matrix products  20.9 us (8%)
  between operations  14.1 us (5%)
  other arithmetic  13.9 us (5%)
    all_to_all x1, waiting for transfers between devices, per_device(): lax.all_to_all(rows_grad, 'expert', split_axis=0, concat_axis=0, tiled=True)  34 us
    all_gather x1, waiting for transfers between devices, per_device(): lax.all_gather(down_weight, 'dp', axis=1, tiled=True)  34 us
    all_to_all x1, waiting for transfers between devices, per_device(): lax.all_to_all(grad_rows.reshape(item_shape), 'expert', split_axis=0, con...  32 us
    all_to_all x1, waiting for transfers between devices, per_device(): lax.all_to_all(outputs.reshape(item_shape), 'expert', split_axis=0, conca...  27.8 us
    all_to_all x1, waiting for transfers between devices, per_device(): lax.all_to_all(rows_in, 'expert', split_axis=0, concat_axis=0, tiled=True)  23.4 us
    all_to_all x1, starting transfers between devices, per_device(): lax.all_to_all(rows_in, 'expert', split_axis=0, concat_axis=0, tiled=True)  6.63 us
    all_to_all x1, starting transfers between devices, per_device(): lax.all_to_all(outputs.reshape(item_shape), 'expert', split_axis=0, conca...  6.36 us
  transfers between devices with their start and end apart: 8, of which 5 were waited for; matrix products, arithmetic and copies ran while one was open for 26% of the time, Pallas kernels for 0%

commit v1 on v0

--- a/solution.py
+++ b/solution.py
@@ -1,7 +1,387 @@
+import functools
+
 import jax
 import jax.numpy as jnp
 from jax import lax
+from jax.experimental import pallas as pl
+from jax.experimental.pallas import tpu as pltpu
 from jax.sharding import PartitionSpec as P
+
+F32, BF16, I32 = jnp.float32, jnp.bfloat16, jnp.int32
+NT = (((1,), (1,)), ((), ()))
+TN = (((0,), (0,)), ((), ()))
+
+
+def mm(a, b, dims=(((1,), (0,)), ((), ()))):
+    return lax.dot_general(a, b, dims, preferred_element_type=F32)
+
+
+def ones_where(mask):
+    return jnp.where(mask, 1.0, 0.0).astype(BF16)
+
+
+def iota(shape, dim):
+    return lax.broadcasted_iota(I32, shape, dim)
+
+
+def call(kernel, out_shape, grid, in_specs, out_specs, scratch=(), flops=0, moved=0, vmem_mib=28):
+    return pl.pallas_call(
+        kernel,
+        out_shape=out_shape,
+        grid=grid,
+        in_specs=in_specs,
+        out_specs=out_specs,
+        scratch_shapes=list(scratch),
+        cost_estimate=pl.CostEstimate(flops=flops, bytes_accessed=moved, transcendentals=0),
+        compiler_params=pltpu.CompilerParams(vmem_limit_bytes=vmem_mib * 2**20),
+    )
+
+
+def whole(shape):
+    return pl.BlockSpec(shape, lambda *_: (0,) * len(shape))
+
+
+SCALAR = pl.BlockSpec(memory_space=pltpu.SMEM)
+
+
+def places_in_lanes(slots, peers, cap):
+    top, count = slots.shape
+    named = [jnp.where(iota((peers, count), 0) == slots[k : k + 1, :], 1.0, 0.0) for k in range(top)]
+    earlier = ones_where(iota((count, count), 0) < iota((count, count), 1))
+    before = mm(sum(named).astype(BF16), earlier)
+    ranks = [jnp.sum(before * each, axis=0, keepdims=True).astype(I32) for each in named]
+    return [slots[k : k + 1, :] * (2 * cap) + ranks[k] for k in range(top)]
+
+
+def places_in_rows(slots, peers, cap):
+    count, top = slots.shape
+    named = [jnp.where(iota((count, peers), 1) == slots[:, k : k + 1], 1.0, 0.0) for k in range(top)]
+    earlier = ones_where(iota((count, count), 1) < iota((count, count), 0))
+    before = mm(earlier, sum(named).astype(BF16))
+    ranks = [jnp.sum(before * each, axis=1, keepdims=True).astype(I32) for each in named]
+    return [slots[:, k : k + 1] * (2 * cap) + ranks[k] for k in range(top)]
+
+
+def send_tokens_kernel(peers, cap, slots_ref, tok_ref, out_ref):
+    places = places_in_lanes(slots_ref[...], peers, cap)
+    rows, count = 2 * cap * peers, slots_ref.shape[1]
+    at = iota((rows, count), 0)
+    halves = [sum(jnp.where(at == place + h * cap, 1.0, 0.0) for place in places) for h in range(2)]
+    pick = jnp.concatenate(halves, axis=1).astype(BF16)
+    width = out_ref.shape[2]
+    for part in range(2):
+        lo = part * 2 * width
+        both = jnp.concatenate(
+            [tok_ref[:, lo : lo + width], tok_ref[:, lo + width : lo + 2 * width]], axis=0
+        )
+        out_ref[part] = mm(pick, both).astype(BF16)
+
+
+def send_grads_kernel(peers, cap, slots_ref, gates_ref, grad_ref, out_ref):
+    places = places_in_lanes(slots_ref[...], peers, cap)
+    rows, count = 2 * cap * peers, slots_ref.shape[1]
+    half = out_ref.shape[1]
+    at = iota((rows, count), 0)
+    gates = gates_ref[...]
+    picks = [
+        jnp.concatenate([jnp.where(at == place + h * cap, 1.0, 0.0) for h in range(2)], axis=1).astype(BF16)
+        for place in places
+    ]
+    step = min(512, half)
+    for lo in range(0, half, step):
+        total = None
+        for k, pick in enumerate(picks):
+            both = jnp.concatenate(
+                [
+                    (gates[:, k : k + 1] * grad_ref[:, c : c + step].astype(F32)).astype(BF16)
+                    for c in (lo, half + lo)
+                ],
+                axis=0,
+            )
+            rows_k = mm(pick, both)
+            total = rows_k if total is None else total + rows_k
+        out_ref[:, lo : lo + step] = total.astype(BF16)
+
+
+def partial_kernel(group_ref, target_ref, recv_ref, wg_ref, wu_ref, gate_ref, up_ref, send_ref, x_ref):
+    rows = gate_ref.shape[0]
+    width = recv_ref.shape[2]
+
+    @pl.when(pl.program_id(0) == 0)
+    def _():
+        pick = ones_where(iota((2 * rows, 2 * rows), 1) == target_ref[...])
+        for part in range(2):
+            for h in range(2):
+                x_ref[part * rows : (part + 1) * rows, h * width : (h + 1) * width] = mm(
+                    pick[h * rows : (h + 1) * rows], recv_ref[part]
+                ).astype(BF16)
+
+    group = group_ref[0]
+    mine = x_ref[pl.ds(pl.multiple_of(group * rows, 16), rows), :]
+    other = x_ref[pl.ds(pl.multiple_of((1 - group) * rows, 16), rows), :]
+    wg, wu = wg_ref[...], wu_ref[...]
+    send_ref[0] = mm(other, wg).astype(BF16)
+    send_ref[1] = mm(other, wu).astype(BF16)
+    gate_ref[...] = mm(mine, wg)
+    up_ref[...] = mm(mine, wu)
+
+
+def forward_kernel(
+    group_ref, target_ref, gate_ref, up_ref, recv_ref, own_ref, other_ref, hid_ref, out_ref, pick_ref, y_ref
+):
+    rows = hid_ref.shape[0]
+
+    @pl.when(pl.program_id(0) == 0)
+    def _():
+        pick_ref[...] = ones_where(iota((2 * rows, 2 * rows), 0) == target_ref[...])
+        gate = gate_ref[...] + recv_ref[0].astype(F32)
+        up = up_ref[...] + recv_ref[1].astype(F32)
+        hid_ref[...] = (gate * jax.nn.sigmoid(gate) * up).astype(BF16)
+
+    group = group_ref[0]
+    hidden = hid_ref[...]
+    y_ref[pl.ds(pl.multiple_of(group * rows, 16), rows), :] = mm(hidden, own_ref[...], NT).astype(BF16)
+    y_ref[pl.ds(pl.multiple_of((1 - group) * rows, 16), rows), :] = mm(hidden, other_ref[...], NT).astype(BF16)
+    out_ref[...] = mm(pick_ref[...], y_ref[...]).astype(BF16)
+
+
+def backward_kernel(
+    group_ref, target_ref, grad_ref, gate_ref, up_ref, recv_ref, own_ref, other_ref, out_ref, dy_ref
+):
+    rows = gate_ref.shape[0]
+
+    @pl.when(pl.program_id(0) == 0)
+    def _():
+        pick = ones_where(iota((2 * rows, 2 * rows), 1) == target_ref[...])
+        dy_ref[...] = mm(pick, grad_ref[...]).astype(BF16)
+
+    group = group_ref[0]
+    mine = dy_ref[pl.ds(pl.multiple_of(group * rows, 16), rows), :]
+    other = dy_ref[pl.ds(pl.multiple_of((1 - group) * rows, 16), rows), :]
+    d_hidden = mm(mine, own_ref[...]) + mm(other, other_ref[...])
+    gate = gate_ref[...] + recv_ref[0].astype(F32)
+    up = up_ref[...] + recv_ref[1].astype(F32)
+    sigma = jax.nn.sigmoid(gate)
+    out_ref[0] = (d_hidden * up * sigma * (1.0 + gate * (1.0 - sigma))).astype(BF16)
+    out_ref[1] = (d_hidden * (gate * sigma)).astype(BF16)
+
+
+def down_kernel(group_ref, dy_mine_ref, dy_other_ref, hid_ref, mine_ref, send_ref):
+    hidden = hid_ref[...]
+    send_ref[...] = mm(dy_other_ref[...], hidden, TN).astype(BF16)
+    mine_ref[...] = mm(dy_mine_ref[...], hidden, TN)
+
+
+def input_grad_kernel(group_ref, target_ref, own_ref, recv_ref, wg_ref, wu_ref, out_ref):
+    rows = own_ref.shape[1]
+    width = out_ref.shape[2]
+    mine = pl.program_id(0) == group_ref[0]
+    d_gate = jnp.where(mine, own_ref[0], recv_ref[0])
+    d_up = jnp.where(mine, own_ref[1], recv_ref[1])
+    halves = []
+    for h in range(2):
+        lo = h * width
+        halves.append(
+            (mm(d_gate, wg_ref[lo : lo + width, :], NT) + mm(d_up, wu_ref[lo : lo + width, :], NT)).astype(BF16)
+        )
+    pick = ones_where(iota((2 * rows, 2 * rows), 0) == target_ref[...])
+    out_ref[0] = mm(pick, jnp.concatenate(halves, axis=0)).astype(BF16)
+
+
+def combine_out_kernel(peers, cap, slots_ref, gates_ref, back_ref, out_ref):
+    places = places_in_rows(slots_ref[...], peers, cap)
+    count = slots_ref.shape[0]
+    rows, half = back_ref.shape
+    at = iota((count, rows), 1)
+    gates = gates_ref[...]
+    for h in range(2):
+        total = None
+        for k, place in enumerate(places):
+            term = gates[:, k : k + 1] * mm(ones_where(at == place + h * cap), back_ref[...])
+            total = term if total is None else total + term
+        out_ref[:, h * half : (h + 1) * half] = total.astype(BF16)
+
+
+def combine_grad_kernel(peers, cap, slots_ref, back_ref, out_ref):
+    places = places_in_rows(slots_ref[...], peers, cap)
+    count = slots_ref.shape[0]
+    _, rows, width = back_ref.shape
+    at = iota((count, rows), 1)
+    for h in range(2):
+        pick = sum(jnp.where(at == place + h * cap, 1.0, 0.0) for place in places).astype(BF16)
+        for part in range(2):
+            lo = (2 * part + h) * width
+            out_ref[:, lo : lo + width] = mm(pick, back_ref[part]).astype(BF16)
+
+
+def split_width(tokens, out_grad, route_gates, route_slot, gate_weight, up_weight, down_weight):
+    count, width = tokens.shape
+    top = route_slot.shape[1]
+    peers = lax.axis_size("expert")
+    cap = capacity_of(count, top, peers)
+    w_gate, w_up, w_down = gate_weight[0], up_weight[0], down_weight[0]
+    half, hidden_width = w_gate.shape
+    quarter = half // 2
+    rows = peers * cap
+    swap = [(0, 1), (1, 0)]
+    group = lax.axis_index("dp").astype(I32).reshape(1)
+    slots_t = route_slot.T
+    place = jnp.arange(rows, dtype=I32)
+    left = place + cap * (place // cap)
+    target = jnp.concatenate([left, left + cap])
+    target_col, target_row = target[:, None], target[None, :]
+    tile = min(256, hidden_width)
+
+    def shape(*dims, dtype=BF16):
+        return jax.ShapeDtypeStruct(dims, dtype)
+
+    one_step = (1,)
+    tok_send = call(
+        functools.partial(send_tokens_kernel, peers, cap),
+        shape(2, 2 * rows, quarter),
+        one_step,
+        [whole(slots_t.shape), whole(tokens.shape)],
+        whole((2, 2 * rows, quarter)),
+        flops=2 * 2 * rows * 2 * count * half,
+        moved=2 * (tokens.size + 2 * rows * half),
+    )(slots_t, tokens)
+    tok_recv = lax.all_to_all(
+        tok_send.reshape(2 * peers, 2 * cap, quarter), ("dp", "expert"), 0, 0, tiled=True
+    ).reshape(2, 2 * rows, quarter)
+    down_other = lax.ppermute(w_down, "dp", swap)
+    dy_send = call(
+        functools.partial(send_grads_kernel, peers, cap),
+        shape(2 * rows, half),
+        one_step,
+        [whole(slots_t.shape), whole(route_gates.shape), whole(out_grad.shape)],
+        whole((2 * rows, half)),
+        flops=2 * 2 * rows * 2 * count * half * top,
+        moved=2 * (out_grad.size + 2 * rows * half),
+    )(slots_t, route_gates, out_grad)
+    dy_recv = lax.all_to_all(
+        dy_send.reshape(peers, 2 * cap, half), "expert", 0, 0, tiled=True
+    ).reshape(2 * rows, half)
+
+    tiles = hidden_width // tile
+    part_block = pl.BlockSpec((rows, tile), lambda i: (0, i))
+    pair_block = pl.BlockSpec((2, rows, tile), lambda i: (0, 0, i))
+    weight_block = pl.BlockSpec((half, tile), lambda i: (0, i))
+    gate_mine, up_mine, part_send = call(
+        partial_kernel,
+        (shape(rows, hidden_width, dtype=F32), shape(rows, hidden_width, dtype=F32), shape(2, rows, hidden_width)),
+        (tiles,),
+        [SCALAR, whole((2 * rows, 1)), whole((2, 2 * rows, quarter)), weight_block, weight_block],
+        (part_block, part_block, pair_block),
+        [pltpu.VMEM((2 * rows, half), BF16)],
+        flops=2 * 2 * rows * half * hidden_width * 2,
+        moved=4 * half * hidden_width + 4 * rows * half,
+    )(group, target_col, tok_recv, w_gate, w_up)
+    part_recv = lax.ppermute(part_send, "dp", swap)
+
+    step = min(512, half)
+    down_rows = pl.BlockSpec((step, hidden_width), lambda i: (i, 0))
+    hidden, y_send = call(
+        forward_kernel,
+        (shape(rows, hidden_width), shape(2 * rows, half)),
+        (half // step,),
+        [
+            SCALAR,
+            whole((1, 2 * rows)),
+            whole((rows, hidden_width)),
+            whole((rows, hidden_width)),
+            whole((2, rows, hidden_width)),
+            down_rows,
+            down_rows,
+        ],
+        (whole((rows, hidden_width)), pl.BlockSpec((2 * rows, step), lambda i: (0, i))),
+        [pltpu.VMEM((2 * rows, 2 * rows), BF16), pltpu.VMEM((2 * rows, step), BF16)],
+        flops=2 * 2 * rows * half * hidden_width,
+        moved=4 * half * hidden_width + 4 * rows * half,
+    )(group, target_row, gate_mine, up_mine, part_recv, w_down, down_other)
+    y_back = lax.all_to_all(
+        y_send.reshape(peers, 2 * cap, half), "expert", 0, 0, tiled=True
+    ).reshape(2 * rows, half)
+
+    d_pair, dy_rows = call(
+        backward_kernel,
+        (shape(2, rows, hidden_width), shape(2 * rows, half)),
+        (tiles,),
+        [
+            SCALAR,
+            whole((2 * rows, 1)),
+            whole((2 * rows, half)),
+            part_block,
+            part_block,
+            pair_block,
+            weight_block,
+            weight_block,
+        ],
+        (pair_block, whole((2 * rows, half))),
+        flops=2 * 2 * rows * half * hidden_width,
+        moved=4 * half * hidden_width + 4 * rows * half,
+    )(group, target_col, dy_recv, gate_mine, up_mine, part_recv, w_down, down_other)
+    d_recv = lax.ppermute(d_pair, "dp", swap)
+    dx_send = call(
+        input_grad_kernel,
+        shape(2, 2 * rows, quarter),
+        (2,),
+        [
+            SCALAR,
+            whole((1, 2 * rows)),
+            whole((2, rows, hidden_width)),
+            whole((2, rows, hidden_width)),
+            whole((half, hidden_width)),
+            whole((half, hidden_width)),
+        ],
+        pl.BlockSpec((1, 2 * rows, quarter), lambda i: (i, 0, 0)),
+        flops=2 * 2 * rows * half * hidden_width * 2,
+        moved=4 * half * hidden_width + 4 * rows * half,
+    )(group, target_row, d_pair, d_recv, w_gate, w_up)
+    dx_back = lax.all_to_all(
+        dx_send.reshape(2 * peers, 2 * cap, quarter), ("dp", "expert"), 0, 0, tiled=True
+    ).reshape(2, 2 * rows, quarter)
+
+    strip = min(256, half)
+    dy_pair = dy_rows.reshape(2, rows, half)
+    dy_mine = lax.dynamic_index_in_dim(dy_pair, group[0], 0, keepdims=False)
+    dy_other = lax.dynamic_index_in_dim(dy_pair, 1 - group[0], 0, keepdims=False)
+    strip_block = pl.BlockSpec((rows, strip), lambda i: (0, i))
+    grad_block = pl.BlockSpec((strip, hidden_width), lambda i: (i, 0))
+    down_mine, down_send = call(
+        down_kernel,
+        (shape(half, hidden_width, dtype=F32), shape(half, hidden_width)),
+        (half // strip,),
+        [SCALAR, strip_block, strip_block, whole((rows, hidden_width))],
+        (grad_block, grad_block),
+        flops=2 * 2 * rows * half * hidden_width,
+        moved=6 * half * hidden_width + 4 * rows * half,
+    )(group, dy_mine, dy_other, hidden)
+    down_recv = lax.ppermute(down_send, "dp", swap)
+    down_grad = (down_mine + down_recv.astype(F32)).astype(BF16)[None]
+
+    moe_out = call(
+        functools.partial(combine_out_kernel, peers, cap),
+        shape(count, width),
+        one_step,
+        [whole(route_slot.shape), whole(route_gates.shape), whole((2 * rows, half))],
+        whole((count, width)),
+        flops=2 * 2 * rows * count * half * 2 * top,
+        moved=2 * (count * width + 2 * rows * half),
+    )(route_slot, route_gates, y_back)
+    token_grad = call(
+        functools.partial(combine_grad_kernel, peers, cap),
+        shape(count, width),
+        one_step,
+        [whole(route_slot.shape), whole((2, 2 * rows, quarter))],
+        whole((count, width)),
+        flops=2 * 2 * rows * count * half * 2,
+        moved=2 * (count * width + 2 * rows * half),
+    )(route_slot, dx_back)
+    return (moe_out, token_grad, down_grad)
+
+
+def capacity_of(count, top, peers):
+    return max(2, (5 * count * top + 4 * peers - 1) // (4 * peers))
 
 
 def expert_forward(rows_in, w_gate, w_up, w_down):
@@ -31,11 +411,11 @@
     return summed.astype(jnp.bfloat16)
 
 
-def per_device(tokens, out_grad, route_gates, route_slot, gate_weight, up_weight, down_weight):
+def gathered_weights(tokens, out_grad, route_gates, route_slot, gate_weight, up_weight, down_weight):
     tok_dev, model_width = tokens.shape
     route_count = route_slot.shape[1]
     peer_count = lax.axis_size("expert")
-    capacity = max(2, (5 * tok_dev * route_count + 4 * peer_count - 1) // (4 * peer_count))
+    capacity = capacity_of(tok_dev, route_count, peer_count)
     route_total = tok_dev * route_count
     send_rows = peer_count * capacity
     flat_slot = route_slot.reshape(-1)
@@ -100,6 +480,23 @@
     return (moe_out, token_grad, down_grad)
 
 
+def per_device(tokens, out_grad, route_gates, route_slot, gate_weight, up_weight, down_weight):
+    count, _ = tokens.shape
+    peers = lax.axis_size("expert")
+    cap = capacity_of(count, route_slot.shape[1], peers)
+    half, hidden_width = gate_weight.shape[1:]
+    fits = (
+        lax.axis_size("dp") == 2
+        and cap % 4 == 0
+        and (peers * cap) % 16 == 0
+        and count % 128 == 0
+        and half % 512 == 0
+        and hidden_width % 256 == 0
+    )
+    plan = split_width if fits else gathered_weights
+    return plan(tokens, out_grad, route_gates, route_slot, gate_weight, up_weight, down_weight)
+
+
 def solution(mesh):
     placed = (
         P(("dp", "expert"), None),

time: 260 us -> 224 us (0.86)
  Pallas kernels: 0 us -> 28.3 us
  matrix products: 20.9 us -> 0 us
  local copies, waits for them, and re-layouts: 33.3 us -> 18.2 us
  between operations: 14.1 us -> 0.81 us
  waiting for transfers between devices: 153 us -> 141 us
  other arithmetic: 13.9 us -> 3.92 us
  starting transfers between devices: 23.5 us -> 29.6 us
    ppermute x0 -> x4, waiting for transfers between devices: none -> 113 us  [the longest x1 43.8 us: split_width(): down_recv = lax.ppermute(down_send, 'dp', swap)]
    all_to_all x4, waiting for transfers between devices: 117 us -> 28.1 us  [the longest x1 28.1 us: split_width(): lax.all_to_all(tok_send.reshape(2 * peers, 2 * cap, quarter), ('dp', 'exp...]
    all_gather x3 -> x0, waiting for transfers between devices: 34 us -> none  [the longest x1 34 us: per_device(): lax.all_gather(down_weight, 'dp', axis=1, tiled=True)]
    pallas_call x0 -> x9, Pallas kernels: none -> 28.3 us  [the longest x1 4.73 us: split_width(): call(backward_kernel, (shape(2, rows, hidden_width), shape(2 * rows, half...]
    dot_general x7 -> x0, matrix products: 20.9 us -> none  [the longest x1 4.31 us: expert_forward(): up_proj = jnp.dot(rows_in, w_up, preferred_element_type=jnp.float32)]
    unnamed x24 -> x50, local copies, waits for them, and re-layouts: 1.9 us -> 18 us
    gather x7 -> x0, local copies, waits for them, and re-layouts: 14.6 us -> none  [the longest x2 5.03 us: per_device(): grad_back.reshape(send_rows, model_width)[send_index].astype(jnp.float32)]
    reshape x7 -> x0, local copies, waits for them, and re-layouts: 8.85 us -> none  [the longest x1 2.28 us: per_device(): grad_back.reshape(send_rows, model_width)[send_index].astype(jnp.float32)]
  transfers between devices with their start and end apart: 8 -> 8, of which waited for: 5 -> 5; matrix products, arithmetic and copies ran while one was open for 26% -> 2% of each run, Pallas kernels for 0% -> 11%
where the time goes in v1:
time: 224 us; the launch traced here: 222 us
  waiting for transfers between devices  141 us (63%)
  starting transfers between devices  29.6 us (13%)
  Pallas kernels  28.3 us (13%)
  local copies, waits for them, and re-layouts  18.2 us (8%)
  other arithmetic  3.92 us (2%)
    ppermute x1, waiting for transfers between devices, split_width(): down_recv = lax.ppermute(down_send, 'dp', swap)  43.8 us
    all_to_all x1, waiting for transfers between devices, split_width(): lax.all_to_all(tok_send.reshape(2 * peers, 2 * cap, quarter), ('dp', 'exp...  28.1 us
    ppermute x1, waiting for transfers between devices, split_width(): down_other = lax.ppermute(w_down, 'dp', swap)  25.5 us
    ppermute x1, waiting for transfers between devices, split_width(): d_recv = lax.ppermute(d_pair, 'dp', swap)  22.2 us
    ppermute x1, waiting for transfers between devices, split_width(): part_recv = lax.ppermute(part_send, 'dp', swap)  21.1 us
    unnamed x50, local copies, waits for them, and re-layouts  18 us
    all_to_all x1, starting transfers between devices, split_width(): lax.all_to_all(y_send.reshape(peers, 2 * cap, half), 'expert', 0, 0, tile...  6.89 us
    all_to_all x1, starting transfers between devices, split_width(): lax.all_to_all(dy_send.reshape(peers, 2 * cap, half), 'expert', 0, 0, til...  6.82 us
  transfers between devices with their start and end apart: 8, of which 5 were waited for; matrix products, arithmetic and copies ran while one was open for 2% of the time, Pallas kernels for 11%

profile of v1, /device:TPU:17, one launch (start us, length us, event | category | flops | bytes accessed | tf_op | source)
XLA Modules:
  0.0 221.6 jit_solution(18370767767127655221)
XLA Ops:
  0.6 1.0 copy-done.13
  1.7 0.7 copy-done.14
  2.4 1.7 shard_map.94
  4.1 6.3 %all-to-all-start = ((bf16[32,40,512]{2,1,0:T(8,128)(2,1)}), bf16[32,40,512]{2,1,0:T(8,128)(2,1)S(1)}, u32[]{:S(2)}, u32[]{:S(2)}) async-start(bf16[32,40,512]{2,1,0:T(8,128)(2,1)} %bitcast.2), calls=%async_computation | async-start | bytes 2621440 | tf_op jit(solution)/shard_map/all_to_all | solution.py:248
  10.3 0.1 copy.16.gates_ref
  10.5 2.1 shard_map.98
  12.5 28.1 %all-to-all-done = bf16[32,40,512]{2,1,0:T(8,128)(2,1)S(1)} async-done(((bf16[32,40,512]{2,1,0:T(8,128)(2,1)}), bf16[32,40,512]{2,1,0:T(8,128)(2,1)S(1)}, u32[]{:S(2)}, u32[]{:S(2)}) %all-to-all-start) | async-done | bytes 1310752 | tf_op jit(solution)/shard_map/all_to_all | solution.py:248
  40.7 6.8 %all-to-all-start.2 = ((bf16[16,40,1024]{2,1,0:T(8,128)(2,1)}), bf16[16,40,1024]{2,1,0:T(8,128)(2,1)}, u32[]{:S(2)}, u32[]{:S(2)}) async-start(bf16[16,40,1024]{2,1,0:T(8,128)(2,1)} %bitcast.9), calls=%async_computation.2 | async-start | bytes 2621440 | tf_op jit(solution)/shard_map/all_to_all | solution.py:261
  47.5 0.8 collective-permute-start.1
  48.3 0.1 pad_add_fusion
  48.4 0.1 broadcast_in_dim.12.target_ref
  48.6 0.0 copy-start.11
  48.6 1.3 copy-done.11
  49.9 1.4 copy-done.16
  51.3 1.4 copy-done.18
  52.7 4.2 %shard_map.95 = (f32[320,768]{1,0:T(8,128)S(1)}, f32[320,768]{1,0:T(8,128)S(1)}, bf16[2,320,768]{2,1,0:T(8,128)(2,1)S(1)}) custom-call(s32[1]{0:T(128)} %bitcast.group_ref, s32[640,1]{1,0:T(8,128)S(1)} %broadcast_in_dim.12.target_ref, bf16[2,640,512]{2,1,0:T(8,128)(2,1)S(1)} %bitcast.25, bf16[1024,768]{1,0:T(8,128)(2,1)S(1)} %bitcast.29, ...), custom_call_target="tpu_custom_call" | custom-call | flops 2013265920 | bytes 4456448 | tf_op jit(solution)/shard_map/pallas_call | solution.py:269
  56.9 0.8 collective-permute-start
  57.7 25.5 %collective-permute-done.1.other_ref = bf16[1024,768]{1,0:T(8,128)(2,1)S(1)} collective-permute-done((bf16[1024,768]{1,0:T(8,128)(2,1)S(1)}, bf16[1024,768]{1,0:T(8,128)(2,1)S(1)}, u32[]{:S(2)}, u32[]{:S(2)}) %collective-permute-start.1) | collective-permute-done | bytes 1572896 | tf_op jit(solution)/shard_map/ppermute | solution.py:251
  83.2 21.1 %collective-permute-done.recv_ref = bf16[2,320,768]{2,1,0:T(8,128)(2,1)S(1)} collective-permute-done((bf16[2,320,768]{2,1,0:T(8,128)(2,1)S(1)}, bf16[2,320,768]{2,1,0:T(8,128)(2,1)S(1)}, u32[]{:S(2)}, u32[]{:S(2)}) %collective-permute-start) | collective-permute-done | bytes 983072 | tf_op jit(solution)/shard_map/ppermute | solution.py:279
  104.3 3.3 %shard_map.96 = (bf16[320,768]{1,0:T(8,128)(2,1)S(1)}, bf16[640,1024]{1,0:T(8,128)(2,1)S(1)}) custom-call(s32[1]{0:T(128)} %bitcast.group_ref, s32[1,640]{1,0:T(1,128)S(1)} %broadcast_in_dim.9.target_ref, f32[320,768]{1,0:T(8,128)S(1)} %get-tuple-element.12.gate_ref, f32[320,768]{1,0:T(8,128)S(1)} %get-tuple-element.13.up_ref, ...), custom_call_target="tpu_custom_call" | custom-call | flops 1006632960 | bytes 4456448 | tf_op jit(solution)/shard_map/pallas_call | solution.py:283
  107.6 0.9 copy-done.1
  108.5 0.9 copy-done.3
  109.5 1.0 copy-done.5
  110.4 1.1 copy-done.12
  111.5 0.8 copy-done.21
  112.2 0.0 all-to-all-done.2
  112.2 6.9 %all-to-all-start.1 = ((bf16[16,40,1024]{2,1,0:T(8,128)(2,1)}), bf16[16,40,1024]{2,1,0:T(8,128)(2,1)}, u32[]{:S(2)}, u32[]{:S(2)}) async-start(bf16[16,40,1024]{2,1,0:T(8,128)(2,1)} %bitcast.26), calls=%async_computation.1 | async-start | bytes 2621440 | tf_op jit(solution)/shard_map/all_to_all | solution.py:301
  119.1 1.2 copy-done.2
  120.3 1.2 copy-done.4
  121.5 1.2 copy-done.6
  122.7 4.7 %shard_map.99 = (bf16[2,320,768]{2,1,0:T(8,128)(2,1)S(1)}, bf16[640,1024]{1,0:T(8,128)(2,1)S(1)}) custom-call(s32[1]{0:T(128)} %bitcast.group_ref, s32[640,1]{1,0:T(8,128)S(1)} %broadcast_in_dim.12.target_ref, bf16[640,1024]{1,0:T(8,128)(2,1)} %bitcast.10.grad_ref, f32[320,768]{1,0:T(8,128)S(1)} %copy-done.2, f32[320,768]{1,0:T(8,128)S(1)} %copy-done.4, ...), custom_call_target="tpu_custom_call" | custom-call | flops 1006632960 | bytes 4456448 | tf_op jit(solution)/shard_map/pallas_call | solution.py:305
  127.5 1.1 copy-done.8
  128.6 0.7 collective-permute-start.2
  129.3 22.2 %collective-permute-done.2.recv_ref = bf16[2,320,768]{2,1,0:T(8,128)(2,1)S(1)} collective-permute-done((bf16[2,320,768]{2,1,0:T(8,128)(2,1)S(1)}, bf16[2,320,768]{2,1,0:T(8,128)(2,1)S(1)}, u32[]{:S(2)}, u32[]{:S(2)}) %collective-permute-start.2) | collective-permute-done | bytes 983072 | tf_op jit(solution)/shard_map/ppermute | solution.py:323
  151.6 4.3 %shard_map.100 = bf16[2,640,512]{2,1,0:T(8,128)(2,1)} custom-call(s32[1]{0:T(128)} %bitcast.group_ref, s32[1,640]{1,0:T(1,128)S(1)} %broadcast_in_dim.9.target_ref, bf16[2,320,768]{2,1,0:T(8,128)(2,1)S(1)} %get-tuple-element.16.own_ref, bf16[2,320,768]{2,1,0:T(8,128)(2,1)S(1)} %collective-permute-done.2.recv_ref, bf16[1024,768]{1,0:T(8,128)(2,1)S(1)} %bitcast.30, ...), custom_call_target="tpu_custom_call" | custom-call | flops 2013265920 | bytes 4456448 | tf_op jit(solution)/shard_map/pallas_call | solution.py:324
  155.9 0.0 all-to-all-done.1
  155.9 6.1 %all-to-all-start.3 = ((bf16[32,40,512]{2,1,0:T(8,128)(2,1)}), bf16[32,40,512]{2,1,0:T(8,128)(2,1)S(1)}, u32[]{:S(2)}, u32[]{:S(2)}) async-start(bf16[32,40,512]{2,1,0:T(8,128)(2,1)} %bitcast.11), calls=%async_computation.3 | async-start | bytes 2621440 | tf_op jit(solution)/shard_map/all_to_all | solution.py:340
  162.0 0.0 copy-start.22
  162.1 0.1 dynamic-slice_bitcast_fusion
  162.2 0.9 copy-done.22
  163.1 2.6 %shard_map.102 = (f32[1024,768]{1,0:T(8,128)S(1)}, bf16[1024,768]{1,0:T(8,128)(2,1)S(1)}) custom-call(s32[1]{0:T(128)} %bitcast.group_ref, bf16[320,1024]{1,0:T(8,128)(2,1)S(1)} %get-tuple-element.22.dy_mine_ref, bf16[320,1024]{1,0:T(8,128)(2,1)S(1)} %get-tuple-element.21.dy_other_ref, bf16[320,768]{1,0:T(8,128)(2,1)S(1)} %copy-done.22), custom_call_target="tpu_custom_call" | custom-call | flops 1006632960 | bytes 6029312 | tf_op jit(solution)/shard_map/pallas_call | solution.py:350
  165.7 1.6 copy-done.7
  167.3 1.2 collective-permute-start.3
  168.5 0.1 copy.15.slots_ref
  168.6 43.8 %collective-permute-done.3 = bf16[1024,768]{1,0:T(8,128)(2,1)} collective-permute-done((bf16[1024,768]{1,0:T(8,128)(2,1)S(1)}, bf16[1024,768]{1,0:T(8,128)(2,1)}, u32[]{:S(2)}, u32[]{:S(2)}) %collective-permute-start.3) | collective-permute-done | bytes 1572896 | tf_op jit(solution)/shard_map/ppermute | solution.py:359
  212.5 3.8 %fusion = bf16[1,1024,768]{2,1,0:T(8,128)(2,1)} fusion(f32[1024,768]{1,0:T(8,128)} %copy-done.7, bf16[1024,768]{1,0:T(8,128)(2,1)} %collective-permute-done.3), kind=kLoop, calls=%fused_computation.1 | loop fusion | flops 2359296 | bytes 6291456 | tf_op jit(solution)/shard_map/broadcast_in_dim | solution.py:360
  216.3 3.5 %shard_map.97 = bf16[128,2048]{1,0:T(8,128)(2,1)} custom-call(s32[128,2]{1,0:T(8,128)S(1)} %copy.15.slots_ref, f32[128,2]{1,0:T(8,128)S(1)} %copy.16.gates_ref, bf16[640,1024]{1,0:T(8,128)(2,1)} %bitcast.8.back_ref), custom_call_target="tpu_custom_call" | custom-call | flops 671088640 | bytes 1835008 | tf_op jit(solution)/shard_map/pallas_call | solution.py:362
  219.8 1.8 shard_map.101
  (33 shorter events, 0.1 us)
Async XLA Ops:
  0.6 1.0 copy-start.13
  1.7 0.7 copy-start.14
  4.1 6.3 %copy-start.23 = (f32[128,2]{0,1:T(2,128)S(1)}, f32[128,2]{0,1:T(2,128)}, u32[]{:S(2)}) copy-start(f32[128,2]{0,1:T(2,128)} %param.9) | copy-start | bytes 3076
  4.1 6.4 %copy-start.15 = (s32[128,2]{0,1:T(2,128)S(1)}, s32[128,2]{0,1:T(2,128)}, u32[]{:S(2)}) copy-start(s32[128,2]{0,1:T(2,128)} %param.10) | copy-start | bytes 3076
  4.1 6.4 %copy-start.20 = (bf16[128,2048]{1,0:T(8,128)(2,1)S(1)}, bf16[128,2048]{1,0:T(8,128)(2,1)}, u32[]{:S(2)}) copy-start(bf16[128,2048]{1,0:T(8,128)(2,1)} %grad_ref.1) | copy-start | bytes 1572868
  4.1 36.6 %all-to-all-start = ((bf16[32,40,512]{2,1,0:T(8,128)(2,1)}), bf16[32,40,512]{2,1,0:T(8,128)(2,1)S(1)}, u32[]{:S(2)}, u32[]{:S(2)}) async-start(bf16[32,40,512]{2,1,0:T(8,128)(2,1)} %bitcast.2), calls=%async_computation | async-start | bytes 2621440 | tf_op jit(solution)/shard_map/all_to_all | solution.py:248
  12.5 35.0 %copy-start = (bf16[1,1024,768]{2,1,0:T(8,128)(2,1)S(1)}, bf16[1,1024,768]{2,1,0:T(8,128)(2,1)}, u32[]{:S(2)}) copy-start(bf16[1,1024,768]{2,1,0:T(8,128)(2,1)} %param.13) | copy-start | bytes 4718596
  40.7 6.8 %copy-start.10 = (bf16[32,40,512]{2,1,0:T(8,128)(2,1)}, bf16[32,40,512]{2,1,0:T(8,128)(2,1)S(1)}, u32[]{:S(2)}) copy-start(bf16[32,40,512]{2,1,0:T(8,128)(2,1)S(1)} %all-to-all-done) | copy-start | bytes 3932164
  40.7 71.6 %all-to-all-start.2 = ((bf16[16,40,1024]{2,1,0:T(8,128)(2,1)}), bf16[16,40,1024]{2,1,0:T(8,128)(2,1)}, u32[]{:S(2)}, u32[]{:S(2)}) async-start(bf16[16,40,1024]{2,1,0:T(8,128)(2,1)} %bitcast.9), calls=%async_computation.2 | async-start | bytes 2621440 | tf_op jit(solution)/shard_map/all_to_all | solution.py:261
  47.5 35.7 %collective-permute-start.1 = (bf16[1024,768]{1,0:T(8,128)(2,1)S(1)}, bf16[1024,768]{1,0:T(8,128)(2,1)S(1)}, u32[]{:S(2)}, u32[]{:S(2)}) collective-permute-start(bf16[1024,768]{1,0:T(8,128)(2,1)S(1)} %bitcast.20), channel_id=1, source_target_pairs={{0,16},{16,0},{1,17},{17,1},{2,18},{18,2},{3,19},{19,3},{4,20},{20... | collective-permute-start | bytes 4718600 | tf_op jit(solution)/shard_map/ppermute | solution.py:251
  48.6 1.3 copy-start.11
  49.9 1.4 copy-start.16
  51.3 1.4 copy-start.18
  56.9 47.3 %collective-permute-start = (bf16[2,320,768]{2,1,0:T(8,128)(2,1)S(1)}, bf16[2,320,768]{2,1,0:T(8,128)(2,1)S(1)}, u32[]{:S(2)}, u32[]{:S(2)}) collective-permute-start(bf16[2,320,768]{2,1,0:T(8,128)(2,1)S(1)} %get-tuple-element.14), channel_id=1, source_target_pairs={{0,16},{16,0},{1,17},{17,1},{2,18},{18,2},{3,19},{19,3},{4,20},{20... | collective-permute-start | bytes 2949128 | tf_op jit(solution)/shard_map/ppermute | solution.py:279
  107.5 1.0 copy-start.1
  108.5 0.9 copy-start.3
  109.4 1.0 copy-start.5
  110.4 1.1 copy-start.12
  111.5 0.8 copy-start.21
  112.2 43.6 %all-to-all-start.1 = ((bf16[16,40,1024]{2,1,0:T(8,128)(2,1)}), bf16[16,40,1024]{2,1,0:T(8,128)(2,1)}, u32[]{:S(2)}, u32[]{:S(2)}) async-start(bf16[16,40,1024]{2,1,0:T(8,128)(2,1)} %bitcast.26), calls=%async_computation.1 | async-start | bytes 2621440 | tf_op jit(solution)/shard_map/all_to_all | solution.py:301
  119.1 1.2 copy-start.2
  120.3 1.2 copy-start.4
  121.5 1.2 copy-start.6
  122.7 28.8 %copy-start.17 = (bf16[1,1024,768]{2,1,0:T(8,128)(2,1)S(1)}, bf16[1,1024,768]{2,1,0:T(8,128)(2,1)}, u32[]{:S(2)}) copy-start(bf16[1,1024,768]{2,1,0:T(8,128)(2,1)} %param.11) | copy-start | bytes 4718596
  122.7 28.8 %copy-start.19 = (bf16[1,1024,768]{2,1,0:T(8,128)(2,1)S(1)}, bf16[1,1024,768]{2,1,0:T(8,128)(2,1)}, u32[]{:S(2)}) copy-start(bf16[1,1024,768]{2,1,0:T(8,128)(2,1)} %param.12) | copy-start | bytes 4718596
  127.5 1.1 copy-start.8
  128.6 23.0 %collective-permute-start.2 = (bf16[2,320,768]{2,1,0:T(8,128)(2,1)S(1)}, bf16[2,320,768]{2,1,0:T(8,128)(2,1)S(1)}, u32[]{:S(2)}, u32[]{:S(2)}) collective-permute-start(bf16[2,320,768]{2,1,0:T(8,128)(2,1)S(1)} %get-tuple-element.16.own_ref), channel_id=1, source_target_pairs={{0,16},{16,0},{1,17},{17,1},{2,18},{18,2},{3,19},{19,3},{4,20},{20... | collective-permute-start | bytes 2949128 | tf_op jit(solution)/shard_map/ppermute | solution.py:323
  155.9 6.2 %copy-start.9 = (bf16[640,1024]{1,0:T(8,128)(2,1)S(1)}, bf16[640,1024]{1,0:T(8,128)(2,1)}, u32[]{:S(2)}) copy-start(bf16[640,1024]{1,0:T(8,128)(2,1)} %copy-done.8) | copy-start | bytes 3932164
  155.9 63.9 %all-to-all-start.3 = ((bf16[32,40,512]{2,1,0:T(8,128)(2,1)}), bf16[32,40,512]{2,1,0:T(8,128)(2,1)S(1)}, u32[]{:S(2)}, u32[]{:S(2)}) async-start(bf16[32,40,512]{2,1,0:T(8,128)(2,1)} %bitcast.11), calls=%async_computation.3 | async-start | bytes 2621440 | tf_op jit(solution)/shard_map/all_to_all | solution.py:340
  162.0 1.0 copy-start.22
  165.7 1.6 copy-start.7
  167.3 45.1 %collective-permute-start.3 = (bf16[1024,768]{1,0:T(8,128)(2,1)S(1)}, bf16[1024,768]{1,0:T(8,128)(2,1)}, u32[]{:S(2)}, u32[]{:S(2)}) collective-permute-start(bf16[1024,768]{1,0:T(8,128)(2,1)S(1)} %get-tuple-element.20), channel_id=1, source_target_pairs={{0,16},{16,0},{1,17},{17,1},{2,18},{18,2},{3,19},{19,3},{4,20},{20... | collective-permute-start | bytes 4718600 | tf_op jit(solution)/shard_map/ppermute | solution.py:359

commit v2 on v0

--- a/solution.py
+++ b/solution.py
@@ -1,7 +1,423 @@
+import functools
+
 import jax
 import jax.numpy as jnp
 from jax import lax
+from jax.experimental import pallas as pl
+from jax.experimental.pallas import tpu as pltpu
 from jax.sharding import PartitionSpec as P
+
+PLANE = 4
+F32, BF16, I32 = jnp.float32, jnp.bfloat16, jnp.int32
+NT = (((1,), (1,)), ((), ()))
+TN = (((0,), (0,)), ((), ()))
+
+
+def mm(a, b, dims=(((1,), (0,)), ((), ()))):
+    return lax.dot_general(a, b, dims, preferred_element_type=F32)
+
+
+def ones_where(mask):
+    return jnp.where(mask, 1.0, 0.0).astype(BF16)
+
+
+def iota(shape, dim):
+    return lax.broadcasted_iota(I32, shape, dim)
+
+
+def call(kernel, out_shape, grid, in_specs, out_specs, scratch=(), flops=0, moved=0, vmem_mib=24):
+    return pl.pallas_call(
+        kernel,
+        out_shape=out_shape,
+        grid=grid,
+        in_specs=in_specs,
+        out_specs=out_specs,
+        scratch_shapes=list(scratch),
+        cost_estimate=pl.CostEstimate(flops=flops, bytes_accessed=moved, transcendentals=0),
+        compiler_params=pltpu.CompilerParams(vmem_limit_bytes=vmem_mib * 2**20),
+    )
+
+
+def whole(shape):
+    return pl.BlockSpec(shape, lambda *_: (0,) * len(shape))
+
+
+def column_half(group, half):
+    return pl.ds(pl.multiple_of(group * half, 128), half)
+
+
+SCALAR = pl.BlockSpec(memory_space=pltpu.SMEM)
+HBM = pl.BlockSpec(memory_space=pltpu.HBM)
+
+
+def ranks_in_lanes(slots, peers):
+    top, count = slots.shape
+    named = [jnp.where(iota((peers, count), 0) == slots[k : k + 1, :], 1.0, 0.0) for k in range(top)]
+    earlier = ones_where(iota((count, count), 0) < iota((count, count), 1))
+    before = mm(sum(named).astype(BF16), earlier)
+    return [jnp.sum(before * each, axis=0, keepdims=True).astype(I32) for each in named]
+
+
+def ranks_in_rows(slots, peers):
+    count, top = slots.shape
+    named = [jnp.where(iota((count, peers), 1) == slots[:, k : k + 1], 1.0, 0.0) for k in range(top)]
+    earlier = ones_where(iota((count, count), 1) < iota((count, count), 0))
+    before = mm(earlier, sum(named).astype(BF16))
+    return [jnp.sum(before * each, axis=1, keepdims=True).astype(I32) for each in named]
+
+
+def masks_of(number, expert):
+    return (number ^ expert) & (PLANE - 1), (number ^ expert) // PLANE
+
+
+def spread(values, refs, columns, block):
+    each = refs[0].shape[0]
+    for m, ref in enumerate(refs):
+        for i in range(each):
+            lo = (each * m + i) * block
+            ref[i, :, columns] = values[lo : lo + block].astype(BF16)
+
+
+def send_tokens_kernel(peers, cap, slots_ref, tok_ref, out_ref):
+    _, rows, width = out_ref.shape
+    slots = slots_ref[...]
+    at = iota((rows, slots.shape[1]), 0)
+    places = [slots[k : k + 1, :] * (2 * cap) + rank for k, rank in enumerate(ranks_in_lanes(slots, peers))]
+    halves = [sum(jnp.where(at == place + h * cap, 1.0, 0.0) for place in places) for h in range(2)]
+    pick = jnp.concatenate(halves, axis=1).astype(BF16)
+    for part in range(2):
+        lo = part * 2 * width
+        both = jnp.concatenate([tok_ref[:, lo : lo + width], tok_ref[:, lo + width : lo + 2 * width]], axis=0)
+        out_ref[part] = mm(pick, both).astype(BF16)
+
+
+def send_grads_kernel(peers, cap, group_ref, expert_ref, slots_ref, gates_ref, grad_ref, *out_refs):
+    slots, gates = slots_ref[...], gates_ref[...]
+    group, expert = group_ref[0], expert_ref[0]
+    rows, count = 2 * cap * peers, slots.shape[1]
+    half = out_refs[0].shape[2]
+    at = iota((rows, count), 0)
+    halves = [grad_ref[:, column_half(g, half)].astype(F32) for g in (group, 1 - group)]
+    total = None
+    for k, rank in enumerate(ranks_in_lanes(slots, peers)):
+        near, far = masks_of(slots[k : k + 1, :], expert)
+        place = (near * (peers // PLANE) + far) * (2 * cap) + rank
+        pick = jnp.concatenate([jnp.where(at == place + o * cap, 1.0, 0.0) for o in range(2)], axis=1).astype(BF16)
+        both = jnp.concatenate([(gates[:, k : k + 1] * each).astype(BF16) for each in halves], axis=0)
+        rows_k = mm(pick, both)
+        total = rows_k if total is None else total + rows_k
+    spread(total, out_refs, slice(None), 2 * cap)
+
+
+def regroup_kernel(count, *refs):
+    blocks, outs = refs[:count], refs[count:]
+    for i, out_ref in enumerate(outs):
+        for m, block_ref in enumerate(blocks):
+            out_ref[m] = block_ref[i]
+
+
+def partial_kernel(
+    tile, group_ref, target_ref, recv_ref, wg_ref, wu_ref, gate_ref, up_ref, send_ref, x_ref, w_ref, sems
+):
+    rows, ff = gate_ref.shape
+    width = recv_ref.shape[2]
+    copies = {}
+    for t in range(ff // tile):
+        columns = pl.ds(t * tile, tile)
+        for i, ref in enumerate((wg_ref, wu_ref)):
+            copies[t, i] = pltpu.make_async_copy(ref.at[:, columns], w_ref.at[i, :, columns], sems.at[i, t])
+            copies[t, i].start()
+    pick = ones_where(iota((2 * rows, 2 * rows), 1) == target_ref[...])
+    for o, g in enumerate((group_ref[0], 1 - group_ref[0])):
+        for h in range(2):
+            x_ref[o * rows : (o + 1) * rows, h * width : (h + 1) * width] = mm(
+                pick[h * rows : (h + 1) * rows], recv_ref[g]
+            ).astype(BF16)
+    for t in range(ff // tile):
+        columns = slice(t * tile, (t + 1) * tile)
+        for i, mine_ref in enumerate((gate_ref, up_ref)):
+            copies[t, i].wait()
+            both = mm(x_ref[...], w_ref[i, :, columns])
+            mine_ref[:, columns] = both[:rows]
+            send_ref[i, :, columns] = both[rows:].astype(BF16)
+
+
+def backward_kernel(target_ref, gate_ref, up_ref, recv_ref, own_ref, other_ref, *refs):
+    *came_refs, hid_ref, out_ref, dy_mine_ref, dy_send_ref, came_ref = refs
+    rows = gate_ref.shape[0]
+
+    @pl.when(pl.program_id(0) == 0)
+    def _():
+        each = came_refs[0].shape[0]
+        for m, ref in enumerate(came_refs):
+            came_ref[m * each : (m + 1) * each, :] = ref[...]
+        pick = ones_where(iota((2 * rows, 2 * rows), 1) == target_ref[...])
+        dy = mm(pick, came_ref[...]).astype(BF16)
+        dy_mine_ref[...] = dy[:rows]
+        dy_send_ref[...] = dy[rows:]
+
+    gate = gate_ref[...] + recv_ref[0].astype(F32)
+    up = up_ref[...] + recv_ref[1].astype(F32)
+    sigma = jax.nn.sigmoid(gate)
+    active = gate * sigma
+    hid_ref[...] = (active * up).astype(BF16)
+    d_hidden = mm(dy_mine_ref[...], own_ref[...]) + mm(dy_send_ref[...], other_ref[...])
+    out_ref[0] = (d_hidden * up * sigma * (1.0 + gate * (1.0 - sigma))).astype(BF16)
+    out_ref[1] = (d_hidden * active).astype(BF16)
+
+
+def forward_kernel(target_ref, hid_ref, own_ref, other_ref, *refs):
+    *out_refs, pick_ref, y_ref = refs
+    rows = hid_ref.shape[0]
+
+    @pl.when(pl.program_id(0) == 0)
+    def _():
+        pick_ref[...] = ones_where(iota((2 * rows, 2 * rows), 0) == target_ref[...])
+
+    hidden = hid_ref[...]
+    y_ref[:rows, :] = mm(hidden, own_ref[...], NT).astype(BF16)
+    y_ref[rows:, :] = mm(hidden, other_ref[...], NT).astype(BF16)
+    spread(mm(pick_ref[...], y_ref[...]), out_refs, slice(None), out_refs[0].shape[1])
+
+
+def input_grad_kernel(group_ref, target_ref, own_ref, recv_ref, wg_ref, wu_ref, out_ref, d_ref, dx_ref):
+    rows = own_ref.shape[1]
+    width = out_ref.shape[2]
+    for i in range(2):
+        d_ref[i, :rows, :] = own_ref[i]
+        d_ref[i, rows:, :] = recv_ref[i]
+    for h in range(2):
+        part = slice(h * width, (h + 1) * width)
+        dx = (mm(d_ref[0], wg_ref[part, :], NT) + mm(d_ref[1], wu_ref[part, :], NT)).astype(BF16)
+        for o in range(2):
+            dx_ref[o, h * rows : (h + 1) * rows, :] = dx[o * rows : (o + 1) * rows]
+    pick = ones_where(iota((2 * rows, 2 * rows), 0) == target_ref[...])
+    group = group_ref[0]
+    out_ref[group] = mm(pick, dx_ref[0]).astype(BF16)
+    out_ref[1 - group] = mm(pick, dx_ref[1]).astype(BF16)
+
+
+def down_kernel(mine_ref, recv_ref, hid_ref, hid_recv_ref, out_ref):
+    out_ref[...] = (mm(mine_ref[...], hid_ref[...], TN) + mm(recv_ref[...], hid_recv_ref[...], TN)).astype(BF16)
+
+
+def combine_out_kernel(peers, cap, group_ref, expert_ref, slots_ref, gates_ref, *refs):
+    *came_refs, out_ref, came_ref = refs
+    slots, gates = slots_ref[...], gates_ref[...]
+    group, expert = group_ref[0], expert_ref[0]
+    rows, half = came_ref.shape
+    each = rows // len(came_refs)
+    for m, ref in enumerate(came_refs):
+        came_ref[m * each : (m + 1) * each, :] = ref[...]
+    at = iota((slots.shape[0], rows), 1)
+    places = []
+    for k, rank in enumerate(ranks_in_rows(slots, peers)):
+        near, far = masks_of(slots[:, k : k + 1], expert)
+        places.append((near * (peers // PLANE) + far) * (2 * cap) + rank)
+    for o, g in enumerate((group, 1 - group)):
+        total = None
+        for k, place in enumerate(places):
+            term = gates[:, k : k + 1] * mm(ones_where(at == place + o * cap), came_ref[...])
+            total = term if total is None else total + term
+        out_ref[:, column_half(g, half)] = total.astype(BF16)
+
+
+def combine_grad_kernel(peers, cap, slots_ref, back_ref, out_ref):
+    slots = slots_ref[...]
+    places = [slots[:, k : k + 1] * (2 * cap) + rank for k, rank in enumerate(ranks_in_rows(slots, peers))]
+    _, rows, width = back_ref.shape
+    at = iota((slots.shape[0], rows), 1)
+    for h in range(2):
+        pick = sum(jnp.where(at == place + h * cap, 1.0, 0.0) for place in places).astype(BF16)
+        for part in range(2):
+            lo = (2 * part + h) * width
+            out_ref[:, lo : lo + width] = mm(pick, back_ref[part]).astype(BF16)
+
+
+def split_width(tokens, out_grad, route_gates, route_slot, gate_weight, up_weight, down_weight):
+    count, width = tokens.shape
+    top = route_slot.shape[1]
+    peers = lax.axis_size("expert")
+    planes = peers // PLANE
+    cap = capacity_of(count, top, peers)
+    w_gate, w_up, w_down = gate_weight[0], up_weight[0], down_weight[0]
+    half, ff = w_gate.shape
+    quarter = half // 2
+    rows = peers * cap
+    swap = [(0, 1), (1, 0)]
+    index = lax.axis_index("dp").astype(I32)
+    group, expert = index.reshape(1), lax.axis_index("expert").astype(I32).reshape(1)
+    slots_t = route_slot.T
+    place = jnp.arange(rows, dtype=I32)
+    straight_left = (place // cap) * (2 * cap) + place % cap
+    straight = jnp.concatenate([straight_left, straight_left + cap])
+    near, far = masks_of(place // cap, expert)
+    moved_left = (far * PLANE + near) * (2 * cap) + place % cap
+    moved = jnp.concatenate([moved_left, moved_left + cap])
+    tile, strip, narrow = min(256, ff), min(512, half), min(256, half)
+    matmul_flops = 2 * 2 * rows * half * ff
+    route_flops = 2 * 2 * rows * 2 * count * half
+    route_bytes = 2 * (tokens.size + 2 * rows * half)
+    weight_bytes = 2 * half * ff
+
+    def shape(*dims, dtype=BF16):
+        return jax.ShapeDtypeStruct(dims, dtype)
+
+    near_block, far_block = (planes, 2 * cap, half), (PLANE, 2 * cap, half)
+
+    def exchange(blocks, stride):
+        return [blocks[0]] + [
+            lax.ppermute(blocks[m], "expert", [(i, i ^ (m * stride)) for i in range(peers)])
+            for m in range(1, len(blocks))
+        ]
+
+    def regroup(blocks):
+        outs, *rest = blocks[0].shape
+        return call(
+            functools.partial(regroup_kernel, len(blocks)),
+            tuple(pltpu.HBM((len(blocks), *rest), BF16) for _ in range(outs)),
+            (1,),
+            [whole(blocks[0].shape)] * len(blocks),
+            tuple(whole((len(blocks), *rest)) for _ in range(outs)),
+            moved=8 * rows * half,
+        )(*blocks)
+
+    down_other = lax.ppermute(w_down, "dp", swap)
+    dy_near = call(
+        functools.partial(send_grads_kernel, peers, cap),
+        tuple(shape(*near_block) for _ in range(PLANE)),
+        (1,),
+        [SCALAR, SCALAR, whole(slots_t.shape), whole(route_gates.shape), whole(out_grad.shape)],
+        tuple(whole(near_block) for _ in range(PLANE)),
+        flops=top * route_flops,
+        moved=route_bytes,
+    )(group, expert, slots_t, route_gates, out_grad)
+    dy_far = regroup(exchange(dy_near, 1))
+
+    tok_send = call(
+        functools.partial(send_tokens_kernel, peers, cap),
+        shape(2, 2 * rows, quarter),
+        (1,),
+        [whole(slots_t.shape), whole(tokens.shape)],
+        whole((2, 2 * rows, quarter)),
+        flops=route_flops,
+        moved=route_bytes,
+    )(slots_t, tokens)
+    tok_recv = lax.all_to_all(
+        tok_send.reshape(2 * peers, 2 * cap, quarter), ("dp", "expert"), 0, 0, tiled=True
+    ).reshape(2, 2 * rows, quarter)
+    tok_recv, dy_far = lax.optimization_barrier((tok_recv, dy_far))
+
+    part_block = pl.BlockSpec((rows, tile), lambda i: (0, i))
+    pair_block = pl.BlockSpec((2, rows, tile), lambda i: (0, 0, i))
+    weight_block = pl.BlockSpec((half, tile), lambda i: (0, i))
+    gate_mine, up_mine, part_send = call(
+        functools.partial(partial_kernel, tile),
+        (shape(rows, ff, dtype=F32), shape(rows, ff, dtype=F32), shape(2, rows, ff)),
+        (1,),
+        [SCALAR, whole((2 * rows, 1)), whole((2, 2 * rows, quarter)), HBM, HBM],
+        (whole((rows, ff)), whole((rows, ff)), whole((2, rows, ff))),
+        [
+            pltpu.VMEM((2 * rows, half), BF16),
+            pltpu.VMEM((2, half, ff), BF16),
+            pltpu.SemaphoreType.DMA((2, ff // tile)),
+        ],
+        flops=2 * matmul_flops,
+        moved=2 * weight_bytes + 4 * rows * half,
+    )(group, straight[:, None], tok_recv, w_gate, w_up)
+    part_recv = lax.ppermute(part_send, "dp", swap)
+    dy_came = exchange(dy_far, PLANE)
+
+    hidden, d_pair, dy_mine, dy_other = call(
+        backward_kernel,
+        (shape(rows, ff), shape(2, rows, ff), shape(rows, half), shape(rows, half)),
+        (ff // tile,),
+        [whole((2 * rows, 1)), part_block, part_block, pair_block, weight_block, weight_block]
+        + [whole((PLANE * 2 * cap, half))] * planes,
+        (part_block, pair_block, whole((rows, half)), whole((rows, half))),
+        [pltpu.VMEM((2 * rows, half), BF16)],
+        flops=matmul_flops,
+        moved=2 * weight_bytes + 4 * rows * half,
+    )(
+        moved[:, None], gate_mine, up_mine, part_recv, w_down, down_other,
+        *(came.reshape(PLANE * 2 * cap, half) for came in dy_came)
+    )
+    down_rows = pl.BlockSpec((strip, ff), lambda i: (i, 0))
+    y_far = call(
+        forward_kernel,
+        tuple(shape(*far_block) for _ in range(planes)),
+        (half // strip,),
+        [whole((1, 2 * rows)), whole((rows, ff)), down_rows, down_rows],
+        tuple(pl.BlockSpec((PLANE, 2 * cap, strip), lambda i: (0, 0, i)) for _ in range(planes)),
+        [pltpu.VMEM((2 * rows, 2 * rows), BF16), pltpu.VMEM((2 * rows, strip), BF16)],
+        flops=matmul_flops,
+        moved=2 * weight_bytes + 4 * rows * half,
+    )(moved[None, :], hidden, w_down, down_other)
+    hidden_recv = lax.ppermute(hidden, "dp", swap)
+    d_recv = lax.ppermute(d_pair, "dp", swap)
+    dy_cross = lax.ppermute(dy_other, "dp", swap)
+
+    *_, d_recv = lax.optimization_barrier((*y_far, d_recv))
+    y_far_came = exchange(y_far, PLANE)
+    dx_send = call(
+        input_grad_kernel,
+        shape(2, 2 * rows, quarter),
+        (1,),
+        [
+            SCALAR,
+            whole((1, 2 * rows)),
+            whole((2, rows, ff)),
+            whole((2, rows, ff)),
+            whole((half, ff)),
+            whole((half, ff)),
+        ],
+        whole((2, 2 * rows, quarter)),
+        [pltpu.VMEM((2, 2 * rows, ff), BF16), pltpu.VMEM((2, 2 * rows, quarter), BF16)],
+        flops=2 * matmul_flops,
+        moved=2 * weight_bytes + 4 * rows * half,
+    )(group, straight[None, :], d_pair, d_recv, w_gate, w_up)
+    dx_send, y_far_came, hidden_recv = lax.optimization_barrier((dx_send, y_far_came, hidden_recv))
+    y_came = exchange(regroup(y_far_came), 1)
+    dx_back = lax.all_to_all(
+        dx_send.reshape(2 * peers, 2 * cap, quarter), ("dp", "expert"), 0, 0, tiled=True
+    ).reshape(2, 2 * rows, quarter)
+
+    strip_block = pl.BlockSpec((rows, narrow), lambda i: (0, i))
+    down_grad = call(
+        down_kernel,
+        shape(half, ff),
+        (half // narrow,),
+        [strip_block, strip_block, whole((rows, ff)), whole((rows, ff))],
+        pl.BlockSpec((narrow, ff), lambda i: (i, 0)),
+        flops=matmul_flops,
+        moved=weight_bytes + 4 * rows * half,
+    )(dy_mine, dy_cross, hidden, hidden_recv)[None]
+    moe_out = call(
+        functools.partial(combine_out_kernel, peers, cap),
+        shape(count, width),
+        (1,),
+        [SCALAR, SCALAR, whole(route_slot.shape), whole(route_gates.shape)]
+        + [whole((planes * 2 * cap, half))] * PLANE,
+        whole((count, width)),
+        [pltpu.VMEM((2 * rows, half), BF16)],
+        flops=top * route_flops,
+        moved=route_bytes,
+    )(group, expert, route_slot, route_gates, *(came.reshape(planes * 2 * cap, half) for came in y_came))
+    dx_back, moe_out, down_grad = lax.optimization_barrier((dx_back, moe_out, down_grad))
+    token_grad = call(
+        functools.partial(combine_grad_kernel, peers, cap),
+        shape(count, width),
+        (1,),
+        [whole(route_slot.shape), whole((2, 2 * rows, quarter))],
+        whole((count, width)),
+        flops=route_flops,
+        moved=route_bytes,
+    )(route_slot, dx_back)
+    return (moe_out, token_grad, down_grad)
+
+
+def capacity_of(count, top, peers):
+    return max(2, (5 * count * top + 4 * peers - 1) // (4 * peers))
 
 
 def expert_forward(rows_in, w_gate, w_up, w_down):
@@ -31,11 +447,11 @@
     return summed.astype(jnp.bfloat16)
 
 
-def per_device(tokens, out_grad, route_gates, route_slot, gate_weight, up_weight, down_weight):
+def gathered_weights(tokens, out_grad, route_gates, route_slot, gate_weight, up_weight, down_weight):
     tok_dev, model_width = tokens.shape
     route_count = route_slot.shape[1]
     peer_count = lax.axis_size("expert")
-    capacity = max(2, (5 * tok_dev * route_count + 4 * peer_count - 1) // (4 * peer_count))
+    capacity = capacity_of(tok_dev, route_count, peer_count)
     route_total = tok_dev * route_count
     send_rows = peer_count * capacity
     flat_slot = route_slot.reshape(-1)
@@ -100,6 +516,25 @@
     return (moe_out, token_grad, down_grad)
 
 
+def per_device(tokens, out_grad, route_gates, route_slot, gate_weight, up_weight, down_weight):
+    count, _ = tokens.shape
+    peers = lax.axis_size("expert")
+    cap = capacity_of(count, route_slot.shape[1], peers)
+    half, hidden_width = gate_weight.shape[1:]
+    fits = (
+        lax.axis_size("dp") == 2
+        and peers % PLANE == 0
+        and peers & (peers - 1) == 0
+        and cap % 4 == 0
+        and (peers * cap) % 16 == 0
+        and count % 128 == 0
+        and half % 512 == 0
+        and hidden_width % 256 == 0
+    )
+    plan = split_width if fits else gathered_weights
+    return plan(tokens, out_grad, route_gates, route_slot, gate_weight, up_weight, down_weight)
+
+
 def solution(mesh):
     placed = (
         P(("dp", "expert"), None),

time: 260 us -> 173 us (0.67)
  waiting for transfers between devices: 153 us -> 95.3 us
  Pallas kernels: 0 us -> 32.2 us
  matrix products: 20.9 us -> 0 us
  local copies, waits for them, and re-layouts: 33.3 us -> 13.9 us
  other arithmetic: 13.9 us -> 0.19 us
  between operations: 14.1 us -> 0.82 us
  starting transfers between devices: 23.5 us -> 28.2 us
    all_to_all x4 -> x2, waiting for transfers between devices: 117 us -> 0.01 us  [the longest x1 0.01 us: split_width(): lax.all_to_all(dx_send.reshape(2 * peers, 2 * cap, quarter), ('dp', 'expe...]
    ppermute x0 -> x17, waiting for transfers between devices: none -> 95.3 us  [the longest x12 55.3 us: exchange(): lax.ppermute(blocks[m], 'expert', [(i, i ^ m * stride) for i in range(pee...]
    all_gather x3 -> x0, waiting for transfers between devices: 34 us -> none  [the longest x1 34 us: per_device(): lax.all_gather(down_weight, 'dp', axis=1, tiled=True)]
    pallas_call x0 -> x11, Pallas kernels: none -> 32.2 us  [the longest x1 7.89 us: split_width(): call(functools.partial(partial_kernel, tile), (shape(rows, ff, dtype=F32)...]
    dot_general x7 -> x0, matrix products: 20.9 us -> none  [the longest x1 4.31 us: expert_forward(): up_proj = jnp.dot(rows_in, w_up, preferred_element_type=jnp.float32)]
    ppermute x0 -> x17, starting transfers between devices: none -> 15 us  [the longest x12 10 us: exchange(): lax.ppermute(blocks[m], 'expert', [(i, i ^ m * stride) for i in range(pee...]
    gather x7 -> x0, local copies, waits for them, and re-layouts: 14.6 us -> none  [the longest x2 5.03 us: per_device(): grad_back.reshape(send_rows, model_width)[send_index].astype(jnp.float32)]
    unnamed x24 -> x58, local copies, waits for them, and re-layouts: 1.9 us -> 13.6 us
  transfers between devices with their start and end apart: 8 -> 19, of which waited for: 5 -> 9; matrix products, arithmetic and copies ran while one was open for 26% -> 0% of each run, Pallas kernels for 0% -> 15%
where the time goes in v2:
time: 173 us; the launch traced here: 171 us
  waiting for transfers between devices  95.3 us (55%)
  Pallas kernels  32.2 us (19%)
  starting transfers between devices  28.2 us (16%)
  local copies, waits for them, and re-layouts  13.9 us (8%)
    ppermute x12, waiting for transfers between devices, exchange(): lax.ppermute(blocks[m], 'expert', [(i, i ^ m * stride) for i in range(pee...  55.3 us
    ppermute x1, waiting for transfers between devices, split_width(): dy_cross = lax.ppermute(dy_other, 'dp', swap)  22.1 us
    ppermute x1, waiting for transfers between devices, split_width(): d_recv = lax.ppermute(d_pair, 'dp', swap)  14.8 us
    unnamed x58, local copies, waits for them, and re-layouts  13.6 us
    ppermute x12, starting transfers between devices, exchange(): lax.ppermute(blocks[m], 'expert', [(i, i ^ m * stride) for i in range(pee...  10 us
    pallas_call x1, Pallas kernels, split_width(): call(functools.partial(partial_kernel, tile), (shape(rows, ff, dtype=F32)...  7.89 us
    all_to_all x1, starting transfers between devices, split_width(): lax.all_to_all(dx_send.reshape(2 * peers, 2 * cap, quarter), ('dp', 'expe...  6.96 us
    all_to_all x1, starting transfers between devices, split_width(): lax.all_to_all(tok_send.reshape(2 * peers, 2 * cap, quarter), ('dp', 'exp...  6.3 us
  transfers between devices with their start and end apart: 19, of which 9 were waited for; matrix products, arithmetic and copies ran while one was open for 0% of the time, Pallas kernels for 15%

profile of v2, /device:TPU:17, one launch (start us, length us, event | category | flops | bytes accessed | tf_op | source)
XLA Modules:
  0.0 170.6 jit_solution(12849226179756282835)
XLA Ops:
  0.6 1.0 copy-done.3
  1.7 0.7 copy-done.15
  2.4 1.7 shard_map.94
  4.1 6.3 %all-to-all-start = ((bf16[32,40,512]{2,1,0:T(8,128)(2,1)}), bf16[32,40,512]{2,1,0:T(8,128)(2,1)}, u32[]{:S(2)}, u32[]{:S(2)}) async-start(bf16[32,40,512]{2,1,0:T(8,128)(2,1)} %bitcast.2), calls=%async_computation | async-start | bytes 2621440 | tf_op jit(solution)/shard_map/all_to_all | solution.py:306
  10.4 1.2 collective-permute-start.4
  11.8 1.0 copy-done.22
  12.8 1.1 shard_map.95
  13.9 0.7 collective-permute-start
  14.6 1.2 collective-permute-start.1
  16.6 12.1 %collective-permute-done.1.refs_2_ = bf16[4,40,1024]{2,1,0:T(8,128)(2,1)S(1)} collective-permute-done((bf16[4,40,1024]{2,1,0:T(8,128)(2,1)S(1)}, bf16[4,40,1024]{2,1,0:T(8,128)(2,1)S(1)}, u32[]{:S(2)}, u32[]{:S(2)}) %collective-permute-start.1) | collective-permute-done | bytes 327712 | tf_op jit(solution)/shard_map/ppermute | solution.py:270
  28.6 12.6 %collective-permute-done.2.refs_3_ = bf16[4,40,1024]{2,1,0:T(8,128)(2,1)S(1)} collective-permute-done((bf16[4,40,1024]{2,1,0:T(8,128)(2,1)S(1)}, bf16[4,40,1024]{2,1,0:T(8,128)(2,1)S(1)}, u32[]{:S(2)}, u32[]{:S(2)}) %collective-permute-start.2) | collective-permute-done | bytes 327712 | tf_op jit(solution)/shard_map/ppermute | solution.py:270
  41.2 1.1 shard_map.96
  42.4 1.4 copy-done.17
  43.8 1.4 copy-done.19
  45.2 7.9 %shard_map.97 = (f32[320,768]{1,0:T(8,128)S(1)}, f32[320,768]{1,0:T(8,128)S(1)}, bf16[2,320,768]{2,1,0:T(8,128)(2,1)S(1)}) custom-call(s32[1]{0:T(128)} %bitcast.group_ref, s32[640,1]{1,0:T(8,128)S(1)} %broadcast_in_dim.21.target_ref, bf16[2,640,512]{2,1,0:T(8,128)(2,1)} %bitcast.3.recv_ref, bf16[1024,768]{1,0:T(8,128)(2,1)S(1)} %bitcast.29, ...), custom_call_target="tpu_custom_call" | custom-call | flops 2013265920 | bytes 4456448 | tf_op jit(solution)/shard_map/pallas_call | solution.py:314
  53.1 0.9 collective-permute-start.3
  54.0 1.3 collective-permute-start.5
  55.3 1.4 collective-permute-start.7
  56.9 3.2 %collective-permute-done.4.other_ref = bf16[1024,768]{1,0:T(8,128)(2,1)S(1)} collective-permute-done((bf16[1024,768]{1,0:T(8,128)(2,1)S(1)}, bf16[1024,768]{1,0:T(8,128)(2,1)S(1)}, u32[]{:S(2)}, u32[]{:S(2)}) %collective-permute-start.4) | collective-permute-done | bytes 1572896 | tf_op jit(solution)/shard_map/ppermute | solution.py:285
  60.1 7.3 %collective-permute-done.5 = bf16[4,40,1024]{2,1,0:T(8,128)(2,1)S(1)} collective-permute-done((bf16[4,40,1024]{2,1,0:T(8,128)(2,1)S(1)}, bf16[4,40,1024]{2,1,0:T(8,128)(2,1)S(1)}, u32[]{:S(2)}, u32[]{:S(2)}) %collective-permute-start.5) | collective-permute-done | bytes 327712 | tf_op jit(solution)/shard_map/ppermute | solution.py:270
  67.4 1.9 %collective-permute-done.6 = bf16[4,40,1024]{2,1,0:T(8,128)(2,1)S(1)} collective-permute-done((bf16[4,40,1024]{2,1,0:T(8,128)(2,1)S(1)}, bf16[4,40,1024]{2,1,0:T(8,128)(2,1)S(1)}, u32[]{:S(2)}, u32[]{:S(2)}) %collective-permute-start.6) | collective-permute-done | bytes 327712 | tf_op jit(solution)/shard_map/ppermute | solution.py:270
  69.3 15.6 %collective-permute-done.7 = bf16[4,40,1024]{2,1,0:T(8,128)(2,1)S(1)} collective-permute-done((bf16[4,40,1024]{2,1,0:T(8,128)(2,1)S(1)}, bf16[4,40,1024]{2,1,0:T(8,128)(2,1)S(1)}, u32[]{:S(2)}, u32[]{:S(2)}) %collective-permute-start.7) | collective-permute-done | bytes 327712 | tf_op jit(solution)/shard_map/ppermute | solution.py:270
  84.9 3.6 %shard_map.98 = (bf16[320,768]{1,0:T(8,128)(2,1)S(1)}, bf16[2,320,768]{2,1,0:T(8,128)(2,1)S(1)}, bf16[320,1024]{1,0:T(8,128)(2,1)S(1)}, bf16[320,1024]{1,0:T(8,128)(2,1)S(1)}) custom-call(s32[640,1]{1,0:T(8,128)S(1)} %broadcast_in_dim.20.target_ref, f32[320,768]{1,0:T(8,128)S(1)} %get-tuple-element.50.gate_ref, f32[320,768]{1,0:T(8,128)S(1)} %get-tuple-element.51.up_ref, ...), custom_call_target="tpu_custom_call" | custom-call | flops 1006632960 | bytes 4456448 | tf_op jit(solution)/shard_map/pallas_call | solution.py:331
  88.4 0.9 copy-done.21
  89.3 0.8 collective-permute-start.8
  90.1 0.7 collective-permute-start.12
  90.8 2.7 %shard_map.99 = (bf16[4,40,1024]{2,1,0:T(8,128)(2,1)S(1)}, bf16[4,40,1024]{2,1,0:T(8,128)(2,1)S(1)}, bf16[4,40,1024]{2,1,0:T(8,128)(2,1)S(1)}, bf16[4,40,1024]{2,1,0:T(8,128)(2,1)S(1)}) custom-call(s32[1,640]{1,0:T(1,128)S(1)} %broadcast_in_dim.18.target_ref, bf16[320,768]{1,0:T(8,128)(2,1)S(1)} %get-tuple-element.58.hid_ref, ...), custom_call_target="tpu_custom_call" | custom-call | flops 1006632960 | bytes 4456448 | tf_op jit(solution)/shard_map/pallas_call | solution.py:346
  93.6 1.4 collective-permute-start.10
  94.9 1.3 collective-permute-start.11
  96.2 14.8 %collective-permute-done.8.recv_ref = bf16[2,320,768]{2,1,0:T(8,128)(2,1)S(1)} collective-permute-done((bf16[2,320,768]{2,1,0:T(8,128)(2,1)S(1)}, bf16[2,320,768]{2,1,0:T(8,128)(2,1)S(1)}, u32[]{:S(2)}, u32[]{:S(2)}) %collective-permute-start.8) | collective-permute-done | bytes 983072 | tf_op jit(solution)/shard_map/ppermute | solution.py:357
  111.0 4.4 %shard_map.100 = bf16[2,640,512]{2,1,0:T(8,128)(2,1)} custom-call(s32[1]{0:T(128)} %bitcast.group_ref, s32[1,640]{1,0:T(1,128)S(1)} %broadcast_in_dim.15.target_ref, bf16[2,320,768]{2,1,0:T(8,128)(2,1)S(1)} %get-tuple-element.57.own_ref, bf16[2,320,768]{2,1,0:T(8,128)(2,1)S(1)} %collective-permute-done.8.recv_ref, bf16[1024,768]{1,0:T(8,128)(2,1)S(1)} %bitcast.30, ...), custom_call_target="tpu_custom_call" | custom-call | flops 2013265920 | bytes 4456448 | tf_op jit(solution)/shard_map/pallas_call | solution.py:362
  115.3 0.7 copy-done.8
  116.1 0.7 copy-done.10
  116.8 5.9 %collective-permute-done.11.refs_3_ = bf16[4,40,1024]{2,1,0:T(8,128)(2,1)S(1)} collective-permute-done((bf16[4,40,1024]{2,1,0:T(8,128)(2,1)S(1)}, bf16[4,40,1024]{2,1,0:T(8,128)(2,1)S(1)}, u32[]{:S(2)}, u32[]{:S(2)}) %collective-permute-start.11) | collective-permute-done | bytes 327712 | tf_op jit(solution)/shard_map/ppermute | solution.py:270
  122.7 0.7 copy-done.12
  123.4 0.8 copy-done.6
  124.2 7.0 %all-to-all-start.1 = ((bf16[32,40,512]{2,1,0:T(8,128)(2,1)}), bf16[32,40,512]{2,1,0:T(8,128)(2,1)S(1)}, u32[]{:S(2)}, u32[]{:S(2)}) async-start(bf16[32,40,512]{2,1,0:T(8,128)(2,1)} %bitcast.12), calls=%async_computation.1 | async-start | bytes 2621440 | tf_op jit(solution)/shard_map/all_to_all | solution.py:381
  131.1 1.2 collective-permute-start.16
  132.4 1.0 copy-done.9
  133.4 1.0 copy-done.11
  134.3 1.0 copy-done.13
  135.3 1.2 shard_map.101
  137.1 1.2 collective-permute-start.14
  138.9 22.1 %collective-permute-done.16.recv_ref = bf16[320,1024]{1,0:T(8,128)(2,1)S(1)} collective-permute-done((bf16[320,1024]{1,0:T(8,128)(2,1)}, bf16[320,1024]{1,0:T(8,128)(2,1)S(1)}, u32[]{:S(2)}, u32[]{:S(2)}) %collective-permute-start.16) | collective-permute-done | bytes 655392 | tf_op jit(solution)/shard_map/ppermute | solution.py:358
  160.9 1.0 copy-done.7
  162.0 3.5 %shard_map.103 = bf16[1024,768]{1,0:T(8,128)(2,1)} custom-call(bf16[320,1024]{1,0:T(8,128)(2,1)S(1)} %copy-done.2, bf16[320,1024]{1,0:T(8,128)(2,1)S(1)} %collective-permute-done.16.recv_ref, bf16[320,768]{1,0:T(8,128)(2,1)S(1)} %copy-done.5, bf16[320,768]{1,0:T(8,128)(2,1)S(1)} %copy-done.7), custom_call_target="tpu_custom_call" | custom-call | flops 1006632960 | bytes 2883584 | tf_op jit(solution)/shard_map/pallas_call | solution.py:386
  165.5 3.4 %shard_map.102 = bf16[128,2048]{1,0:T(8,128)(2,1)} custom-call(s32[1]{0:T(128)} %bitcast.group_ref, s32[1]{0:T(128)} %bitcast.4.expert_ref, s32[128,2]{1,0:T(8,128)S(1)} %copy.17.slots_ref, f32[128,2]{1,0:T(8,128)S(1)} %copy.14.gates_ref, bf16[160,1024]{1,0:T(8,128)(2,1)S(1)} %bitcast.33, bf16[160,1024]{1,0:T(8,128)(2,1)} %bitcast.15.refs_1_, ...), custom_call_target="tpu_custom_call" | custom-call | flops 671088640 | bytes 1835008 | tf_op jit(solution)/shard_map/pallas_call | solution.py:395
  168.8 1.8 %shard_map.104 = bf16[128,2048]{1,0:T(8,128)(2,1)} custom-call(s32[128,2]{1,0:T(8,128)S(1)} %copy.17.slots_ref, bf16[2,640,512]{2,1,0:T(8,128)(2,1)S(1)} %bitcast.19), custom_call_target="tpu_custom_call" | custom-call | flops 335544320 | bytes 1835008 | tf_op jit(solution)/shard_map/pallas_call | solution.py:407
  (67 shorter events, 2.4 us)
Async XLA Ops:
  0.6 1.0 copy-start.3
  1.7 0.7 copy-start.15
  4.1 6.3 %copy-start = (bf16[1,1024,768]{2,1,0:T(8,128)(2,1)S(1)}, bf16[1,1024,768]{2,1,0:T(8,128)(2,1)}, u32[]{:S(2)}) copy-start(bf16[1,1024,768]{2,1,0:T(8,128)(2,1)} %param.13) | copy-start | bytes 4718596
  4.1 7.6 %copy-start.24 = (f32[128,2]{0,1:T(2,128)S(1)}, f32[128,2]{0,1:T(2,128)}, u32[]{:S(2)}) copy-start(f32[128,2]{0,1:T(2,128)} %param.9) | copy-start | bytes 3076
  4.1 7.7 %copy-start.16 = (s32[128,2]{0,1:T(2,128)S(1)}, s32[128,2]{0,1:T(2,128)}, u32[]{:S(2)}) copy-start(s32[128,2]{0,1:T(2,128)} %param.10) | copy-start | bytes 3076
  4.1 38.3 %all-to-all-start = ((bf16[32,40,512]{2,1,0:T(8,128)(2,1)}), bf16[32,40,512]{2,1,0:T(8,128)(2,1)}, u32[]{:S(2)}, u32[]{:S(2)}) async-start(bf16[32,40,512]{2,1,0:T(8,128)(2,1)} %bitcast.2), calls=%async_computation | async-start | bytes 2621440 | tf_op jit(solution)/shard_map/all_to_all | solution.py:306
  10.4 49.7 %collective-permute-start.4 = (bf16[1024,768]{1,0:T(8,128)(2,1)S(1)}, bf16[1024,768]{1,0:T(8,128)(2,1)S(1)}, u32[]{:S(2)}, u32[]{:S(2)}) collective-permute-start(bf16[1024,768]{1,0:T(8,128)(2,1)S(1)} %bitcast.20), channel_id=1, source_target_pairs={{0,16},{16,0},{1,17},{17,1},{2,18},{18,2},{3,19},{19,3},{4,20},{20... | collective-permute-start | bytes 4718600 | tf_op jit(solution)/shard_map/ppermute | solution.py:285
  11.7 1.0 copy-start.22
  13.9 2.7 %collective-permute-start = (bf16[4,40,1024]{2,1,0:T(8,128)(2,1)S(1)}, bf16[4,40,1024]{2,1,0:T(8,128)(2,1)S(1)}, u32[]{:S(2)}, u32[]{:S(2)}) collective-permute-start(bf16[4,40,1024]{2,1,0:T(8,128)(2,1)S(1)} %get-tuple-element.42), channel_id=1, source_target_pairs={{0,1},{1,0},{2,3},{3,2},{4,5},{5,4},{6,7},{7,6},{8,9},{9,8},{10,11... | collective-permute-start | bytes 983048 | tf_op jit(solution)/shard_map/ppermute | solution.py:270
  14.6 14.0 %collective-permute-start.1 = (bf16[4,40,1024]{2,1,0:T(8,128)(2,1)S(1)}, bf16[4,40,1024]{2,1,0:T(8,128)(2,1)S(1)}, u32[]{:S(2)}, u32[]{:S(2)}) collective-permute-start(bf16[4,40,1024]{2,1,0:T(8,128)(2,1)S(1)} %get-tuple-element.43), channel_id=1, source_target_pairs={{0,2},{1,3},{2,0},{3,1},{4,6},{5,7},{6,4},{7,5},{8,10},{9,11},{10,... | collective-permute-start | bytes 983048 | tf_op jit(solution)/shard_map/ppermute | solution.py:270
  15.8 25.4 %collective-permute-start.2 = (bf16[4,40,1024]{2,1,0:T(8,128)(2,1)S(1)}, bf16[4,40,1024]{2,1,0:T(8,128)(2,1)S(1)}, u32[]{:S(2)}, u32[]{:S(2)}) collective-permute-start(bf16[4,40,1024]{2,1,0:T(8,128)(2,1)S(1)} %get-tuple-element.44), channel_id=1, source_target_pairs={{0,3},{1,2},{2,1},{3,0},{4,7},{5,6},{6,5},{7,4},{8,11},{9,10},{10,... | collective-permute-start | bytes 983048 | tf_op jit(solution)/shard_map/ppermute | solution.py:270
  42.4 1.4 copy-start.17
  43.8 1.4 copy-start.19
  45.2 8.9 %copy-start.27 = (bf16[4,40,1024]{2,1,0:T(8,128)(2,1)S(1)}, bf16[4,40,1024]{2,1,0:T(8,128)(2,1)}, u32[]{:S(2)}) copy-start(bf16[4,40,1024]{2,1,0:T(8,128)(2,1)} %get-tuple-element.54) | copy-start | bytes 983044
  45.2 10.1 %copy-start.26 = (bf16[4,40,1024]{2,1,0:T(8,128)(2,1)S(1)}, bf16[4,40,1024]{2,1,0:T(8,128)(2,1)}, u32[]{:S(2)}) copy-start(bf16[4,40,1024]{2,1,0:T(8,128)(2,1)} %get-tuple-element.55) | copy-start | bytes 983044
  45.2 10.2 %copy-start.25 = (bf16[4,40,1024]{2,1,0:T(8,128)(2,1)S(1)}, bf16[4,40,1024]{2,1,0:T(8,128)(2,1)}, u32[]{:S(2)}) copy-start(bf16[4,40,1024]{2,1,0:T(8,128)(2,1)} %get-tuple-element.56) | copy-start | bytes 983044
  45.2 39.7 %copy-start.14 = (bf16[4,40,1024]{2,1,0:T(8,128)(2,1)S(1)}, bf16[4,40,1024]{2,1,0:T(8,128)(2,1)}, u32[]{:S(2)}) copy-start(bf16[4,40,1024]{2,1,0:T(8,128)(2,1)} %get-tuple-element.53) | copy-start | bytes 983044
  53.1 31.8 %collective-permute-start.3 = (bf16[2,320,768]{2,1,0:T(8,128)(2,1)S(1)}, bf16[2,320,768]{2,1,0:T(8,128)(2,1)S(1)}, u32[]{:S(2)}, u32[]{:S(2)}) collective-permute-start(bf16[2,320,768]{2,1,0:T(8,128)(2,1)S(1)} %get-tuple-element.52), channel_id=1, source_target_pairs={{0,16},{16,0},{1,17},{17,1},{2,18},{18,2},{3,19},{19,3},{4,20},{20... | collective-permute-start | bytes 2949128 | tf_op jit(solution)/shard_map/ppermute | solution.py:328
  54.0 13.4 %collective-permute-start.5 = (bf16[4,40,1024]{2,1,0:T(8,128)(2,1)S(1)}, bf16[4,40,1024]{2,1,0:T(8,128)(2,1)S(1)}, u32[]{:S(2)}, u32[]{:S(2)}) collective-permute-start(bf16[4,40,1024]{2,1,0:T(8,128)(2,1)S(1)} %copy-done.27), channel_id=1, source_target_pairs={{0,4},{1,5},{2,6},{3,7},{4,0},{5,1},{6,2},{7,3},{8,12},{9,13},{10,... | collective-permute-start | bytes 983048 | tf_op jit(solution)/shard_map/ppermute | solution.py:270
  55.3 14.0 %collective-permute-start.6 = (bf16[4,40,1024]{2,1,0:T(8,128)(2,1)S(1)}, bf16[4,40,1024]{2,1,0:T(8,128)(2,1)S(1)}, u32[]{:S(2)}, u32[]{:S(2)}) collective-permute-start(bf16[4,40,1024]{2,1,0:T(8,128)(2,1)S(1)} %copy-done.26), channel_id=1, source_target_pairs={{0,8},{1,9},{2,10},{3,11},{4,12},{5,13},{6,14},{7,15},{8,0},{9,1},... | collective-permute-start | bytes 983048 | tf_op jit(solution)/shard_map/ppermute | solution.py:270
  55.3 29.5 %collective-permute-start.7 = (bf16[4,40,1024]{2,1,0:T(8,128)(2,1)S(1)}, bf16[4,40,1024]{2,1,0:T(8,128)(2,1)S(1)}, u32[]{:S(2)}, u32[]{:S(2)}) collective-permute-start(bf16[4,40,1024]{2,1,0:T(8,128)(2,1)S(1)} %copy-done.25), channel_id=1, source_target_pairs={{0,12},{1,13},{2,14},{3,15},{4,8},{5,9},{6,10},{7,11},{8,4},{9,5},... | collective-permute-start | bytes 983048 | tf_op jit(solution)/shard_map/ppermute | solution.py:270
  88.4 0.9 copy-start.21
  89.3 4.2 %copy-start.1 = (bf16[320,1024]{1,0:T(8,128)(2,1)}, bf16[320,1024]{1,0:T(8,128)(2,1)S(1)}, u32[]{:S(2)}) copy-start(bf16[320,1024]{1,0:T(8,128)(2,1)S(1)} %get-tuple-element.73.mine_ref) | copy-start | bytes 1966084
  89.3 4.2 %copy-start.4 = (bf16[320,768]{1,0:T(8,128)(2,1)}, bf16[320,768]{1,0:T(8,128)(2,1)S(1)}, u32[]{:S(2)}) copy-start(bf16[320,768]{1,0:T(8,128)(2,1)S(1)} %get-tuple-element.58.hid_ref) | copy-start | bytes 1474564
  89.3 21.7 %collective-permute-start.8 = (bf16[2,320,768]{2,1,0:T(8,128)(2,1)S(1)}, bf16[2,320,768]{2,1,0:T(8,128)(2,1)S(1)}, u32[]{:S(2)}, u32[]{:S(2)}) collective-permute-start(bf16[2,320,768]{2,1,0:T(8,128)(2,1)S(1)} %get-tuple-element.57.own_ref), channel_id=1, source_target_pairs={{0,16},{16,0},{1,17},{17,1},{2,18},{18,2},{3,19},{19,3},{4,20},{20... | collective-permute-start | bytes 2949128 | tf_op jit(solution)/shard_map/ppermute | solution.py:357
  90.1 33.3 %collective-permute-start.12 = (bf16[320,768]{1,0:T(8,128)(2,1)S(1)}, bf16[320,768]{1,0:T(8,128)(2,1)S(1)}, u32[]{:S(2)}, u32[]{:S(2)}) collective-permute-start(bf16[320,768]{1,0:T(8,128)(2,1)S(1)} %get-tuple-element.58.hid_ref), channel_id=1, source_target_pairs={{0,16},{16,0},{1,17},{17,1},{2,18},{18,2},{3,19},{19,3},{4,20},{20... | collective-permute-start | bytes 1474568 | tf_op jit(solution)/shard_map/ppermute | solution.py:356
  90.8 20.2 %copy-start.18 = (bf16[1,1024,768]{2,1,0:T(8,128)(2,1)S(1)}, bf16[1,1024,768]{2,1,0:T(8,128)(2,1)}, u32[]{:S(2)}) copy-start(bf16[1,1024,768]{2,1,0:T(8,128)(2,1)} %param.11) | copy-start | bytes 4718596
  90.8 20.2 %copy-start.20 = (bf16[1,1024,768]{2,1,0:T(8,128)(2,1)S(1)}, bf16[1,1024,768]{2,1,0:T(8,128)(2,1)}, u32[]{:S(2)}) copy-start(bf16[1,1024,768]{2,1,0:T(8,128)(2,1)} %param.12) | copy-start | bytes 4718596
  93.5 21.8 %collective-permute-start.9 = (bf16[4,40,1024]{2,1,0:T(8,128)(2,1)S(1)}, bf16[4,40,1024]{2,1,0:T(8,128)(2,1)S(1)}, u32[]{:S(2)}, u32[]{:S(2)}) collective-permute-start(bf16[4,40,1024]{2,1,0:T(8,128)(2,1)S(1)} %get-tuple-element.60), channel_id=1, source_target_pairs={{0,4},{1,5},{2,6},{3,7},{4,0},{5,1},{6,2},{7,3},{8,12},{9,13},{10,... | collective-permute-start | bytes 983048 | tf_op jit(solution)/shard_map/ppermute | solution.py:270
  93.6 22.5 %collective-permute-start.10 = (bf16[4,40,1024]{2,1,0:T(8,128)(2,1)S(1)}, bf16[4,40,1024]{2,1,0:T(8,128)(2,1)S(1)}, u32[]{:S(2)}, u32[]{:S(2)}) collective-permute-start(bf16[4,40,1024]{2,1,0:T(8,128)(2,1)S(1)} %get-tuple-element.61), channel_id=1, source_target_pairs={{0,8},{1,9},{2,10},{3,11},{4,12},{5,13},{6,14},{7,15},{8,0},{9,1},... | collective-permute-start | bytes 983048 | tf_op jit(solution)/shard_map/ppermute | solution.py:270
  94.9 27.7 %collective-permute-start.11 = (bf16[4,40,1024]{2,1,0:T(8,128)(2,1)S(1)}, bf16[4,40,1024]{2,1,0:T(8,128)(2,1)S(1)}, u32[]{:S(2)}, u32[]{:S(2)}) collective-permute-start(bf16[4,40,1024]{2,1,0:T(8,128)(2,1)S(1)} %get-tuple-element.62), channel_id=1, source_target_pairs={{0,12},{1,13},{2,14},{3,15},{4,8},{5,9},{6,10},{7,11},{8,4},{9,5},... | collective-permute-start | bytes 983048 | tf_op jit(solution)/shard_map/ppermute | solution.py:270
  115.3 0.7 copy-start.8
  116.1 0.7 copy-start.10
  122.7 0.7 copy-start.12
  123.4 0.8 copy-start.6
  124.2 36.8 %copy-start.2 = (bf16[320,1024]{1,0:T(8,128)(2,1)S(1)}, bf16[320,1024]{1,0:T(8,128)(2,1)}, u32[]{:S(2)}) copy-start(bf16[320,1024]{1,0:T(8,128)(2,1)} %copy-done.1) | copy-start | bytes 1966084
  124.2 36.8 %copy-start.5 = (bf16[320,768]{1,0:T(8,128)(2,1)S(1)}, bf16[320,768]{1,0:T(8,128)(2,1)}, u32[]{:S(2)}) copy-start(bf16[320,768]{1,0:T(8,128)(2,1)} %copy-done.4) | copy-start | bytes 1474564
  124.2 44.7 %all-to-all-start.1 = ((bf16[32,40,512]{2,1,0:T(8,128)(2,1)}), bf16[32,40,512]{2,1,0:T(8,128)(2,1)S(1)}, u32[]{:S(2)}, u32[]{:S(2)}) async-start(bf16[32,40,512]{2,1,0:T(8,128)(2,1)} %bitcast.12), calls=%async_computation.1 | async-start | bytes 2621440 | tf_op jit(solution)/shard_map/all_to_all | solution.py:381
  131.1 29.8 %collective-permute-start.16 = (bf16[320,1024]{1,0:T(8,128)(2,1)}, bf16[320,1024]{1,0:T(8,128)(2,1)S(1)}, u32[]{:S(2)}, u32[]{:S(2)}) collective-permute-start(bf16[320,1024]{1,0:T(8,128)(2,1)} %copy-done.21), channel_id=1, source_target_pairs={{0,16},{16,0},{1,17},{17,1},{2,18},{18,2},{3,19},{19,3},{4,20},{20... | collective-permute-start | bytes 1966088 | tf_op jit(solution)/shard_map/ppermute | solution.py:358
  132.4 1.0 copy-start.9
  133.4 1.0 copy-start.11
  134.3 1.0 copy-start.13
  136.5 29.0 %collective-permute-start.13 = (bf16[4,40,1024]{2,1,0:T(8,128)(2,1)}, bf16[4,40,1024]{2,1,0:T(8,128)(2,1)}, u32[]{:S(2)}, u32[]{:S(2)}) collective-permute-start(bf16[4,40,1024]{2,1,0:T(8,128)(2,1)} %get-tuple-element.70), channel_id=1, source_target_pairs={{0,1},{1,0},{2,3},{3,2},{4,5},{5,4},{6,7},{7,6},{8,9},{9,8},{10,11... | collective-permute-start | bytes 983048 | tf_op jit(solution)/shard_map/ppermute | solution.py:270
  137.1 28.3 %collective-permute-start.14 = (bf16[4,40,1024]{2,1,0:T(8,128)(2,1)}, bf16[4,40,1024]{2,1,0:T(8,128)(2,1)}, u32[]{:S(2)}, u32[]{:S(2)}) collective-permute-start(bf16[4,40,1024]{2,1,0:T(8,128)(2,1)} %get-tuple-element.71), channel_id=1, source_target_pairs={{0,2},{1,3},{2,0},{3,1},{4,6},{5,7},{6,4},{7,5},{8,10},{9,11},{10,... | collective-permute-start | bytes 983048 | tf_op jit(solution)/shard_map/ppermute | solution.py:270
  138.3 27.1 %collective-permute-start.15 = (bf16[4,40,1024]{2,1,0:T(8,128)(2,1)}, bf16[4,40,1024]{2,1,0:T(8,128)(2,1)}, u32[]{:S(2)}, u32[]{:S(2)}) collective-permute-start(bf16[4,40,1024]{2,1,0:T(8,128)(2,1)} %get-tuple-element.72), channel_id=1, source_target_pairs={{0,3},{1,2},{2,1},{3,0},{4,7},{5,6},{6,5},{7,4},{8,11},{9,10},{10,... | collective-permute-start | bytes 983048 | tf_op jit(solution)/shard_map/ppermute | solution.py:270
  160.9 1.0 copy-start.7
  162.0 3.5 %copy-start.23 = (bf16[4,40,1024]{2,1,0:T(8,128)(2,1)S(1)}, bf16[4,40,1024]{2,1,0:T(8,128)(2,1)}, u32[]{:S(2)}) copy-start(bf16[4,40,1024]{2,1,0:T(8,128)(2,1)} %get-tuple-element.69) | copy-start | bytes 983044

commit v3 on v2

--- a/solution.py
+++ b/solution.py
@@ -46,6 +46,7 @@
     return pl.ds(pl.multiple_of(group * half, 128), half)
 
 
+AHEAD_OF_PARTIAL, AHEAD_OF_BACKWARD, AHEAD_OF_REGROUP = (int(each) for each in (20e9, 8e9, 20e9))
 SCALAR = pl.BlockSpec(memory_space=pltpu.SMEM)
 HBM = pl.BlockSpec(memory_space=pltpu.HBM)
 
@@ -116,10 +117,12 @@
             out_ref[m] = block_ref[i]
 
 
-def partial_kernel(
-    tile, group_ref, target_ref, recv_ref, wg_ref, wu_ref, gate_ref, up_ref, send_ref, x_ref, w_ref, sems
-):
-    rows, ff = gate_ref.shape
+def pick_kernel(target_ref, out_ref):
+    out_ref[...] = ones_where(iota(out_ref.shape, 1) == target_ref[...])
+
+
+def partial_kernel(tile, group_ref, pick_ref, recv_ref, wg_ref, wu_ref, out_ref, x_ref, w_ref, sems):
+    _, rows, ff = out_ref.shape
     width = recv_ref.shape[2]
     copies = {}
     for t in range(ff // tile):
@@ -127,24 +130,18 @@
         for i, ref in enumerate((wg_ref, wu_ref)):
             copies[t, i] = pltpu.make_async_copy(ref.at[:, columns], w_ref.at[i, :, columns], sems.at[i, t])
             copies[t, i].start()
-    pick = ones_where(iota((2 * rows, 2 * rows), 1) == target_ref[...])
-    for o, g in enumerate((group_ref[0], 1 - group_ref[0])):
-        for h in range(2):
-            x_ref[o * rows : (o + 1) * rows, h * width : (h + 1) * width] = mm(
-                pick[h * rows : (h + 1) * rows], recv_ref[g]
-            ).astype(BF16)
+    for h in range(2):
+        x_ref[:, h * width : (h + 1) * width] = mm(pick_ref[h * rows : (h + 1) * rows, :], recv_ref[0]).astype(BF16)
     for t in range(ff // tile):
         columns = slice(t * tile, (t + 1) * tile)
-        for i, mine_ref in enumerate((gate_ref, up_ref)):
+        for i in range(2):
             copies[t, i].wait()
-            both = mm(x_ref[...], w_ref[i, :, columns])
-            mine_ref[:, columns] = both[:rows]
-            send_ref[i, :, columns] = both[rows:].astype(BF16)
-
-
-def backward_kernel(target_ref, gate_ref, up_ref, recv_ref, own_ref, other_ref, *refs):
-    *came_refs, hid_ref, out_ref, dy_mine_ref, dy_send_ref, came_ref = refs
-    rows = gate_ref.shape[0]
+            out_ref[i, :, columns] = mm(x_ref[...], w_ref[i, :, columns]).astype(out_ref.dtype)
+
+
+def hidden_grad_kernel(target_ref, own_ref, other_ref, *refs):
+    *came_refs, out_ref, dy_mine_ref, dy_send_ref, came_ref = refs
+    rows = out_ref.shape[0]
 
     @pl.when(pl.program_id(0) == 0)
     def _():
@@ -156,14 +153,18 @@
         dy_mine_ref[...] = dy[:rows]
         dy_send_ref[...] = dy[rows:]
 
-    gate = gate_ref[...] + recv_ref[0].astype(F32)
-    up = up_ref[...] + recv_ref[1].astype(F32)
+    out_ref[...] = mm(dy_mine_ref[...], own_ref[...]) + mm(dy_send_ref[...], other_ref[...])
+
+
+def pointwise_kernel(mine_ref, recv_ref, d_hidden_ref, hid_ref, out_ref):
+    gate = mine_ref[0] + recv_ref[0].astype(F32)
+    up = mine_ref[1] + recv_ref[1].astype(F32)
     sigma = jax.nn.sigmoid(gate)
     active = gate * sigma
-    hid_ref[...] = (active * up).astype(BF16)
-    d_hidden = mm(dy_mine_ref[...], own_ref[...]) + mm(dy_send_ref[...], other_ref[...])
+    d_hidden = d_hidden_ref[...]
     out_ref[0] = (d_hidden * up * sigma * (1.0 + gate * (1.0 - sigma))).astype(BF16)
     out_ref[1] = (d_hidden * active).astype(BF16)
+    hid_ref[...] = (active * up).astype(BF16)
 
 
 def forward_kernel(target_ref, hid_ref, own_ref, other_ref, *refs):
@@ -180,21 +181,16 @@
     spread(mm(pick_ref[...], y_ref[...]), out_refs, slice(None), out_refs[0].shape[1])
 
 
-def input_grad_kernel(group_ref, target_ref, own_ref, recv_ref, wg_ref, wu_ref, out_ref, d_ref, dx_ref):
-    rows = own_ref.shape[1]
+def input_grad_kernel(other, group_ref, target_ref, d_ref, wg_ref, wu_ref, *refs):
+    *_, out_ref, dx_ref = refs
+    rows = d_ref.shape[1]
     width = out_ref.shape[2]
-    for i in range(2):
-        d_ref[i, :rows, :] = own_ref[i]
-        d_ref[i, rows:, :] = recv_ref[i]
     for h in range(2):
         part = slice(h * width, (h + 1) * width)
-        dx = (mm(d_ref[0], wg_ref[part, :], NT) + mm(d_ref[1], wu_ref[part, :], NT)).astype(BF16)
-        for o in range(2):
-            dx_ref[o, h * rows : (h + 1) * rows, :] = dx[o * rows : (o + 1) * rows]
+        dx = mm(d_ref[0], wg_ref[part, :], NT) + mm(d_ref[1], wu_ref[part, :], NT)
+        dx_ref[h * rows : (h + 1) * rows, :] = dx.astype(BF16)
     pick = ones_where(iota((2 * rows, 2 * rows), 0) == target_ref[...])
-    group = group_ref[0]
-    out_ref[group] = mm(pick, dx_ref[0]).astype(BF16)
-    out_ref[1 - group] = mm(pick, dx_ref[1]).astype(BF16)
+    out_ref[0] = mm(pick, dx_ref[...]).astype(BF16)
 
 
 def down_kernel(mine_ref, recv_ref, hid_ref, hid_recv_ref, out_ref):
@@ -271,7 +267,7 @@
             for m in range(1, len(blocks))
         ]
 
-    def regroup(blocks):
+    def regroup(blocks, hold=0):
         outs, *rest = blocks[0].shape
         return call(
             functools.partial(regroup_kernel, len(blocks)),
@@ -279,6 +275,7 @@
             (1,),
             [whole(blocks[0].shape)] * len(blocks),
             tuple(whole((len(blocks), *rest)) for _ in range(outs)),
+            flops=hold,
             moved=8 * rows * half,
         )(*blocks)
 
@@ -306,42 +303,77 @@
     tok_recv = lax.all_to_all(
         tok_send.reshape(2 * peers, 2 * cap, quarter), ("dp", "expert"), 0, 0, tiled=True
     ).reshape(2, 2 * rows, quarter)
-    tok_recv, dy_far = lax.optimization_barrier((tok_recv, dy_far))
 
     part_block = pl.BlockSpec((rows, tile), lambda i: (0, i))
     pair_block = pl.BlockSpec((2, rows, tile), lambda i: (0, 0, i))
     weight_block = pl.BlockSpec((half, tile), lambda i: (0, i))
-    gate_mine, up_mine, part_send = call(
-        functools.partial(partial_kernel, tile),
-        (shape(rows, ff, dtype=F32), shape(rows, ff, dtype=F32), shape(2, rows, ff)),
+    target, *_ = lax.optimization_barrier((straight[:, None], down_other, *dy_far))
+    pick = call(
+        pick_kernel,
+        shape(2 * rows, 2 * rows),
         (1,),
-        [SCALAR, whole((2 * rows, 1)), whole((2, 2 * rows, quarter)), HBM, HBM],
-        (whole((rows, ff)), whole((rows, ff)), whole((2, rows, ff))),
-        [
-            pltpu.VMEM((2 * rows, half), BF16),
-            pltpu.VMEM((2, half, ff), BF16),
-            pltpu.SemaphoreType.DMA((2, ff // tile)),
-        ],
-        flops=2 * matmul_flops,
-        moved=2 * weight_bytes + 4 * rows * half,
-    )(group, straight[:, None], tok_recv, w_gate, w_up)
+        [whole((2 * rows, 1))],
+        whole((2 * rows, 2 * rows)),
+        flops=AHEAD_OF_PARTIAL,
+        moved=8 * rows * rows,
+    )(target)
+
+    def partial(other, dtype, received, hold=0):
+        return pl.pallas_call(
+            functools.partial(partial_kernel, tile),
+            out_shape=shape(2, rows, ff, dtype=dtype),
+            grid_spec=pltpu.PrefetchScalarGridSpec(
+                num_scalar_prefetch=1,
+                grid=(1,),
+                in_specs=[
+                    whole((2 * rows, 2 * rows)),
+                    pl.BlockSpec((1, 2 * rows, quarter), lambda i, g: (other ^ g[0], 0, 0)),
+                    HBM,
+                    HBM,
+                ],
+                out_specs=whole((2, rows, ff)),
+                scratch_shapes=[
+                    pltpu.VMEM((rows, half), BF16),
+                    pltpu.VMEM((2, half, ff), BF16),
+                    pltpu.SemaphoreType.DMA((2, ff // tile)),
+                ],
+            ),
+            cost_estimate=pl.CostEstimate(
+                flops=matmul_flops + hold, bytes_accessed=2 * weight_bytes + 2 * rows * half, transcendentals=0
+            ),
+            compiler_params=pltpu.CompilerParams(vmem_limit_bytes=24 * 2**20),
+        )(
+            group,
+            pick,
+            received,
+            pltpu.with_memory_space_constraint(w_gate, pltpu.HBM),
+            pltpu.with_memory_space_constraint(w_up, pltpu.HBM),
+        )
+
+    part_send = partial(1, BF16, tok_recv)
     part_recv = lax.ppermute(part_send, "dp", swap)
     dy_came = exchange(dy_far, PLANE)
-
-    hidden, d_pair, dy_mine, dy_other = call(
-        backward_kernel,
-        (shape(rows, ff), shape(2, rows, ff), shape(rows, half), shape(rows, half)),
+    part_mine = partial(0, F32, tok_recv)
+
+    d_hidden, dy_mine, dy_other = call(
+        hidden_grad_kernel,
+        (shape(rows, ff, dtype=F32), shape(rows, half), shape(rows, half)),
         (ff // tile,),
-        [whole((2 * rows, 1)), part_block, part_block, pair_block, weight_block, weight_block]
-        + [whole((PLANE * 2 * cap, half))] * planes,
-        (part_block, pair_block, whole((rows, half)), whole((rows, half))),
+        [whole((2 * rows, 1)), weight_block, weight_block] + [whole((PLANE * 2 * cap, half))] * planes,
+        (part_block, whole((rows, half)), whole((rows, half))),
         [pltpu.VMEM((2 * rows, half), BF16)],
-        flops=matmul_flops,
+        flops=matmul_flops + AHEAD_OF_BACKWARD,
         moved=2 * weight_bytes + 4 * rows * half,
-    )(
-        moved[:, None], gate_mine, up_mine, part_recv, w_down, down_other,
-        *(came.reshape(PLANE * 2 * cap, half) for came in dy_came)
-    )
+    )(moved[:, None], w_down, down_other, *(came.reshape(PLANE * 2 * cap, half) for came in dy_came))
+    hidden, d_pair = call(
+        pointwise_kernel,
+        (shape(rows, ff), shape(2, rows, ff)),
+        (ff // tile,),
+        [pair_block, pair_block, part_block],
+        (part_block, pair_block),
+        flops=20 * rows * ff,
+        moved=22 * rows * ff,
+    )(part_mine, part_recv, d_hidden)
     down_rows = pl.BlockSpec((strip, ff), lambda i: (i, 0))
     y_far = call(
         forward_kernel,
@@ -355,29 +387,40 @@
     )(moved[None, :], hidden, w_down, down_other)
     hidden_recv = lax.ppermute(hidden, "dp", swap)
     d_recv = lax.ppermute(d_pair, "dp", swap)
+    dy_other, _ = lax.optimization_barrier((dy_other, d_pair))
     dy_cross = lax.ppermute(dy_other, "dp", swap)
 
     *_, d_recv = lax.optimization_barrier((*y_far, d_recv))
     y_far_came = exchange(y_far, PLANE)
-    dx_send = call(
-        input_grad_kernel,
-        shape(2, 2 * rows, quarter),
-        (1,),
-        [
-            SCALAR,
-            whole((1, 2 * rows)),
-            whole((2, rows, ff)),
-            whole((2, rows, ff)),
-            whole((half, ff)),
-            whole((half, ff)),
-        ],
-        whole((2, 2 * rows, quarter)),
-        [pltpu.VMEM((2, 2 * rows, ff), BF16), pltpu.VMEM((2, 2 * rows, quarter), BF16)],
-        flops=2 * matmul_flops,
-        moved=2 * weight_bytes + 4 * rows * half,
-    )(group, straight[None, :], d_pair, d_recv, w_gate, w_up)
-    dx_send, y_far_came, hidden_recv = lax.optimization_barrier((dx_send, y_far_came, hidden_recv))
-    y_came = exchange(regroup(y_far_came), 1)
+    def input_grad(other, d_rows, *before):
+        return pl.pallas_call(
+            functools.partial(input_grad_kernel, other),
+            out_shape=shape(2, 2 * rows, quarter),
+            grid_spec=pltpu.PrefetchScalarGridSpec(
+                num_scalar_prefetch=1,
+                grid=(1,),
+                in_specs=[
+                    whole((1, 2 * rows)),
+                    whole((2, rows, ff)),
+                    whole((half, ff)),
+                    whole((half, ff)),
+                    *[HBM for _ in before],
+                ],
+                out_specs=pl.BlockSpec((1, 2 * rows, quarter), lambda i, g: (other ^ g[0], 0, 0)),
+                scratch_shapes=[pltpu.VMEM((2 * rows, quarter), BF16)],
+            ),
+            input_output_aliases={5: 0} if before else {},
+            cost_estimate=pl.CostEstimate(
+                flops=matmul_flops, bytes_accessed=2 * weight_bytes + 2 * rows * half, transcendentals=0
+            ),
+            compiler_params=pltpu.CompilerParams(vmem_limit_bytes=24 * 2**20),
+        )(group, straight[None, :], d_rows, w_gate, w_up, *before)
+
+    dx_send = input_grad(1, d_recv, input_grad(0, d_pair))
+    y_far_done = y_far_came
+    _, *y_far_came = lax.optimization_barrier((dy_cross, *y_far_came))
+    y_near = regroup(y_far_came, AHEAD_OF_REGROUP)
+    y_came = exchange(y_near, 1)
     dx_back = lax.all_to_all(
         dx_send.reshape(2 * peers, 2 * cap, quarter), ("dp", "expert"), 0, 0, tiled=True
     ).reshape(2, 2 * rows, quarter)
@@ -403,7 +446,6 @@
         flops=top * route_flops,
         moved=route_bytes,
     )(group, expert, route_slot, route_gates, *(came.reshape(planes * 2 * cap, half) for came in y_came))
-    dx_back, moe_out, down_grad = lax.optimization_barrier((dx_back, moe_out, down_grad))
     token_grad = call(
         functools.partial(combine_grad_kernel, peers, cap),
         shape(count, width),

time: 173 us -> 160 us (0.925)
  waiting for transfers between devices: 95.3 us -> 76.7 us
  Pallas kernels: 32.2 us -> 40.1 us
  local copies, waits for them, and re-layouts: 13.9 us -> 6.19 us
  starting transfers between devices: 28.2 us -> 35.2 us
    ppermute x1, waiting for transfers between devices: 22.1 us -> 0.74 us  [split_width(): dy_cross = lax.ppermute(dy_other, 'dp', swap)]
    ppermute x1, waiting for transfers between devices: 0.01 us -> 8.93 us  [split_width(): hidden_recv = lax.ppermute(hidden, 'dp', swap)]
    unnamed x58 -> x30, local copies, waits for them, and re-layouts: 13.6 us -> 5.87 us
    ppermute x12, starting transfers between devices: 10 us -> 17.7 us  [exchange(): lax.ppermute(blocks[m], 'expert', [(i, i ^ m * stride) for i in range(pee...]
    ppermute x12, waiting for transfers between devices: 55.3 us -> 49.2 us  [exchange(): lax.ppermute(blocks[m], 'expert', [(i, i ^ m * stride) for i in range(pee...]
    pallas_call x3 -> x7, Pallas kernels: 15.8 us -> 20.8 us  [the longest x2 9.39 us: partial(): pl.pallas_call(functools.partial(partial_kernel, tile), out_shape=shape(2...]
    all_to_all x1, waiting for transfers between devices: 0.01 us -> 3.75 us  [split_width(): lax.all_to_all(tok_send.reshape(2 * peers, 2 * cap, quarter), ('dp', 'exp...]
    ppermute x1, waiting for transfers between devices: 14.8 us -> 11.2 us  [split_width(): d_recv = lax.ppermute(d_pair, 'dp', swap)]
  transfers between devices with their start and end apart: 19 -> 19, of which waited for: 9 -> 11; matrix products, arithmetic and copies ran while one was open for 0% -> 0% of each run, Pallas kernels for 15% -> 23%
where the time goes in v3:
time: 160 us; the launch traced here: 159 us
  waiting for transfers between devices  76.7 us (48%)
  Pallas kernels  40.1 us (25%)
  starting transfers between devices  35.2 us (22%)
  local copies, waits for them, and re-layouts  6.19 us (4%)
    ppermute x12, waiting for transfers between devices, exchange(): lax.ppermute(blocks[m], 'expert', [(i, i ^ m * stride) for i in range(pee...  49.2 us
    ppermute x12, starting transfers between devices, exchange(): lax.ppermute(blocks[m], 'expert', [(i, i ^ m * stride) for i in range(pee...  17.7 us
    ppermute x1, waiting for transfers between devices, split_width(): d_recv = lax.ppermute(d_pair, 'dp', swap)  11.2 us
    pallas_call x2, Pallas kernels, partial(): pl.pallas_call(functools.partial(partial_kernel, tile), out_shape=shape(2...  9.39 us
    ppermute x1, waiting for transfers between devices, split_width(): hidden_recv = lax.ppermute(hidden, 'dp', swap)  8.93 us
    all_to_all x1, starting transfers between devices, split_width(): lax.all_to_all(dx_send.reshape(2 * peers, 2 * cap, quarter), ('dp', 'expe...  6.63 us
    unnamed x30, local copies, waits for them, and re-layouts  5.87 us
    all_to_all x1, starting transfers between devices, split_width(): lax.all_to_all(tok_send.reshape(2 * peers, 2 * cap, quarter), ('dp', 'exp...  5.6 us
  transfers between devices with their start and end apart: 19, of which 11 were waited for; matrix products, arithmetic and copies ran while one was open for 0% of the time, Pallas kernels for 23%

profile of v3, /device:TPU:17, one launch (start us, length us, event | category | flops | bytes accessed | tf_op | source)
XLA Modules:
  0.0 159.2 jit_solution(17200871551310185060)
XLA Ops:
  0.6 1.3 collective-permute-start
  1.9 1.0 copy-done.2
  3.0 0.7 copy-done.3
  3.6 1.8 %shard_map.98 = bf16[2,640,512]{2,1,0:T(8,128)(2,1)} custom-call(s32[2,128]{1,0:T(2,128)S(1)} %bitcast.30, bf16[128,2048]{1,0:T(8,128)(2,1)S(1)} %copy-done.2), custom_call_target="tpu_custom_call" | custom-call | flops 335544320 | bytes 1835008 | tf_op jit(solution)/shard_map/pallas_call | solution.py:294
  5.4 5.6 %all-to-all-start = ((bf16[32,40,512]{2,1,0:T(8,128)(2,1)}), bf16[32,40,512]{2,1,0:T(8,128)(2,1)S(1)}, u32[]{:S(2)}, u32[]{:S(2)}) async-start(bf16[32,40,512]{2,1,0:T(8,128)(2,1)} %bitcast.8), calls=%async_computation | async-start | bytes 2621440 | tf_op jit(solution)/shard_map/all_to_all | solution.py:303
  11.1 1.0 copy-done.8
  12.2 1.1 shard_map.94
  13.3 0.4 collective-permute-start.1
  13.7 1.2 collective-permute-start.2
  14.9 0.6 collective-permute-start.3
  15.6 11.8 %collective-permute-done.2.refs_2_ = bf16[4,40,1024]{2,1,0:T(8,128)(2,1)S(1)} collective-permute-done((bf16[4,40,1024]{2,1,0:T(8,128)(2,1)S(1)}, bf16[4,40,1024]{2,1,0:T(8,128)(2,1)S(1)}, u32[]{:S(2)}, u32[]{:S(2)}) %collective-permute-start.2) | collective-permute-done | bytes 327712 | tf_op jit(solution)/shard_map/ppermute | solution.py:266
  27.4 12.7 %collective-permute-done.3.refs_3_ = bf16[4,40,1024]{2,1,0:T(8,128)(2,1)S(1)} collective-permute-done((bf16[4,40,1024]{2,1,0:T(8,128)(2,1)S(1)}, bf16[4,40,1024]{2,1,0:T(8,128)(2,1)S(1)}, u32[]{:S(2)}, u32[]{:S(2)}) %collective-permute-start.3) | collective-permute-done | bytes 327712 | tf_op jit(solution)/shard_map/ppermute | solution.py:266
  40.1 1.1 shard_map.95
  41.2 0.7 collective-permute-start.4
  41.9 1.2 collective-permute-start.5
  43.1 0.7 collective-permute-start.6
  43.9 2.8 %collective-permute-done.other_ref = bf16[1024,768]{1,0:T(8,128)(2,1)S(1)} collective-permute-done((bf16[1024,768]{1,0:T(8,128)(2,1)}, bf16[1024,768]{1,0:T(8,128)(2,1)S(1)}, u32[]{:S(2)}, u32[]{:S(2)}) %collective-permute-start) | collective-permute-done | bytes 1572896 | tf_op jit(solution)/shard_map/ppermute | solution.py:282
  46.7 1.1 copy-done.6
  48.2 3.7 %all-to-all-done = bf16[32,40,512]{2,1,0:T(8,128)(2,1)S(1)} async-done(((bf16[32,40,512]{2,1,0:T(8,128)(2,1)}), bf16[32,40,512]{2,1,0:T(8,128)(2,1)S(1)}, u32[]{:S(2)}, u32[]{:S(2)}) %all-to-all-start) | async-done | bytes 1310752 | tf_op jit(solution)/shard_map/all_to_all | solution.py:303
  52.0 4.8 %shard_map.100 = bf16[2,320,768]{2,1,0:T(8,128)(2,1)S(1)} custom-call(s32[1]{0:T(128)} %bitcast.group_ref, bf16[640,640]{1,0:T(8,128)(2,1)S(1)} %shard_map.97.pick_ref, bf16[2,640,512]{2,1,0:T(8,128)(2,1)S(1)} %bitcast.27, bf16[1024,768]{1,0:T(8,128)(2,1)} %bitcast.19, bf16[1024,768]{1,0:T(8,128)(2,1)} %bitcast.23), custom_call_target="tpu_custom_call" | custom-call | flops 1006632960 | bytes 3801088 | tf_op jit(solution)/shard_map/pallas_call | solution.py:322
  56.8 1.3 collective-permute-start.7
  58.3 6.7 %collective-permute-done.5 = bf16[4,40,1024]{2,1,0:T(8,128)(2,1)} collective-permute-done((bf16[4,40,1024]{2,1,0:T(8,128)(2,1)}, bf16[4,40,1024]{2,1,0:T(8,128)(2,1)}, u32[]{:S(2)}, u32[]{:S(2)}) %collective-permute-start.5) | collective-permute-done | bytes 327712 | tf_op jit(solution)/shard_map/ppermute | solution.py:266
  65.1 8.3 %collective-permute-done.6 = bf16[4,40,1024]{2,1,0:T(8,128)(2,1)} collective-permute-done((bf16[4,40,1024]{2,1,0:T(8,128)(2,1)}, bf16[4,40,1024]{2,1,0:T(8,128)(2,1)}, u32[]{:S(2)}, u32[]{:S(2)}) %collective-permute-start.6) | collective-permute-done | bytes 327712 | tf_op jit(solution)/shard_map/ppermute | solution.py:266
  73.3 4.9 %shard_map.96 = (f32[320,768]{1,0:T(8,128)S(1)}, bf16[320,1024]{1,0:T(8,128)(2,1)S(1)}, bf16[320,1024]{1,0:T(8,128)(2,1)}) custom-call(s32[640,1]{1,0:T(8,128)S(1)} %broadcast_in_dim.21.target_ref, bf16[1024,768]{1,0:T(8,128)(2,1)S(1)} %bitcast.33, bf16[1024,768]{1,0:T(8,128)(2,1)S(1)} %copy-done.7, bf16[160,1024]{1,0:T(8,128)(2,1)S(1)} %bitcast.35, ...), custom_call_target="tpu_custom_call" | custom-call | flops 9006632960 | bytes 4456448 | tf_op jit(solution)/shard_map/pallas_call | solution.py:358
  78.3 4.6 %shard_map.99.mine_ref = f32[2,320,768]{2,1,0:T(8,128)S(1)} custom-call(s32[1]{0:T(128)} %bitcast.group_ref, bf16[640,640]{1,0:T(8,128)(2,1)S(1)} %shard_map.97.pick_ref, bf16[2,640,512]{2,1,0:T(8,128)(2,1)S(1)} %bitcast.28, bf16[1024,768]{1,0:T(8,128)(2,1)} %bitcast.20, bf16[1024,768]{1,0:T(8,128)(2,1)} %bitcast.24), custom_call_target="tpu_custom_call" | custom-call | flops 1006632960 | bytes 3801088 | tf_op jit(solution)/shard_map/pallas_call | solution.py:322
  82.8 1.1 shard_map.101
  83.9 0.4 collective-permute-start.15
  84.3 1.2 collective-permute-start.8
  85.5 3.4 %shard_map.102 = (bf16[4,40,1024]{2,1,0:T(8,128)(2,1)S(1)}, bf16[4,40,1024]{2,1,0:T(8,128)(2,1)}, bf16[4,40,1024]{2,1,0:T(8,128)(2,1)}, bf16[4,40,1024]{2,1,0:T(8,128)(2,1)}) custom-call(s32[1,640]{1,0:T(1,128)S(1)} %broadcast_in_dim.18.target_ref, bf16[320,768]{1,0:T(8,128)(2,1)S(1)} %get-tuple-element.44.hid_ref, bf16[1024,768]{1,0:T(8,128)(2,1)S(1)} %bitcast.34, ...), custom_call_target="tpu_custom_call" | custom-call | flops 1006632960 | bytes 4456448 | tf_op jit(solution)/shard_map/pallas_call | solution.py:378
  88.9 0.7 copy-done.11
  89.6 0.9 collective-permute-start.11
  90.5 2.7 %collective-permute-start.9 = (bf16[4,40,1024]{2,1,0:T(8,128)(2,1)}, bf16[4,40,1024]{2,1,0:T(8,128)(2,1)}, u32[]{:S(2)}, u32[]{:S(2)}) collective-permute-start(bf16[4,40,1024]{2,1,0:T(8,128)(2,1)} %get-tuple-element.46), channel_id=1, source_target_pairs={{0,4},{1,5},{2,6},{3,7},{4,0},{5,1},{6,2},{7,3},{8,12},{9,13},{10,... | collective-permute-start | bytes 983048 | tf_op jit(solution)/shard_map/ppermute | solution.py:266
  93.2 2.6 %shard_map.105.refs_0_ = bf16[2,640,512]{2,1,0:T(8,128)(2,1)} custom-call(s32[1]{0:T(128)} %bitcast.group_ref, s32[1,640]{1,0:T(1,128)S(1)} %broadcast_in_dim.19.target_ref, bf16[2,320,768]{2,1,0:T(8,128)(2,1)S(1)} %get-tuple-element.42.d_ref, bf16[1024,768]{1,0:T(8,128)(2,1)S(1)} %bitcast.21, bf16[1024,768]{1,0:T(8,128)(2,1)S(1)} %bitcast.25), custom_call_target="tpu_custom_call" | custom-call | flops 1006632960 | bytes 3801088 | tf_op jit(solution)/shard_map/pallas_call | solution.py:396
  95.8 11.2 %collective-permute-done.15.d_ref = bf16[2,320,768]{2,1,0:T(8,128)(2,1)S(1)} collective-permute-done((bf16[2,320,768]{2,1,0:T(8,128)(2,1)S(1)}, bf16[2,320,768]{2,1,0:T(8,128)(2,1)S(1)}, u32[]{:S(2)}, u32[]{:S(2)}) %collective-permute-start.15) | collective-permute-done | bytes 983072 | tf_op jit(solution)/shard_map/ppermute | solution.py:389
  107.0 2.6 %shard_map.106 = bf16[2,640,512]{2,1,0:T(8,128)(2,1)} custom-call(s32[1]{0:T(128)} %bitcast.group_ref, s32[1,640]{1,0:T(1,128)S(1)} %broadcast_in_dim.19.target_ref, bf16[2,320,768]{2,1,0:T(8,128)(2,1)S(1)} %collective-permute-done.15.d_ref, bf16[1024,768]{1,0:T(8,128)(2,1)S(1)} %bitcast.22, ...), custom_call_target="tpu_custom_call", output_to_operand_aliasing={{}: (5, {})} | custom-call | flops 1006632960 | bytes 3801088 | tf_op jit(solution)/shard_map/pallas_call | solution.py:396
  109.6 6.6 %all-to-all-start.1 = ((bf16[32,40,512]{2,1,0:T(8,128)(2,1)}), bf16[32,40,512]{2,1,0:T(8,128)(2,1)S(1)}, u32[]{:S(2)}, u32[]{:S(2)}) async-start(bf16[32,40,512]{2,1,0:T(8,128)(2,1)} %bitcast.16), calls=%async_computation.1 | async-start | bytes 2621440 | tf_op jit(solution)/shard_map/all_to_all | solution.py:424
  116.2 1.2 collective-permute-start.16
  117.5 4.2 %collective-permute-done.11.refs_3_ = bf16[4,40,1024]{2,1,0:T(8,128)(2,1)} collective-permute-done((bf16[4,40,1024]{2,1,0:T(8,128)(2,1)}, bf16[4,40,1024]{2,1,0:T(8,128)(2,1)}, u32[]{:S(2)}, u32[]{:S(2)}) %collective-permute-start.11) | collective-permute-done | bytes 327712 | tf_op jit(solution)/shard_map/ppermute | solution.py:266
  121.7 0.7 collective-permute-done.8.recv_ref
  122.4 1.0 copy-done.12
  123.4 2.3 %shard_map.103 = (bf16[4,40,1024]{2,1,0:T(8,128)(2,1)}, bf16[4,40,1024]{2,1,0:T(8,128)(2,1)}, bf16[4,40,1024]{2,1,0:T(8,128)(2,1)}, bf16[4,40,1024]{2,1,0:T(8,128)(2,1)}) custom-call(bf16[4,40,1024]{2,1,0:T(8,128)(2,1)S(1)} %copy-done.12, bf16[4,40,1024]{2,1,0:T(8,128)(2,1)} %collective-permute-done.9.refs_1_, ...), custom_call_target="tpu_custom_call" | custom-call | flops 20000000000 | bytes 2621440 | tf_op jit(solution)/shard_map/pallas_call | solution.py:272
  125.7 7.6 %collective-permute-start.12 = (bf16[4,40,1024]{2,1,0:T(8,128)(2,1)}, bf16[4,40,1024]{2,1,0:T(8,128)(2,1)}, u32[]{:S(2)}, u32[]{:S(2)}) collective-permute-start(bf16[4,40,1024]{2,1,0:T(8,128)(2,1)} %get-tuple-element.54), channel_id=1, source_target_pairs={{0,1},{1,0},{2,3},{3,2},{4,5},{5,4},{6,7},{7,6},{8,9},{9,8},{10,11... | collective-permute-start | bytes 983048 | tf_op jit(solution)/shard_map/ppermute | solution.py:266
  133.3 1.6 %collective-permute-start.14 = (bf16[4,40,1024]{2,1,0:T(8,128)(2,1)}, bf16[4,40,1024]{2,1,0:T(8,128)(2,1)}, u32[]{:S(2)}, u32[]{:S(2)}) collective-permute-start(bf16[4,40,1024]{2,1,0:T(8,128)(2,1)} %get-tuple-element.56), channel_id=1, source_target_pairs={{0,3},{1,2},{2,1},{3,0},{4,7},{5,6},{6,5},{7,4},{8,11},{9,10},{10,... | collective-permute-start | bytes 983048 | tf_op jit(solution)/shard_map/ppermute | solution.py:266
  135.0 8.9 %collective-permute-done.16.hid_recv_ref = bf16[320,768]{1,0:T(8,128)(2,1)} collective-permute-done((bf16[320,768]{1,0:T(8,128)(2,1)S(1)}, bf16[320,768]{1,0:T(8,128)(2,1)}, u32[]{:S(2)}, u32[]{:S(2)}) %collective-permute-start.16) | collective-permute-done | bytes 491552 | tf_op jit(solution)/shard_map/ppermute | solution.py:388
  144.0 4.5 %shard_map.108 = bf16[1024,768]{1,0:T(8,128)(2,1)} custom-call(bf16[320,1024]{1,0:T(8,128)(2,1)S(1)} %get-tuple-element.58.mine_ref, bf16[320,1024]{1,0:T(8,128)(2,1)S(1)} %collective-permute-done.8.recv_ref, bf16[320,768]{1,0:T(8,128)(2,1)S(1)} %get-tuple-element.44.hid_ref, bf16[320,768]{1,0:T(8,128)(2,1)} %collective-permute-done.16.hid_recv_ref), custom_call_target="tpu_custom_call" | custom-call | flops 1006632960 | bytes 2883584 | tf_op jit(solution)/shard_map/pallas_call | solution.py:429
  148.5 5.5 %collective-permute-done.14 = bf16[4,40,1024]{2,1,0:T(8,128)(2,1)} collective-permute-done((bf16[4,40,1024]{2,1,0:T(8,128)(2,1)}, bf16[4,40,1024]{2,1,0:T(8,128)(2,1)}, u32[]{:S(2)}, u32[]{:S(2)}) %collective-permute-start.14) | collective-permute-done | bytes 327712 | tf_op jit(solution)/shard_map/ppermute | solution.py:266
  154.0 3.4 %shard_map.104 = bf16[128,2048]{1,0:T(8,128)(2,1)} custom-call(s32[1]{0:T(128)} %bitcast.group_ref, s32[1]{0:T(128)} %bitcast.1.expert_ref, s32[128,2]{1,0:T(8,128)S(1)} %copy.18.slots_ref, f32[128,2]{1,0:T(8,128)S(1)} %copy.19.gates_ref, bf16[160,1024]{1,0:T(8,128)(2,1)S(1)} %bitcast.37, bf16[160,1024]{1,0:T(8,128)(2,1)} %bitcast.13.refs_1_, ...), custom_call_target="tpu_custom_call" | custom-call | flops 671088640 | bytes 1835008 | tf_op jit(solution)/shard_map/pallas_call | solution.py:438
  157.4 1.8 %shard_map.107 = bf16[128,2048]{1,0:T(8,128)(2,1)} custom-call(s32[128,2]{1,0:T(8,128)S(1)} %copy.18.slots_ref, bf16[2,640,512]{2,1,0:T(8,128)(2,1)S(1)} %bitcast.29), custom_call_target="tpu_custom_call" | custom-call | flops 335544320 | bytes 1835008 | tf_op jit(solution)/shard_map/pallas_call | solution.py:449
  (44 shorter events, 1.0 us)
Async XLA Ops:
  0.6 46.1 %collective-permute-start = (bf16[1024,768]{1,0:T(8,128)(2,1)}, bf16[1024,768]{1,0:T(8,128)(2,1)S(1)}, u32[]{:S(2)}, u32[]{:S(2)}) collective-permute-start(bf16[1024,768]{1,0:T(8,128)(2,1)} %bitcast.32), channel_id=1, source_target_pairs={{0,16},{16,0},{1,17},{17,1},{2,18},{18,2},{3,19},{19,3},{4,20},{20... | collective-permute-start | bytes 4718600 | tf_op jit(solution)/shard_map/ppermute | solution.py:282
  1.9 1.0 copy-start.2
  2.9 0.7 copy-start.3
  5.4 5.6 %copy-start.13 = (f32[128,2]{0,1:T(2,128)S(1)}, f32[128,2]{0,1:T(2,128)}, u32[]{:S(2)}) copy-start(f32[128,2]{0,1:T(2,128)} %param.9) | copy-start | bytes 3076
  5.4 5.7 %copy-start.4 = (s32[128,2]{0,1:T(2,128)S(1)}, s32[128,2]{0,1:T(2,128)}, u32[]{:S(2)}) copy-start(s32[128,2]{0,1:T(2,128)} %param.10) | copy-start | bytes 3076
  5.4 46.6 %all-to-all-start = ((bf16[32,40,512]{2,1,0:T(8,128)(2,1)}), bf16[32,40,512]{2,1,0:T(8,128)(2,1)S(1)}, u32[]{:S(2)}, u32[]{:S(2)}) async-start(bf16[32,40,512]{2,1,0:T(8,128)(2,1)} %bitcast.8), calls=%async_computation | async-start | bytes 2621440 | tf_op jit(solution)/shard_map/all_to_all | solution.py:303
  11.1 1.0 copy-start.8
  13.3 2.3 %collective-permute-start.1 = (bf16[4,40,1024]{2,1,0:T(8,128)(2,1)S(1)}, bf16[4,40,1024]{2,1,0:T(8,128)(2,1)S(1)}, u32[]{:S(2)}, u32[]{:S(2)}) collective-permute-start(bf16[4,40,1024]{2,1,0:T(8,128)(2,1)S(1)} %get-tuple-element.32), channel_id=1, source_target_pairs={{0,1},{1,0},{2,3},{3,2},{4,5},{5,4},{6,7},{7,6},{8,9},{9,8},{10,11... | collective-permute-start | bytes 983048 | tf_op jit(solution)/shard_map/ppermute | solution.py:266
  13.7 13.7 %collective-permute-start.2 = (bf16[4,40,1024]{2,1,0:T(8,128)(2,1)S(1)}, bf16[4,40,1024]{2,1,0:T(8,128)(2,1)S(1)}, u32[]{:S(2)}, u32[]{:S(2)}) collective-permute-start(bf16[4,40,1024]{2,1,0:T(8,128)(2,1)S(1)} %get-tuple-element.33), channel_id=1, source_target_pairs={{0,2},{1,3},{2,0},{3,1},{4,6},{5,7},{6,4},{7,5},{8,10},{9,11},{10,... | collective-permute-start | bytes 983048 | tf_op jit(solution)/shard_map/ppermute | solution.py:266
  14.9 25.2 %collective-permute-start.3 = (bf16[4,40,1024]{2,1,0:T(8,128)(2,1)S(1)}, bf16[4,40,1024]{2,1,0:T(8,128)(2,1)S(1)}, u32[]{:S(2)}, u32[]{:S(2)}) collective-permute-start(bf16[4,40,1024]{2,1,0:T(8,128)(2,1)S(1)} %get-tuple-element.34), channel_id=1, source_target_pairs={{0,3},{1,2},{2,1},{3,0},{4,7},{5,6},{6,5},{7,4},{8,11},{9,10},{10,... | collective-permute-start | bytes 983048 | tf_op jit(solution)/shard_map/ppermute | solution.py:266
  41.2 17.1 %collective-permute-start.4 = (bf16[4,40,1024]{2,1,0:T(8,128)(2,1)}, bf16[4,40,1024]{2,1,0:T(8,128)(2,1)S(1)}, u32[]{:S(2)}, u32[]{:S(2)}) collective-permute-start(bf16[4,40,1024]{2,1,0:T(8,128)(2,1)} %get-tuple-element.36), channel_id=1, source_target_pairs={{0,4},{1,5},{2,6},{3,7},{4,0},{5,1},{6,2},{7,3},{8,12},{9,13},{10,... | collective-permute-start | bytes 983048 | tf_op jit(solution)/shard_map/ppermute | solution.py:266
  41.9 23.1 %collective-permute-start.5 = (bf16[4,40,1024]{2,1,0:T(8,128)(2,1)}, bf16[4,40,1024]{2,1,0:T(8,128)(2,1)}, u32[]{:S(2)}, u32[]{:S(2)}) collective-permute-start(bf16[4,40,1024]{2,1,0:T(8,128)(2,1)} %get-tuple-element.37), channel_id=1, source_target_pairs={{0,8},{1,9},{2,10},{3,11},{4,12},{5,13},{6,14},{7,15},{8,0},{9,1},... | collective-permute-start | bytes 983048 | tf_op jit(solution)/shard_map/ppermute | solution.py:266
  43.1 30.2 %collective-permute-start.6 = (bf16[4,40,1024]{2,1,0:T(8,128)(2,1)}, bf16[4,40,1024]{2,1,0:T(8,128)(2,1)}, u32[]{:S(2)}, u32[]{:S(2)}) collective-permute-start(bf16[4,40,1024]{2,1,0:T(8,128)(2,1)} %get-tuple-element.38), channel_id=1, source_target_pairs={{0,12},{1,13},{2,14},{3,15},{4,8},{5,9},{6,10},{7,11},{8,4},{9,5},... | collective-permute-start | bytes 983048 | tf_op jit(solution)/shard_map/ppermute | solution.py:266
  46.7 1.1 copy-start.6
  52.0 21.3 %copy-start.5 = (bf16[1,1024,768]{2,1,0:T(8,128)(2,1)S(1)}, bf16[1,1024,768]{2,1,0:T(8,128)(2,1)}, u32[]{:S(2)}) copy-start(bf16[1,1024,768]{2,1,0:T(8,128)(2,1)} %param.13) | copy-start | bytes 4718596
  52.0 21.3 %copy-start.7 = (bf16[1024,768]{1,0:T(8,128)(2,1)S(1)}, bf16[1024,768]{1,0:T(8,128)(2,1)}, u32[]{:S(2)}) copy-start(bf16[1024,768]{1,0:T(8,128)(2,1)} %copy-done.6) | copy-start | bytes 4718596
  52.0 21.3 %copy-start.9 = (bf16[4,40,1024]{2,1,0:T(8,128)(2,1)S(1)}, bf16[4,40,1024]{2,1,0:T(8,128)(2,1)}, u32[]{:S(2)}) copy-start(bf16[4,40,1024]{2,1,0:T(8,128)(2,1)} %get-tuple-element.35) | copy-start | bytes 983044
  56.8 26.0 %collective-permute-start.7 = (bf16[2,320,768]{2,1,0:T(8,128)(2,1)S(1)}, bf16[2,320,768]{2,1,0:T(8,128)(2,1)S(1)}, u32[]{:S(2)}, u32[]{:S(2)}) collective-permute-start(bf16[2,320,768]{2,1,0:T(8,128)(2,1)S(1)} %shard_map.100), channel_id=1, source_target_pairs={{0,16},{16,0},{1,17},{17,1},{2,18},{18,2},{3,19},{19,3},{4,20},{20... | collective-permute-start | bytes 2949128 | tf_op jit(solution)/shard_map/ppermute | solution.py:354
  83.9 23.1 %collective-permute-start.15 = (bf16[2,320,768]{2,1,0:T(8,128)(2,1)S(1)}, bf16[2,320,768]{2,1,0:T(8,128)(2,1)S(1)}, u32[]{:S(2)}, u32[]{:S(2)}) collective-permute-start(bf16[2,320,768]{2,1,0:T(8,128)(2,1)S(1)} %get-tuple-element.42.d_ref), channel_id=1, source_target_pairs={{0,16},{16,0},{1,17},{17,1},{2,18},{18,2},{3,19},{19,3},{4,20},{20... | collective-permute-start | bytes 2949128 | tf_op jit(solution)/shard_map/ppermute | solution.py:389
  84.3 38.2 %collective-permute-start.8 = (bf16[320,1024]{1,0:T(8,128)(2,1)}, bf16[320,1024]{1,0:T(8,128)(2,1)S(1)}, u32[]{:S(2)}, u32[]{:S(2)}) collective-permute-start(bf16[320,1024]{1,0:T(8,128)(2,1)} %get-tuple-element.43), channel_id=1, source_target_pairs={{0,16},{16,0},{1,17},{17,1},{2,18},{18,2},{3,19},{19,3},{4,20},{20... | collective-permute-start | bytes 1966088 | tf_op jit(solution)/shard_map/ppermute | solution.py:391
  85.4 7.7 %copy-start = (bf16[1,1024,768]{2,1,0:T(8,128)(2,1)S(1)}, bf16[1,1024,768]{2,1,0:T(8,128)(2,1)}, u32[]{:S(2)}) copy-start(bf16[1,1024,768]{2,1,0:T(8,128)(2,1)} %param.11) | copy-start | bytes 4718596
  85.5 7.7 %copy-start.1 = (bf16[1,1024,768]{2,1,0:T(8,128)(2,1)S(1)}, bf16[1,1024,768]{2,1,0:T(8,128)(2,1)}, u32[]{:S(2)}) copy-start(bf16[1,1024,768]{2,1,0:T(8,128)(2,1)} %param.12) | copy-start | bytes 4718596
  88.9 0.7 copy-start.11
  89.6 27.8 %collective-permute-start.10 = (bf16[4,40,1024]{2,1,0:T(8,128)(2,1)}, bf16[4,40,1024]{2,1,0:T(8,128)(2,1)}, u32[]{:S(2)}, u32[]{:S(2)}) collective-permute-start(bf16[4,40,1024]{2,1,0:T(8,128)(2,1)} %get-tuple-element.47), channel_id=1, source_target_pairs={{0,8},{1,9},{2,10},{3,11},{4,12},{5,13},{6,14},{7,15},{8,0},{9,1},... | collective-permute-start | bytes 983048 | tf_op jit(solution)/shard_map/ppermute | solution.py:266
  89.6 32.0 %collective-permute-start.11 = (bf16[4,40,1024]{2,1,0:T(8,128)(2,1)}, bf16[4,40,1024]{2,1,0:T(8,128)(2,1)}, u32[]{:S(2)}, u32[]{:S(2)}) collective-permute-start(bf16[4,40,1024]{2,1,0:T(8,128)(2,1)} %get-tuple-element.48), channel_id=1, source_target_pairs={{0,12},{1,13},{2,14},{3,15},{4,8},{5,9},{6,10},{7,11},{8,4},{9,5},... | collective-permute-start | bytes 983048 | tf_op jit(solution)/shard_map/ppermute | solution.py:266
  90.5 31.2 %collective-permute-start.9 = (bf16[4,40,1024]{2,1,0:T(8,128)(2,1)}, bf16[4,40,1024]{2,1,0:T(8,128)(2,1)}, u32[]{:S(2)}, u32[]{:S(2)}) collective-permute-start(bf16[4,40,1024]{2,1,0:T(8,128)(2,1)} %get-tuple-element.46), channel_id=1, source_target_pairs={{0,4},{1,5},{2,6},{3,7},{4,0},{5,1},{6,2},{7,3},{8,12},{9,13},{10,... | collective-permute-start | bytes 983048 | tf_op jit(solution)/shard_map/ppermute | solution.py:266
  109.6 47.8 %all-to-all-start.1 = ((bf16[32,40,512]{2,1,0:T(8,128)(2,1)}), bf16[32,40,512]{2,1,0:T(8,128)(2,1)S(1)}, u32[]{:S(2)}, u32[]{:S(2)}) async-start(bf16[32,40,512]{2,1,0:T(8,128)(2,1)} %bitcast.16), calls=%async_computation.1 | async-start | bytes 2621440 | tf_op jit(solution)/shard_map/all_to_all | solution.py:424
  116.2 27.8 %collective-permute-start.16 = (bf16[320,768]{1,0:T(8,128)(2,1)S(1)}, bf16[320,768]{1,0:T(8,128)(2,1)}, u32[]{:S(2)}, u32[]{:S(2)}) collective-permute-start(bf16[320,768]{1,0:T(8,128)(2,1)S(1)} %get-tuple-element.44.hid_ref), channel_id=1, source_target_pairs={{0,16},{16,0},{1,17},{17,1},{2,18},{18,2},{3,19},{19,3},{4,20},{20... | collective-permute-start | bytes 1474568 | tf_op jit(solution)/shard_map/ppermute | solution.py:388
  122.4 1.0 copy-start.12
  125.7 22.8 %collective-permute-start.12 = (bf16[4,40,1024]{2,1,0:T(8,128)(2,1)}, bf16[4,40,1024]{2,1,0:T(8,128)(2,1)}, u32[]{:S(2)}, u32[]{:S(2)}) collective-permute-start(bf16[4,40,1024]{2,1,0:T(8,128)(2,1)} %get-tuple-element.54), channel_id=1, source_target_pairs={{0,1},{1,0},{2,3},{3,2},{4,5},{5,4},{6,7},{7,6},{8,9},{9,8},{10,11... | collective-permute-start | bytes 983048 | tf_op jit(solution)/shard_map/ppermute | solution.py:266
  133.3 15.2 %collective-permute-start.13 = (bf16[4,40,1024]{2,1,0:T(8,128)(2,1)}, bf16[4,40,1024]{2,1,0:T(8,128)(2,1)}, u32[]{:S(2)}, u32[]{:S(2)}) collective-permute-start(bf16[4,40,1024]{2,1,0:T(8,128)(2,1)} %get-tuple-element.55), channel_id=1, source_target_pairs={{0,2},{1,3},{2,0},{3,1},{4,6},{5,7},{6,4},{7,5},{8,10},{9,11},{10,... | collective-permute-start | bytes 983048 | tf_op jit(solution)/shard_map/ppermute | solution.py:266
  133.3 20.7 %collective-permute-start.14 = (bf16[4,40,1024]{2,1,0:T(8,128)(2,1)}, bf16[4,40,1024]{2,1,0:T(8,128)(2,1)}, u32[]{:S(2)}, u32[]{:S(2)}) collective-permute-start(bf16[4,40,1024]{2,1,0:T(8,128)(2,1)} %get-tuple-element.56), channel_id=1, source_target_pairs={{0,3},{1,2},{2,1},{3,0},{4,7},{5,6},{6,5},{7,4},{8,11},{9,10},{10,... | collective-permute-start | bytes 983048 | tf_op jit(solution)/shard_map/ppermute | solution.py:266
  144.0 10.0 %copy-start.10 = (bf16[4,40,1024]{2,1,0:T(8,128)(2,1)S(1)}, bf16[4,40,1024]{2,1,0:T(8,128)(2,1)}, u32[]{:S(2)}) copy-start(bf16[4,40,1024]{2,1,0:T(8,128)(2,1)} %get-tuple-element.53) | copy-start | bytes 983044

commit v4 on v3

--- a/solution.py
+++ b/solution.py
@@ -139,7 +139,7 @@
             out_ref[i, :, columns] = mm(x_ref[...], w_ref[i, :, columns]).astype(out_ref.dtype)
 
 
-def hidden_grad_kernel(target_ref, own_ref, other_ref, *refs):
+def hidden_grad_kernel(target_ref, own_ref, other_0_ref, other_1_ref, *refs):
     *came_refs, out_ref, dy_mine_ref, dy_send_ref, came_ref = refs
     rows = out_ref.shape[0]
 
@@ -153,7 +153,10 @@
         dy_mine_ref[...] = dy[:rows]
         dy_send_ref[...] = dy[rows:]
 
-    out_ref[...] = mm(dy_mine_ref[...], own_ref[...]) + mm(dy_send_ref[...], other_ref[...])
+    cut = other_0_ref.shape[0]
+    total = mm(dy_mine_ref[...], own_ref[...])
+    total = total + mm(dy_send_ref[:, :cut], other_0_ref[...])
+    out_ref[...] = total + mm(dy_send_ref[:, cut:], other_1_ref[...])
 
 
 def pointwise_kernel(mine_ref, recv_ref, d_hidden_ref, hid_ref, out_ref):
@@ -167,18 +170,16 @@
     hid_ref[...] = (active * up).astype(BF16)
 
 
-def forward_kernel(target_ref, hid_ref, own_ref, other_ref, *refs):
-    *out_refs, pick_ref, y_ref = refs
+def forward_kernel(target_ref, hid_ref, own_ref, other_0_ref, other_1_ref, *refs):
+    *out_refs, y_ref = refs
     rows = hid_ref.shape[0]
-
-    @pl.when(pl.program_id(0) == 0)
-    def _():
-        pick_ref[...] = ones_where(iota((2 * rows, 2 * rows), 0) == target_ref[...])
-
-    hidden = hid_ref[...]
-    y_ref[:rows, :] = mm(hidden, own_ref[...], NT).astype(BF16)
-    y_ref[rows:, :] = mm(hidden, other_ref[...], NT).astype(BF16)
-    spread(mm(pick_ref[...], y_ref[...]), out_refs, slice(None), out_refs[0].shape[1])
+    cut = other_0_ref.shape[0]
+    pick = ones_where(iota((2 * rows, 2 * rows), 0) == target_ref[...])
+    for i, other_ref in enumerate((other_0_ref, other_1_ref)):
+        columns = slice(i * cut, (i + 1) * cut)
+        y_ref[:rows, :] = mm(hid_ref[...], own_ref[columns, :], NT).astype(BF16)
+        y_ref[rows:, :] = mm(hid_ref[...], other_ref[...], NT).astype(BF16)
+        spread(mm(pick, y_ref[...]), out_refs, columns, out_refs[0].shape[1])
 
 
 def input_grad_kernel(other, group_ref, target_ref, d_ref, wg_ref, wu_ref, *refs):
@@ -250,7 +251,7 @@
     near, far = masks_of(place // cap, expert)
     moved_left = (far * PLANE + near) * (2 * cap) + place % cap
     moved = jnp.concatenate([moved_left, moved_left + cap])
-    tile, strip, narrow = min(256, ff), min(512, half), min(256, half)
+    tile, narrow = min(256, ff), min(256, half)
     matmul_flops = 2 * 2 * rows * half * ff
     route_flops = 2 * 2 * rows * 2 * count * half
     route_bytes = 2 * (tokens.size + 2 * rows * half)
@@ -279,7 +280,8 @@
             moved=8 * rows * half,
         )(*blocks)
 
-    down_other = lax.ppermute(w_down, "dp", swap)
+    cuts = (0, quarter, half)
+    down_others = [lax.ppermute(w_down[lo:hi], "dp", swap) for lo, hi in zip(cuts, cuts[1:])]
     dy_near = call(
         functools.partial(send_grads_kernel, peers, cap),
         tuple(shape(*near_block) for _ in range(PLANE)),
@@ -307,7 +309,8 @@
     part_block = pl.BlockSpec((rows, tile), lambda i: (0, i))
     pair_block = pl.BlockSpec((2, rows, tile), lambda i: (0, 0, i))
     weight_block = pl.BlockSpec((half, tile), lambda i: (0, i))
-    target, *_ = lax.optimization_barrier((straight[:, None], down_other, *dy_far))
+    quarter_block = pl.BlockSpec((quarter, tile), lambda i: (0, i))
+    target, *_ = lax.optimization_barrier((straight[:, None], down_others[0], *dy_far))
     pick = call(
         pick_kernel,
         shape(2 * rows, 2 * rows),
@@ -351,6 +354,7 @@
         )
 
     part_send = partial(1, BF16, tok_recv)
+    part_send, down_others[1] = lax.optimization_barrier((part_send, down_others[1]))
     part_recv = lax.ppermute(part_send, "dp", swap)
     dy_came = exchange(dy_far, PLANE)
     part_mine = partial(0, F32, tok_recv)
@@ -359,12 +363,12 @@
         hidden_grad_kernel,
         (shape(rows, ff, dtype=F32), shape(rows, half), shape(rows, half)),
         (ff // tile,),
-        [whole((2 * rows, 1)), weight_block, weight_block] + [whole((PLANE * 2 * cap, half))] * planes,
+        [whole((2 * rows, 1)), weight_block] + [quarter_block] * 2 + [whole((PLANE * 2 * cap, half))] * planes,
         (part_block, whole((rows, half)), whole((rows, half))),
         [pltpu.VMEM((2 * rows, half), BF16)],
         flops=matmul_flops + AHEAD_OF_BACKWARD,
         moved=2 * weight_bytes + 4 * rows * half,
-    )(moved[:, None], w_down, down_other, *(came.reshape(PLANE * 2 * cap, half) for came in dy_came))
+    )(moved[:, None], w_down, *down_others, *(came.reshape(PLANE * 2 * cap, half) for came in dy_came))
     hidden, d_pair = call(
         pointwise_kernel,
         (shape(rows, ff), shape(2, rows, ff)),
@@ -374,17 +378,16 @@
         flops=20 * rows * ff,
         moved=22 * rows * ff,
     )(part_mine, part_recv, d_hidden)
-    down_rows = pl.BlockSpec((strip, ff), lambda i: (i, 0))
     y_far = call(
         forward_kernel,
         tuple(shape(*far_block) for _ in range(planes)),
-        (half // strip,),
-        [whole((1, 2 * rows)), whole((rows, ff)), down_rows, down_rows],
-        tuple(pl.BlockSpec((PLANE, 2 * cap, strip), lambda i: (0, 0, i)) for _ in range(planes)),
-        [pltpu.VMEM((2 * rows, 2 * rows), BF16), pltpu.VMEM((2 * rows, strip), BF16)],
+        (1,),
+        [whole((1, 2 * rows)), whole((rows, ff)), whole((half, ff))] + [whole((quarter, ff))] * 2,
+        tuple(whole(far_block) for _ in range(planes)),
+        [pltpu.VMEM((2 * rows, quarter), BF16)],
         flops=matmul_flops,
         moved=2 * weight_bytes + 4 * rows * half,
-    )(moved[None, :], hidden, w_down, down_other)
+    )(moved[None, :], hidden, w_down, *down_others)
     hidden_recv = lax.ppermute(hidden, "dp", swap)
     d_recv = lax.ppermute(d_pair, "dp", swap)
     dy_other, _ = lax.optimization_barrier((dy_other, d_pair))
@@ -420,6 +423,7 @@
     y_far_done = y_far_came
     _, *y_far_came = lax.optimization_barrier((dy_cross, *y_far_came))
     y_near = regroup(y_far_came, AHEAD_OF_REGROUP)
+    dx_send, *_ = lax.optimization_barrier((dx_send, y_far_done[2]))
     y_came = exchange(y_near, 1)
     dx_back = lax.all_to_all(
         dx_send.reshape(2 * peers, 2 * cap, quarter), ("dp", "expert"), 0, 0, tiled=True

time: 160 us -> 156 us (0.975)
  waiting for transfers between devices: 76.7 us -> 73.3 us
  starting transfers between devices: 35.2 us -> 32.2 us
    ppermute x1, waiting for transfers between devices: 8.93 us -> 17.3 us  [split_width(): hidden_recv = lax.ppermute(hidden, 'dp', swap)]
    ppermute x12, starting transfers between devices: 17.7 us -> 10.2 us  [exchange(): lax.ppermute(blocks[m], 'expert', [(i, i ^ m * stride) for i in range(pee...]
    ppermute x12, waiting for transfers between devices: 49.2 us -> 44.5 us  [exchange(): lax.ppermute(blocks[m], 'expert', [(i, i ^ m * stride) for i in range(pee...]
    all_to_all x1, waiting for transfers between devices: 3.75 us -> 0.01 us  [split_width(): lax.all_to_all(tok_send.reshape(2 * peers, 2 * cap, quarter), ('dp', 'exp...]
    all_to_all x1, starting transfers between devices: 6.63 us -> 10 us  [split_width(): lax.all_to_all(dx_send.reshape(2 * peers, 2 * cap, quarter), ('dp', 'expe...]
    slice x0 -> x1, local copies, waits for them, and re-layouts: none -> 2.69 us  [split_width(): w_down[lo:hi]]
    ppermute x1 -> x2, waiting for transfers between devices: 2.82 us -> 0.74 us  [split_width(): lax.ppermute(w_down[lo:hi], 'dp', swap)]
    unnamed x30 -> x32, local copies, waits for them, and re-layouts: 5.87 us -> 4.56 us
  transfers between devices with their start and end apart: 19 -> 20, of which waited for: 11 -> 8; matrix products, arithmetic and copies ran while one was open for 0% -> 0% of each run, Pallas kernels for 23% -> 25%
where the time goes in v4:
time: 156 us; the launch traced here: 155 us
  waiting for transfers between devices  73.3 us (47%)
  Pallas kernels  41.1 us (26%)
  starting transfers between devices  32.2 us (21%)
  local copies, waits for them, and re-layouts  7.57 us (5%)
    ppermute x12, waiting for transfers between devices, exchange(): lax.ppermute(blocks[m], 'expert', [(i, i ^ m * stride) for i in range(pee...  44.5 us
    ppermute x1, waiting for transfers between devices, split_width(): hidden_recv = lax.ppermute(hidden, 'dp', swap)  17.3 us
    ppermute x1, waiting for transfers between devices, split_width(): d_recv = lax.ppermute(d_pair, 'dp', swap)  10.9 us
    ppermute x12, starting transfers between devices, exchange(): lax.ppermute(blocks[m], 'expert', [(i, i ^ m * stride) for i in range(pee...  10.2 us
    all_to_all x1, starting transfers between devices, split_width(): lax.all_to_all(dx_send.reshape(2 * peers, 2 * cap, quarter), ('dp', 'expe...  10 us
    pallas_call x2, Pallas kernels, partial(): pl.pallas_call(functools.partial(partial_kernel, tile), out_shape=shape(2...  9.36 us
    all_to_all x1, starting transfers between devices, split_width(): lax.all_to_all(tok_send.reshape(2 * peers, 2 * cap, quarter), ('dp', 'exp...  5.6 us
    pallas_call x1, Pallas kernels, split_width(): call(hidden_grad_kernel, (shape(rows, ff, dtype=F32), shape(rows, half),...  5.3 us
  transfers between devices with their start and end apart: 20, of which 8 were waited for; matrix products, arithmetic and copies ran while one was open for 0% of the time, Pallas kernels for 25%

profile of v4, /device:TPU:17, one launch (start us, length us, event | category | flops | bytes accessed | tf_op | source)
XLA Modules:
  0.0 155.2 jit_solution(5285145973861555425)
XLA Ops:
  0.6 2.7 %slice_bitcast_fusion = (bf16[512,768]{1,0:T(8,128)(2,1)}, bf16[512,768]{1,0:T(8,128)(2,1)}) fusion(bf16[1,1024,768]{2,1,0:T(8,128)(2,1)} %param.13), kind=kLoop, calls=%fused_computation | loop fusion | bytes 3145728 | tf_op jit(solution)/shard_map/slice | solution.py:284
  3.3 1.2 collective-permute-start
  4.6 1.7 %shard_map.97 = bf16[2,640,512]{2,1,0:T(8,128)(2,1)} custom-call(s32[2,128]{1,0:T(2,128)S(1)} %bitcast.36, bf16[128,2048]{1,0:T(8,128)(2,1)S(1)} %copy-done.3), custom_call_target="tpu_custom_call" | custom-call | flops 335544320 | bytes 1835008 | tf_op jit(solution)/shard_map/pallas_call | solution.py:296
  6.3 5.6 %all-to-all-start = ((bf16[32,40,512]{2,1,0:T(8,128)(2,1)}), bf16[32,40,512]{2,1,0:T(8,128)(2,1)S(1)}, u32[]{:S(2)}, u32[]{:S(2)}) async-start(bf16[32,40,512]{2,1,0:T(8,128)(2,1)} %bitcast.5), calls=%async_computation | async-start | bytes 2621440 | tf_op jit(solution)/shard_map/all_to_all | solution.py:305
  12.0 1.1 shard_map.94
  13.1 0.4 collective-permute-start.1
  13.5 1.2 collective-permute-start.2
  14.7 0.6 collective-permute-start.3
  15.3 1.2 collective-permute-start.4
  16.6 11.1 %collective-permute-done.2.refs_2_ = bf16[4,40,1024]{2,1,0:T(8,128)(2,1)S(1)} collective-permute-done((bf16[4,40,1024]{2,1,0:T(8,128)(2,1)S(1)}, bf16[4,40,1024]{2,1,0:T(8,128)(2,1)S(1)}, u32[]{:S(2)}, u32[]{:S(2)}) %collective-permute-start.2) | collective-permute-done | bytes 327712 | tf_op jit(solution)/shard_map/ppermute | solution.py:267
  27.8 14.8 %collective-permute-done.3.refs_3_ = bf16[4,40,1024]{2,1,0:T(8,128)(2,1)S(1)} collective-permute-done((bf16[4,40,1024]{2,1,0:T(8,128)(2,1)S(1)}, bf16[4,40,1024]{2,1,0:T(8,128)(2,1)S(1)}, u32[]{:S(2)}, u32[]{:S(2)}) %collective-permute-start.3) | collective-permute-done | bytes 327712 | tf_op jit(solution)/shard_map/ppermute | solution.py:267
  42.6 1.1 shard_map.95
  43.7 1.3 collective-permute-start.5
  45.0 1.4 collective-permute-start.7
  46.4 0.9 copy-done.5
  47.2 0.2 copy.16.target_ref
  47.4 0.2 shard_map.96.pick_ref
  47.6 4.6 %shard_map.98 = bf16[2,320,768]{2,1,0:T(8,128)(2,1)S(1)} custom-call(s32[1]{0:T(128)} %bitcast.group_ref, bf16[640,640]{1,0:T(8,128)(2,1)S(1)} %shard_map.96.pick_ref, bf16[2,640,512]{2,1,0:T(8,128)(2,1)S(1)} %bitcast.31, bf16[1024,768]{1,0:T(8,128)(2,1)} %bitcast.23, bf16[1024,768]{1,0:T(8,128)(2,1)} %bitcast.27), custom_call_target="tpu_custom_call" | custom-call | flops 1006632960 | bytes 3801088 | tf_op jit(solution)/shard_map/pallas_call | solution.py:325
  52.2 0.7 collective-permute-done.4.other_1_ref
  53.0 1.2 collective-permute-start.8
  54.5 4.8 %shard_map.100.mine_ref = f32[2,320,768]{2,1,0:T(8,128)S(1)} custom-call(s32[1]{0:T(128)} %bitcast.group_ref, bf16[640,640]{1,0:T(8,128)(2,1)S(1)} %shard_map.96.pick_ref, bf16[2,640,512]{2,1,0:T(8,128)(2,1)S(1)} %bitcast.32, bf16[1024,768]{1,0:T(8,128)(2,1)} %bitcast.24, bf16[1024,768]{1,0:T(8,128)(2,1)} %bitcast.28), custom_call_target="tpu_custom_call" | custom-call | flops 1006632960 | bytes 3801088 | tf_op jit(solution)/shard_map/pallas_call | solution.py:325
  59.3 1.0 collective-permute-done.6
  60.2 15.4 %collective-permute-done.7 = bf16[4,40,1024]{2,1,0:T(8,128)(2,1)} collective-permute-done((bf16[4,40,1024]{2,1,0:T(8,128)(2,1)}, bf16[4,40,1024]{2,1,0:T(8,128)(2,1)}, u32[]{:S(2)}, u32[]{:S(2)}) %collective-permute-start.7) | collective-permute-done | bytes 327712 | tf_op jit(solution)/shard_map/ppermute | solution.py:267
  75.6 5.3 %shard_map.99 = (f32[320,768]{1,0:T(8,128)S(1)}, bf16[320,1024]{1,0:T(8,128)(2,1)S(1)}, bf16[320,1024]{1,0:T(8,128)(2,1)}) custom-call(s32[640,1]{1,0:T(8,128)S(1)} %broadcast_in_dim.21.target_ref, bf16[1024,768]{1,0:T(8,128)(2,1)S(1)} %bitcast.34, bf16[512,768]{1,0:T(8,128)(2,1)S(1)} %copy-done.6, bf16[512,768]{1,0:T(8,128)(2,1)} %collective-permute-done.4.other_1_ref, ...), custom_call_target="tpu_custom_call" | custom-call | flops 9006632960 | bytes 4456448 | tf_op jit(solution)/shard_map/pallas_call | solution.py:362
  80.9 1.1 shard_map.101
  82.0 1.1 collective-permute-start.16
  83.1 0.4 collective-permute-start.9
  83.5 4.3 %shard_map.102 = (bf16[4,40,1024]{2,1,0:T(8,128)(2,1)S(1)}, bf16[4,40,1024]{2,1,0:T(8,128)(2,1)}, bf16[4,40,1024]{2,1,0:T(8,128)(2,1)S(1)}, bf16[4,40,1024]{2,1,0:T(8,128)(2,1)}) custom-call(s32[1,640]{1,0:T(1,128)S(1)} %broadcast_in_dim.18.target_ref, bf16[320,768]{1,0:T(8,128)(2,1)S(1)} %get-tuple-element.49.hid_ref, bf16[1024,768]{1,0:T(8,128)(2,1)S(1)} %bitcast.35, ...), custom_call_target="tpu_custom_call" | custom-call | flops 1006632960 | bytes 4456448 | tf_op jit(solution)/shard_map/pallas_call | solution.py:381
  87.8 0.7 copy-done.12
  88.5 1.4 collective-permute-start.10
  89.9 1.3 collective-permute-start.12
  91.2 2.6 %shard_map.105.refs_0_ = bf16[2,640,512]{2,1,0:T(8,128)(2,1)} custom-call(s32[1]{0:T(128)} %bitcast.group_ref, s32[1,640]{1,0:T(1,128)S(1)} %broadcast_in_dim.19.target_ref, bf16[2,320,768]{2,1,0:T(8,128)(2,1)S(1)} %get-tuple-element.47.d_ref, bf16[1024,768]{1,0:T(8,128)(2,1)S(1)} %bitcast.25, bf16[1024,768]{1,0:T(8,128)(2,1)S(1)} %bitcast.29), custom_call_target="tpu_custom_call" | custom-call | flops 1006632960 | bytes 3801088 | tf_op jit(solution)/shard_map/pallas_call | solution.py:399
  93.7 10.9 %collective-permute-done.16.d_ref = bf16[2,320,768]{2,1,0:T(8,128)(2,1)S(1)} collective-permute-done((bf16[2,320,768]{2,1,0:T(8,128)(2,1)S(1)}, bf16[2,320,768]{2,1,0:T(8,128)(2,1)S(1)}, u32[]{:S(2)}, u32[]{:S(2)}) %collective-permute-start.16) | collective-permute-done | bytes 983072 | tf_op jit(solution)/shard_map/ppermute | solution.py:392
  104.6 2.6 %shard_map.106 = bf16[2,640,512]{2,1,0:T(8,128)(2,1)} custom-call(s32[1]{0:T(128)} %bitcast.group_ref, s32[1,640]{1,0:T(1,128)S(1)} %broadcast_in_dim.19.target_ref, bf16[2,320,768]{2,1,0:T(8,128)(2,1)S(1)} %collective-permute-done.16.d_ref, bf16[1024,768]{1,0:T(8,128)(2,1)S(1)} %bitcast.26, ...), custom_call_target="tpu_custom_call", output_to_operand_aliasing={{}: (5, {})} | custom-call | flops 1006632960 | bytes 3801088 | tf_op jit(solution)/shard_map/pallas_call | solution.py:399
  107.2 0.7 copy-done.9
  107.9 10.0 %all-to-all-start.1 = ((bf16[32,40,512]{2,1,0:T(8,128)(2,1)}), bf16[32,40,512]{2,1,0:T(8,128)(2,1)S(1)}, u32[]{:S(2)}, u32[]{:S(2)}) async-start(bf16[32,40,512]{2,1,0:T(8,128)(2,1)} %bitcast.18), calls=%async_computation.1 | async-start | bytes 2621440 | tf_op jit(solution)/shard_map/all_to_all | solution.py:428
  117.9 1.3 collective-permute-start.17
  119.2 1.0 copy-done.10
  120.2 1.0 copy-done.13
  121.2 2.2 %shard_map.103 = (bf16[4,40,1024]{2,1,0:T(8,128)(2,1)}, bf16[4,40,1024]{2,1,0:T(8,128)(2,1)}, bf16[4,40,1024]{2,1,0:T(8,128)(2,1)}, bf16[4,40,1024]{2,1,0:T(8,128)(2,1)}) custom-call(bf16[4,40,1024]{2,1,0:T(8,128)(2,1)S(1)} %copy-done.13, bf16[4,40,1024]{2,1,0:T(8,128)(2,1)} %collective-permute-done.10.refs_1_, bf16[4,40,1024]{2,1,0:T(8,128)(2,1)S(1)} %copy-done.10, ...), custom_call_target="tpu_custom_call" | custom-call | flops 20000000000 | bytes 2621440 | tf_op jit(solution)/shard_map/pallas_call | solution.py:273
  123.3 1.0 collective-permute-start.13
  124.4 0.8 collective-permute-start.14
  125.2 0.8 collective-permute-start.15
  126.1 17.3 %collective-permute-done.17.hid_recv_ref = bf16[320,768]{1,0:T(8,128)(2,1)} collective-permute-done((bf16[320,768]{1,0:T(8,128)(2,1)S(1)}, bf16[320,768]{1,0:T(8,128)(2,1)}, u32[]{:S(2)}, u32[]{:S(2)}) %collective-permute-start.17) | collective-permute-done | bytes 491552 | tf_op jit(solution)/shard_map/ppermute | solution.py:391
  143.4 4.5 %shard_map.108 = bf16[1024,768]{1,0:T(8,128)(2,1)} custom-call(bf16[320,1024]{1,0:T(8,128)(2,1)S(1)} %get-tuple-element.64.mine_ref, bf16[320,1024]{1,0:T(8,128)(2,1)S(1)} %collective-permute-done.9.recv_ref, bf16[320,768]{1,0:T(8,128)(2,1)S(1)} %get-tuple-element.49.hid_ref, bf16[320,768]{1,0:T(8,128)(2,1)} %collective-permute-done.17.hid_recv_ref), custom_call_target="tpu_custom_call" | custom-call | flops 1006632960 | bytes 2883584 | tf_op jit(solution)/shard_map/pallas_call | solution.py:433
  147.9 2.2 %collective-permute-done.15 = bf16[4,40,1024]{2,1,0:T(8,128)(2,1)} collective-permute-done((bf16[4,40,1024]{2,1,0:T(8,128)(2,1)}, bf16[4,40,1024]{2,1,0:T(8,128)(2,1)}, u32[]{:S(2)}, u32[]{:S(2)}) %collective-permute-start.15) | collective-permute-done | bytes 327712 | tf_op jit(solution)/shard_map/ppermute | solution.py:267
  150.1 3.4 %shard_map.104 = bf16[128,2048]{1,0:T(8,128)(2,1)} custom-call(s32[1]{0:T(128)} %bitcast.group_ref, s32[1]{0:T(128)} %bitcast.1.expert_ref, s32[128,2]{1,0:T(8,128)S(1)} %copy.18.slots_ref, f32[128,2]{1,0:T(8,128)S(1)} %copy.19.gates_ref, bf16[160,1024]{1,0:T(8,128)(2,1)S(1)} %bitcast.41, bf16[160,1024]{1,0:T(8,128)(2,1)} %bitcast.15.refs_1_, ...), custom_call_target="tpu_custom_call" | custom-call | flops 671088640 | bytes 1835008 | tf_op jit(solution)/shard_map/pallas_call | solution.py:442
  153.4 1.8 %shard_map.107 = bf16[128,2048]{1,0:T(8,128)(2,1)} custom-call(s32[128,2]{1,0:T(8,128)S(1)} %copy.18.slots_ref, bf16[2,640,512]{2,1,0:T(8,128)(2,1)S(1)} %bitcast.33), custom_call_target="tpu_custom_call" | custom-call | flops 335544320 | bytes 1835008 | tf_op jit(solution)/shard_map/pallas_call | solution.py:453
  (49 shorter events, 0.7 us)
Async XLA Ops:
  0.6 3.9 %copy-start.4 = (s32[128,2]{0,1:T(2,128)S(1)}, s32[128,2]{0,1:T(2,128)}, u32[]{:S(2)}) copy-start(s32[128,2]{0,1:T(2,128)} %param.10) | copy-start | bytes 3076
  0.6 3.9 %copy-start.3 = (bf16[128,2048]{1,0:T(8,128)(2,1)S(1)}, bf16[128,2048]{1,0:T(8,128)(2,1)}, u32[]{:S(2)}) copy-start(bf16[128,2048]{1,0:T(8,128)(2,1)} %tok_ref.1) | copy-start | bytes 1572868
  3.3 43.0 %collective-permute-start = (bf16[512,768]{1,0:T(8,128)(2,1)}, bf16[512,768]{1,0:T(8,128)(2,1)S(1)}, u32[]{:S(2)}, u32[]{:S(2)}) collective-permute-start(bf16[512,768]{1,0:T(8,128)(2,1)} %get-tuple-element.66), channel_id=1, source_target_pairs={{0,16},{16,0},{1,17},{17,1},{2,18},{18,2},{3,19},{19,3},{4,20},{20... | collective-permute-start | bytes 2359304 | tf_op jit(solution)/shard_map/ppermute | solution.py:284
  6.3 5.6 %copy-start.14 = (f32[128,2]{0,1:T(2,128)S(1)}, f32[128,2]{0,1:T(2,128)}, u32[]{:S(2)}) copy-start(f32[128,2]{0,1:T(2,128)} %param.9) | copy-start | bytes 3076
  6.3 5.7 %copy-start.7 = (bf16[128,2048]{1,0:T(8,128)(2,1)S(1)}, bf16[128,2048]{1,0:T(8,128)(2,1)}, u32[]{:S(2)}) copy-start(bf16[128,2048]{1,0:T(8,128)(2,1)} %grad_ref.1) | copy-start | bytes 1572868
  6.3 41.4 %all-to-all-start = ((bf16[32,40,512]{2,1,0:T(8,128)(2,1)}), bf16[32,40,512]{2,1,0:T(8,128)(2,1)S(1)}, u32[]{:S(2)}, u32[]{:S(2)}) async-start(bf16[32,40,512]{2,1,0:T(8,128)(2,1)} %bitcast.5), calls=%async_computation | async-start | bytes 2621440 | tf_op jit(solution)/shard_map/all_to_all | solution.py:305
  13.1 3.5 %collective-permute-start.1 = (bf16[4,40,1024]{2,1,0:T(8,128)(2,1)S(1)}, bf16[4,40,1024]{2,1,0:T(8,128)(2,1)S(1)}, u32[]{:S(2)}, u32[]{:S(2)}) collective-permute-start(bf16[4,40,1024]{2,1,0:T(8,128)(2,1)S(1)} %get-tuple-element.35), channel_id=1, source_target_pairs={{0,1},{1,0},{2,3},{3,2},{4,5},{5,4},{6,7},{7,6},{8,9},{9,8},{10,11... | collective-permute-start | bytes 983048 | tf_op jit(solution)/shard_map/ppermute | solution.py:267
  13.5 14.2 %collective-permute-start.2 = (bf16[4,40,1024]{2,1,0:T(8,128)(2,1)S(1)}, bf16[4,40,1024]{2,1,0:T(8,128)(2,1)S(1)}, u32[]{:S(2)}, u32[]{:S(2)}) collective-permute-start(bf16[4,40,1024]{2,1,0:T(8,128)(2,1)S(1)} %get-tuple-element.36), channel_id=1, source_target_pairs={{0,2},{1,3},{2,0},{3,1},{4,6},{5,7},{6,4},{7,5},{8,10},{9,11},{10,... | collective-permute-start | bytes 983048 | tf_op jit(solution)/shard_map/ppermute | solution.py:267
  14.7 27.8 %collective-permute-start.3 = (bf16[4,40,1024]{2,1,0:T(8,128)(2,1)S(1)}, bf16[4,40,1024]{2,1,0:T(8,128)(2,1)S(1)}, u32[]{:S(2)}, u32[]{:S(2)}) collective-permute-start(bf16[4,40,1024]{2,1,0:T(8,128)(2,1)S(1)} %get-tuple-element.37), channel_id=1, source_target_pairs={{0,3},{1,2},{2,1},{3,0},{4,7},{5,6},{6,5},{7,4},{8,11},{9,10},{10,... | collective-permute-start | bytes 983048 | tf_op jit(solution)/shard_map/ppermute | solution.py:267
  15.3 37.6 %collective-permute-start.4 = (bf16[512,768]{1,0:T(8,128)(2,1)}, bf16[512,768]{1,0:T(8,128)(2,1)}, u32[]{:S(2)}, u32[]{:S(2)}) collective-permute-start(bf16[512,768]{1,0:T(8,128)(2,1)} %get-tuple-element.65), channel_id=1, source_target_pairs={{0,16},{16,0},{1,17},{17,1},{2,18},{18,2},{3,19},{19,3},{4,20},{20... | collective-permute-start | bytes 2359304 | tf_op jit(solution)/shard_map/ppermute | solution.py:284
  43.7 15.6 %collective-permute-start.5 = (bf16[4,40,1024]{2,1,0:T(8,128)(2,1)}, bf16[4,40,1024]{2,1,0:T(8,128)(2,1)S(1)}, u32[]{:S(2)}, u32[]{:S(2)}) collective-permute-start(bf16[4,40,1024]{2,1,0:T(8,128)(2,1)} %get-tuple-element.39), channel_id=1, source_target_pairs={{0,4},{1,5},{2,6},{3,7},{4,0},{5,1},{6,2},{7,3},{8,12},{9,13},{10,... | collective-permute-start | bytes 983048 | tf_op jit(solution)/shard_map/ppermute | solution.py:267
  45.0 15.2 %collective-permute-start.6 = (bf16[4,40,1024]{2,1,0:T(8,128)(2,1)}, bf16[4,40,1024]{2,1,0:T(8,128)(2,1)S(1)}, u32[]{:S(2)}, u32[]{:S(2)}) collective-permute-start(bf16[4,40,1024]{2,1,0:T(8,128)(2,1)} %get-tuple-element.40), channel_id=1, source_target_pairs={{0,8},{1,9},{2,10},{3,11},{4,12},{5,13},{6,14},{7,15},{8,0},{9,1},... | collective-permute-start | bytes 983048 | tf_op jit(solution)/shard_map/ppermute | solution.py:267
  45.0 30.6 %collective-permute-start.7 = (bf16[4,40,1024]{2,1,0:T(8,128)(2,1)}, bf16[4,40,1024]{2,1,0:T(8,128)(2,1)}, u32[]{:S(2)}, u32[]{:S(2)}) collective-permute-start(bf16[4,40,1024]{2,1,0:T(8,128)(2,1)} %get-tuple-element.41), channel_id=1, source_target_pairs={{0,12},{1,13},{2,14},{3,15},{4,8},{5,9},{6,10},{7,11},{8,4},{9,5},... | collective-permute-start | bytes 983048 | tf_op jit(solution)/shard_map/ppermute | solution.py:267
  46.4 0.9 copy-start.5
  53.0 28.0 %collective-permute-start.8 = (bf16[2,320,768]{2,1,0:T(8,128)(2,1)S(1)}, bf16[2,320,768]{2,1,0:T(8,128)(2,1)S(1)}, u32[]{:S(2)}, u32[]{:S(2)}) collective-permute-start(bf16[2,320,768]{2,1,0:T(8,128)(2,1)S(1)} %shard_map.98), channel_id=1, source_target_pairs={{0,16},{16,0},{1,17},{17,1},{2,18},{18,2},{3,19},{19,3},{4,20},{20... | collective-permute-start | bytes 2949128 | tf_op jit(solution)/shard_map/ppermute | solution.py:358
  54.4 21.2 %copy-start.2 = (bf16[1,1024,768]{2,1,0:T(8,128)(2,1)S(1)}, bf16[1,1024,768]{2,1,0:T(8,128)(2,1)}, u32[]{:S(2)}) copy-start(bf16[1,1024,768]{2,1,0:T(8,128)(2,1)} %param.13) | copy-start | bytes 4718596
  54.4 21.2 %copy-start.6 = (bf16[512,768]{1,0:T(8,128)(2,1)S(1)}, bf16[512,768]{1,0:T(8,128)(2,1)}, u32[]{:S(2)}) copy-start(bf16[512,768]{1,0:T(8,128)(2,1)} %copy-done.5) | copy-start | bytes 2359300
  54.4 21.2 %copy-start.8 = (bf16[4,40,1024]{2,1,0:T(8,128)(2,1)S(1)}, bf16[4,40,1024]{2,1,0:T(8,128)(2,1)}, u32[]{:S(2)}) copy-start(bf16[4,40,1024]{2,1,0:T(8,128)(2,1)} %get-tuple-element.38) | copy-start | bytes 983044
  82.0 22.6 %collective-permute-start.16 = (bf16[2,320,768]{2,1,0:T(8,128)(2,1)S(1)}, bf16[2,320,768]{2,1,0:T(8,128)(2,1)S(1)}, u32[]{:S(2)}, u32[]{:S(2)}) collective-permute-start(bf16[2,320,768]{2,1,0:T(8,128)(2,1)S(1)} %get-tuple-element.47.d_ref), channel_id=1, source_target_pairs={{0,16},{16,0},{1,17},{17,1},{2,18},{18,2},{3,19},{19,3},{4,20},{20... | collective-permute-start | bytes 2949128 | tf_op jit(solution)/shard_map/ppermute | solution.py:392
  83.1 36.1 %collective-permute-start.9 = (bf16[320,1024]{1,0:T(8,128)(2,1)}, bf16[320,1024]{1,0:T(8,128)(2,1)S(1)}, u32[]{:S(2)}, u32[]{:S(2)}) collective-permute-start(bf16[320,1024]{1,0:T(8,128)(2,1)} %get-tuple-element.48), channel_id=1, source_target_pairs={{0,16},{16,0},{1,17},{17,1},{2,18},{18,2},{3,19},{19,3},{4,20},{20... | collective-permute-start | bytes 1966088 | tf_op jit(solution)/shard_map/ppermute | solution.py:394
  83.5 7.6 %copy-start = (bf16[1,1024,768]{2,1,0:T(8,128)(2,1)S(1)}, bf16[1,1024,768]{2,1,0:T(8,128)(2,1)}, u32[]{:S(2)}) copy-start(bf16[1,1024,768]{2,1,0:T(8,128)(2,1)} %param.11) | copy-start | bytes 4718596
  83.5 7.6 %copy-start.1 = (bf16[1,1024,768]{2,1,0:T(8,128)(2,1)S(1)}, bf16[1,1024,768]{2,1,0:T(8,128)(2,1)}, u32[]{:S(2)}) copy-start(bf16[1,1024,768]{2,1,0:T(8,128)(2,1)} %param.12) | copy-start | bytes 4718596
  87.8 0.7 copy-start.12
  88.5 18.7 %collective-permute-start.11 = (bf16[4,40,1024]{2,1,0:T(8,128)(2,1)S(1)}, bf16[4,40,1024]{2,1,0:T(8,128)(2,1)S(1)}, u32[]{:S(2)}, u32[]{:S(2)}) collective-permute-start(bf16[4,40,1024]{2,1,0:T(8,128)(2,1)S(1)} %get-tuple-element.52), channel_id=1, source_target_pairs={{0,8},{1,9},{2,10},{3,11},{4,12},{5,13},{6,14},{7,15},{8,0},{9,1},... | collective-permute-start | bytes 983048 | tf_op jit(solution)/shard_map/ppermute | solution.py:267
  88.5 30.7 %collective-permute-start.10 = (bf16[4,40,1024]{2,1,0:T(8,128)(2,1)}, bf16[4,40,1024]{2,1,0:T(8,128)(2,1)}, u32[]{:S(2)}, u32[]{:S(2)}) collective-permute-start(bf16[4,40,1024]{2,1,0:T(8,128)(2,1)} %get-tuple-element.51), channel_id=1, source_target_pairs={{0,4},{1,5},{2,6},{3,7},{4,0},{5,1},{6,2},{7,3},{8,12},{9,13},{10,... | collective-permute-start | bytes 983048 | tf_op jit(solution)/shard_map/ppermute | solution.py:267
  89.9 29.3 %collective-permute-start.12 = (bf16[4,40,1024]{2,1,0:T(8,128)(2,1)}, bf16[4,40,1024]{2,1,0:T(8,128)(2,1)}, u32[]{:S(2)}, u32[]{:S(2)}) collective-permute-start(bf16[4,40,1024]{2,1,0:T(8,128)(2,1)} %get-tuple-element.53), channel_id=1, source_target_pairs={{0,12},{1,13},{2,14},{3,15},{4,8},{5,9},{6,10},{7,11},{8,4},{9,5},... | collective-permute-start | bytes 983048 | tf_op jit(solution)/shard_map/ppermute | solution.py:267
  107.2 0.7 copy-start.9
  107.9 45.5 %all-to-all-start.1 = ((bf16[32,40,512]{2,1,0:T(8,128)(2,1)}), bf16[32,40,512]{2,1,0:T(8,128)(2,1)S(1)}, u32[]{:S(2)}, u32[]{:S(2)}) async-start(bf16[32,40,512]{2,1,0:T(8,128)(2,1)} %bitcast.18), calls=%async_computation.1 | async-start | bytes 2621440 | tf_op jit(solution)/shard_map/all_to_all | solution.py:428
  117.9 25.4 %collective-permute-start.17 = (bf16[320,768]{1,0:T(8,128)(2,1)S(1)}, bf16[320,768]{1,0:T(8,128)(2,1)}, u32[]{:S(2)}, u32[]{:S(2)}) collective-permute-start(bf16[320,768]{1,0:T(8,128)(2,1)S(1)} %get-tuple-element.49.hid_ref), channel_id=1, source_target_pairs={{0,16},{16,0},{1,17},{17,1},{2,18},{18,2},{3,19},{19,3},{4,20},{20... | collective-permute-start | bytes 1474568 | tf_op jit(solution)/shard_map/ppermute | solution.py:391
  119.2 1.0 copy-start.10
  120.2 1.0 copy-start.13
  123.3 24.5 %collective-permute-start.13 = (bf16[4,40,1024]{2,1,0:T(8,128)(2,1)}, bf16[4,40,1024]{2,1,0:T(8,128)(2,1)}, u32[]{:S(2)}, u32[]{:S(2)}) collective-permute-start(bf16[4,40,1024]{2,1,0:T(8,128)(2,1)} %get-tuple-element.59), channel_id=1, source_target_pairs={{0,1},{1,0},{2,3},{3,2},{4,5},{5,4},{6,7},{7,6},{8,9},{9,8},{10,11... | collective-permute-start | bytes 983048 | tf_op jit(solution)/shard_map/ppermute | solution.py:267
  124.4 23.5 %collective-permute-start.14 = (bf16[4,40,1024]{2,1,0:T(8,128)(2,1)}, bf16[4,40,1024]{2,1,0:T(8,128)(2,1)}, u32[]{:S(2)}, u32[]{:S(2)}) collective-permute-start(bf16[4,40,1024]{2,1,0:T(8,128)(2,1)} %get-tuple-element.60), channel_id=1, source_target_pairs={{0,2},{1,3},{2,0},{3,1},{4,6},{5,7},{6,4},{7,5},{8,10},{9,11},{10,... | collective-permute-start | bytes 983048 | tf_op jit(solution)/shard_map/ppermute | solution.py:267
  125.2 24.9 %collective-permute-start.15 = (bf16[4,40,1024]{2,1,0:T(8,128)(2,1)}, bf16[4,40,1024]{2,1,0:T(8,128)(2,1)}, u32[]{:S(2)}, u32[]{:S(2)}) collective-permute-start(bf16[4,40,1024]{2,1,0:T(8,128)(2,1)} %get-tuple-element.61), channel_id=1, source_target_pairs={{0,3},{1,2},{2,1},{3,0},{4,7},{5,6},{6,5},{7,4},{8,11},{9,10},{10,... | collective-permute-start | bytes 983048 | tf_op jit(solution)/shard_map/ppermute | solution.py:267
  143.4 6.7 %copy-start.11 = (bf16[4,40,1024]{2,1,0:T(8,128)(2,1)S(1)}, bf16[4,40,1024]{2,1,0:T(8,128)(2,1)}, u32[]{:S(2)}) copy-start(bf16[4,40,1024]{2,1,0:T(8,128)(2,1)} %get-tuple-element.58) | copy-start | bytes 983044

commit v5 on v4

--- a/solution.py
+++ b/solution.py
@@ -108,6 +108,24 @@
         rows_k = mm(pick, both)
         total = rows_k if total is None else total + rows_k
     spread(total, out_refs, slice(None), 2 * cap)
+
+
+def halve_kernel(pieces, from_ref, *refs):
+    *out_refs, held_ref, sems = refs
+    size = out_refs[0].shape[0] // pieces
+    parts = [(i, p, pl.ds((i * pieces + p) * size, size)) for i in range(2) for p in range(pieces)]
+    arrive = [pltpu.make_async_copy(from_ref.at[at], held_ref.at[at], sems.at[0, i, p]) for i, p, at in parts]
+    leave = [
+        pltpu.make_async_copy(held_ref.at[at], out_refs[i].at[pl.ds(p * size, size)], sems.at[1, i, p])
+        for i, p, at in parts
+    ]
+    for copy in arrive:
+        copy.start()
+    for came, copy in zip(arrive, leave):
+        came.wait()
+        copy.start()
+    for copy in leave:
+        copy.wait()
 
 
 def regroup_kernel(count, *refs):
@@ -280,8 +298,17 @@
             moved=8 * rows * half,
         )(*blocks)
 
-    cuts = (0, quarter, half)
-    down_others = [lax.ppermute(w_down[lo:hi], "dp", swap) for lo, hi in zip(cuts, cuts[1:])]
+    pieces = 4
+    down_halves = call(
+        functools.partial(halve_kernel, pieces),
+        tuple(pltpu.HBM((quarter, ff), BF16) for _ in range(2)),
+        (1,),
+        [HBM],
+        (HBM, HBM),
+        [pltpu.VMEM((half, ff), BF16), pltpu.SemaphoreType.DMA((2, 2, pieces))],
+        moved=2 * weight_bytes,
+    )(pltpu.with_memory_space_constraint(w_down, pltpu.HBM))
+    down_others = [lax.ppermute(each, "dp", swap) for each in down_halves]
     dy_near = call(
         functools.partial(send_grads_kernel, peers, cap),
         tuple(shape(*near_block) for _ in range(PLANE)),

time: 156 us -> 155 us (level)
  local copies, waits for them, and re-layouts: 7.57 us -> 4.88 us
  Pallas kernels: 41.1 us -> 43.4 us
    slice x1 -> x0, local copies, waits for them, and re-layouts: 2.69 us -> none  [split_width(): w_down[lo:hi]]
    pallas_call x0 -> x1, Pallas kernels: none -> 2.37 us  [split_width(): call(functools.partial(halve_kernel, pieces), tuple((pltpu.HBM((quarter,...]
where the time goes in v5:
time: 155 us
  waiting for transfers between devices  73.3 us (47%)
  Pallas kernels  43.4 us (28%)
  starting transfers between devices  32.3 us (21%)
  local copies, waits for them, and re-layouts  4.88 us (3%)
    ppermute x12, waiting for transfers between devices, exchange(): lax.ppermute(blocks[m], 'expert', [(i, i ^ m * stride) for i in range(pee...  44.5 us
    ppermute x1, waiting for transfers between devices, split_width(): hidden_recv = lax.ppermute(hidden, 'dp', swap)  17.2 us
    ppermute x1, waiting for transfers between devices, split_width(): d_recv = lax.ppermute(d_pair, 'dp', swap)  10.9 us
    ppermute x12, starting transfers between devices, exchange(): lax.ppermute(blocks[m], 'expert', [(i, i ^ m * stride) for i in range(pee...  10.2 us
    all_to_all x1, starting transfers between devices, split_width(): lax.all_to_all(dx_send.reshape(2 * peers, 2 * cap, quarter), ('dp', 'expe...  9.97 us
    pallas_call x2, Pallas kernels, partial(): pl.pallas_call(functools.partial(partial_kernel, tile), out_shape=shape(2...  9.36 us
    all_to_all x1, starting transfers between devices, split_width(): lax.all_to_all(tok_send.reshape(2 * peers, 2 * cap, quarter), ('dp', 'exp...  5.61 us
    pallas_call x1, Pallas kernels, split_width(): call(hidden_grad_kernel, (shape(rows, ff, dtype=F32), shape(rows, half),...  5.29 us
  transfers between devices with their start and end apart: 20, of which 8 were waited for; matrix products, arithmetic and copies ran while one was open for 0% of the time, Pallas kernels for 25%

profile of v5, /device:TPU:17, one launch (start us, length us, event | category | flops | bytes accessed | tf_op | source)
XLA Modules:
  0.0 155.0 jit_solution(7621342695992727421)
XLA Ops:
  0.6 2.4 %shard_map.94 = (bf16[512,768]{1,0:T(8,128)(2,1)}, bf16[512,768]{1,0:T(8,128)(2,1)}) custom-call(bf16[1024,768]{1,0:T(8,128)(2,1)} %bitcast.30), custom_call_target="tpu_custom_call" | custom-call | bytes 3145728 | tf_op jit(solution)/shard_map/pallas_call | solution.py:302
  3.0 1.3 collective-permute-start
  4.3 1.7 %shard_map.98 = bf16[2,640,512]{2,1,0:T(8,128)(2,1)} custom-call(s32[2,128]{1,0:T(2,128)S(1)} %bitcast.33, bf16[128,2048]{1,0:T(8,128)(2,1)S(1)} %copy-done.3), custom_call_target="tpu_custom_call" | custom-call | flops 335544320 | bytes 1835008 | tf_op jit(solution)/shard_map/pallas_call | solution.py:323
  6.0 5.6 %all-to-all-start = ((bf16[32,40,512]{2,1,0:T(8,128)(2,1)}), bf16[32,40,512]{2,1,0:T(8,128)(2,1)S(1)}, u32[]{:S(2)}, u32[]{:S(2)}) async-start(bf16[32,40,512]{2,1,0:T(8,128)(2,1)} %bitcast.4), calls=%async_computation | async-start | bytes 2621440 | tf_op jit(solution)/shard_map/all_to_all | solution.py:332
  11.8 1.1 shard_map.95
  12.9 0.4 collective-permute-start.1
  13.3 1.2 collective-permute-start.2
  14.5 0.6 collective-permute-start.3
  15.1 1.2 collective-permute-start.4
  16.4 11.1 %collective-permute-done.2.refs_2_ = bf16[4,40,1024]{2,1,0:T(8,128)(2,1)S(1)} collective-permute-done((bf16[4,40,1024]{2,1,0:T(8,128)(2,1)S(1)}, bf16[4,40,1024]{2,1,0:T(8,128)(2,1)S(1)}, u32[]{:S(2)}, u32[]{:S(2)}) %collective-permute-start.2) | collective-permute-done | bytes 327712 | tf_op jit(solution)/shard_map/ppermute | solution.py:285
  27.5 14.8 %collective-permute-done.3.refs_3_ = bf16[4,40,1024]{2,1,0:T(8,128)(2,1)S(1)} collective-permute-done((bf16[4,40,1024]{2,1,0:T(8,128)(2,1)S(1)}, bf16[4,40,1024]{2,1,0:T(8,128)(2,1)S(1)}, u32[]{:S(2)}, u32[]{:S(2)}) %collective-permute-start.3) | collective-permute-done | bytes 327712 | tf_op jit(solution)/shard_map/ppermute | solution.py:285
  42.3 1.1 shard_map.96
  43.5 1.3 collective-permute-start.5
  44.8 1.4 collective-permute-start.7
  46.1 0.9 copy-done.5
  47.0 0.2 copy.16.target_ref
  47.2 0.2 shard_map.97.pick_ref
  47.4 4.6 %shard_map.99 = bf16[2,320,768]{2,1,0:T(8,128)(2,1)S(1)} custom-call(s32[1]{0:T(128)} %bitcast.group_ref, bf16[640,640]{1,0:T(8,128)(2,1)S(1)} %shard_map.97.pick_ref, bf16[2,640,512]{2,1,0:T(8,128)(2,1)S(1)} %bitcast.27, bf16[1024,768]{1,0:T(8,128)(2,1)} %bitcast.19, bf16[1024,768]{1,0:T(8,128)(2,1)} %bitcast.23), custom_call_target="tpu_custom_call" | custom-call | flops 1006632960 | bytes 3801088 | tf_op jit(solution)/shard_map/pallas_call | solution.py:352
  52.0 0.7 collective-permute-done.4.other_1_ref
  52.7 1.2 collective-permute-start.8
  54.2 4.8 %shard_map.101.mine_ref = f32[2,320,768]{2,1,0:T(8,128)S(1)} custom-call(s32[1]{0:T(128)} %bitcast.group_ref, bf16[640,640]{1,0:T(8,128)(2,1)S(1)} %shard_map.97.pick_ref, bf16[2,640,512]{2,1,0:T(8,128)(2,1)S(1)} %bitcast.28, bf16[1024,768]{1,0:T(8,128)(2,1)} %bitcast.20, bf16[1024,768]{1,0:T(8,128)(2,1)} %bitcast.24), custom_call_target="tpu_custom_call" | custom-call | flops 1006632960 | bytes 3801088 | tf_op jit(solution)/shard_map/pallas_call | solution.py:352
  59.0 1.0 collective-permute-done.6
  60.0 15.4 %collective-permute-done.7 = bf16[4,40,1024]{2,1,0:T(8,128)(2,1)} collective-permute-done((bf16[4,40,1024]{2,1,0:T(8,128)(2,1)}, bf16[4,40,1024]{2,1,0:T(8,128)(2,1)}, u32[]{:S(2)}, u32[]{:S(2)}) %collective-permute-start.7) | collective-permute-done | bytes 327712 | tf_op jit(solution)/shard_map/ppermute | solution.py:285
  75.4 5.3 %shard_map.100 = (f32[320,768]{1,0:T(8,128)S(1)}, bf16[320,1024]{1,0:T(8,128)(2,1)S(1)}, bf16[320,1024]{1,0:T(8,128)(2,1)}) custom-call(s32[640,1]{1,0:T(8,128)S(1)} %broadcast_in_dim.21.target_ref, bf16[1024,768]{1,0:T(8,128)(2,1)S(1)} %bitcast.31, bf16[512,768]{1,0:T(8,128)(2,1)S(1)} %copy-done.6, bf16[512,768]{1,0:T(8,128)(2,1)} %collective-permute-done.4.other_1_ref, ...), custom_call_target="tpu_custom_call" | custom-call | flops 9006632960 | bytes 4456448 | tf_op jit(solution)/shard_map/pallas_call | solution.py:389
  80.7 1.1 shard_map.102
  81.7 1.1 collective-permute-start.16
  82.9 0.4 collective-permute-start.9
  83.3 4.3 %shard_map.103 = (bf16[4,40,1024]{2,1,0:T(8,128)(2,1)S(1)}, bf16[4,40,1024]{2,1,0:T(8,128)(2,1)}, bf16[4,40,1024]{2,1,0:T(8,128)(2,1)S(1)}, bf16[4,40,1024]{2,1,0:T(8,128)(2,1)}) custom-call(s32[1,640]{1,0:T(1,128)S(1)} %broadcast_in_dim.18.target_ref, bf16[320,768]{1,0:T(8,128)(2,1)S(1)} %get-tuple-element.53.hid_ref, bf16[1024,768]{1,0:T(8,128)(2,1)S(1)} %bitcast.32, ...), custom_call_target="tpu_custom_call" | custom-call | flops 1006632960 | bytes 4456448 | tf_op jit(solution)/shard_map/pallas_call | solution.py:408
  87.5 0.7 copy-done.12
  88.3 1.4 collective-permute-start.10
  89.6 1.3 collective-permute-start.12
  90.9 2.6 %shard_map.106.refs_0_ = bf16[2,640,512]{2,1,0:T(8,128)(2,1)} custom-call(s32[1]{0:T(128)} %bitcast.group_ref, s32[1,640]{1,0:T(1,128)S(1)} %broadcast_in_dim.19.target_ref, bf16[2,320,768]{2,1,0:T(8,128)(2,1)S(1)} %get-tuple-element.51.d_ref, bf16[1024,768]{1,0:T(8,128)(2,1)S(1)} %bitcast.21, bf16[1024,768]{1,0:T(8,128)(2,1)S(1)} %bitcast.25), custom_call_target="tpu_custom_call" | custom-call | flops 1006632960 | bytes 3801088 | tf_op jit(solution)/shard_map/pallas_call | solution.py:426
  93.5 10.9 %collective-permute-done.16.d_ref = bf16[2,320,768]{2,1,0:T(8,128)(2,1)S(1)} collective-permute-done((bf16[2,320,768]{2,1,0:T(8,128)(2,1)S(1)}, bf16[2,320,768]{2,1,0:T(8,128)(2,1)S(1)}, u32[]{:S(2)}, u32[]{:S(2)}) %collective-permute-start.16) | collective-permute-done | bytes 983072 | tf_op jit(solution)/shard_map/ppermute | solution.py:419
  104.4 2.6 %shard_map.107 = bf16[2,640,512]{2,1,0:T(8,128)(2,1)} custom-call(s32[1]{0:T(128)} %bitcast.group_ref, s32[1,640]{1,0:T(1,128)S(1)} %broadcast_in_dim.19.target_ref, bf16[2,320,768]{2,1,0:T(8,128)(2,1)S(1)} %collective-permute-done.16.d_ref, bf16[1024,768]{1,0:T(8,128)(2,1)S(1)} %bitcast.22, ...), custom_call_target="tpu_custom_call", output_to_operand_aliasing={{}: (5, {})} | custom-call | flops 1006632960 | bytes 3801088 | tf_op jit(solution)/shard_map/pallas_call | solution.py:426
  107.0 0.7 copy-done.9
  107.7 10.0 %all-to-all-start.1 = ((bf16[32,40,512]{2,1,0:T(8,128)(2,1)}), bf16[32,40,512]{2,1,0:T(8,128)(2,1)S(1)}, u32[]{:S(2)}, u32[]{:S(2)}) async-start(bf16[32,40,512]{2,1,0:T(8,128)(2,1)} %bitcast.16), calls=%async_computation.1 | async-start | bytes 2621440 | tf_op jit(solution)/shard_map/all_to_all | solution.py:455
  117.7 1.3 collective-permute-start.17
  119.0 1.0 copy-done.10
  119.9 1.0 copy-done.13
  120.9 2.2 %shard_map.104 = (bf16[4,40,1024]{2,1,0:T(8,128)(2,1)}, bf16[4,40,1024]{2,1,0:T(8,128)(2,1)}, bf16[4,40,1024]{2,1,0:T(8,128)(2,1)}, bf16[4,40,1024]{2,1,0:T(8,128)(2,1)}) custom-call(bf16[4,40,1024]{2,1,0:T(8,128)(2,1)S(1)} %copy-done.13, bf16[4,40,1024]{2,1,0:T(8,128)(2,1)} %collective-permute-done.10.refs_1_, bf16[4,40,1024]{2,1,0:T(8,128)(2,1)S(1)} %copy-done.10, ...), custom_call_target="tpu_custom_call" | custom-call | flops 20000000000 | bytes 2621440 | tf_op jit(solution)/shard_map/pallas_call | solution.py:291
  123.1 1.1 collective-permute-start.13
  124.1 0.8 collective-permute-start.14
  124.9 0.8 collective-permute-start.15
  125.9 17.2 %collective-permute-done.17.hid_recv_ref = bf16[320,768]{1,0:T(8,128)(2,1)} collective-permute-done((bf16[320,768]{1,0:T(8,128)(2,1)S(1)}, bf16[320,768]{1,0:T(8,128)(2,1)}, u32[]{:S(2)}, u32[]{:S(2)}) %collective-permute-start.17) | collective-permute-done | bytes 491552 | tf_op jit(solution)/shard_map/ppermute | solution.py:418
  143.1 4.5 %shard_map.109 = bf16[1024,768]{1,0:T(8,128)(2,1)} custom-call(bf16[320,1024]{1,0:T(8,128)(2,1)S(1)} %get-tuple-element.68.mine_ref, bf16[320,1024]{1,0:T(8,128)(2,1)S(1)} %collective-permute-done.9.recv_ref, bf16[320,768]{1,0:T(8,128)(2,1)S(1)} %get-tuple-element.53.hid_ref, bf16[320,768]{1,0:T(8,128)(2,1)} %collective-permute-done.17.hid_recv_ref), custom_call_target="tpu_custom_call" | custom-call | flops 1006632960 | bytes 2883584 | tf_op jit(solution)/shard_map/pallas_call | solution.py:460
  147.6 2.2 %collective-permute-done.15 = bf16[4,40,1024]{2,1,0:T(8,128)(2,1)} collective-permute-done((bf16[4,40,1024]{2,1,0:T(8,128)(2,1)}, bf16[4,40,1024]{2,1,0:T(8,128)(2,1)}, u32[]{:S(2)}, u32[]{:S(2)}) %collective-permute-start.15) | collective-permute-done | bytes 327712 | tf_op jit(solution)/shard_map/ppermute | solution.py:285
  149.8 3.4 %shard_map.105 = bf16[128,2048]{1,0:T(8,128)(2,1)} custom-call(s32[1]{0:T(128)} %bitcast.group_ref, s32[1]{0:T(128)} %bitcast.1.expert_ref, s32[128,2]{1,0:T(8,128)S(1)} %copy.18.slots_ref, f32[128,2]{1,0:T(8,128)S(1)} %copy.19.gates_ref, bf16[160,1024]{1,0:T(8,128)(2,1)S(1)} %bitcast.38, bf16[160,1024]{1,0:T(8,128)(2,1)} %bitcast.13.refs_1_, ...), custom_call_target="tpu_custom_call" | custom-call | flops 671088640 | bytes 1835008 | tf_op jit(solution)/shard_map/pallas_call | solution.py:469
  153.2 1.8 %shard_map.108 = bf16[128,2048]{1,0:T(8,128)(2,1)} custom-call(s32[128,2]{1,0:T(8,128)S(1)} %copy.18.slots_ref, bf16[2,640,512]{2,1,0:T(8,128)(2,1)S(1)} %bitcast.29), custom_call_target="tpu_custom_call" | custom-call | flops 335544320 | bytes 1835008 | tf_op jit(solution)/shard_map/pallas_call | solution.py:480
  (49 shorter events, 0.7 us)
Async XLA Ops:
  0.6 3.7 %copy-start.4 = (s32[128,2]{0,1:T(2,128)S(1)}, s32[128,2]{0,1:T(2,128)}, u32[]{:S(2)}) copy-start(s32[128,2]{0,1:T(2,128)} %param.10) | copy-start | bytes 3076
  0.6 3.7 %copy-start.3 = (bf16[128,2048]{1,0:T(8,128)(2,1)S(1)}, bf16[128,2048]{1,0:T(8,128)(2,1)}, u32[]{:S(2)}) copy-start(bf16[128,2048]{1,0:T(8,128)(2,1)} %tok_ref.1) | copy-start | bytes 1572868
  3.0 43.1 %collective-permute-start = (bf16[512,768]{1,0:T(8,128)(2,1)}, bf16[512,768]{1,0:T(8,128)(2,1)S(1)}, u32[]{:S(2)}, u32[]{:S(2)}) collective-permute-start(bf16[512,768]{1,0:T(8,128)(2,1)} %get-tuple-element.36), channel_id=1, source_target_pairs={{0,16},{16,0},{1,17},{17,1},{2,18},{18,2},{3,19},{19,3},{4,20},{20... | collective-permute-start | bytes 2359304 | tf_op jit(solution)/shard_map/ppermute | solution.py:311
  6.0 5.6 %copy-start.14 = (f32[128,2]{0,1:T(2,128)S(1)}, f32[128,2]{0,1:T(2,128)}, u32[]{:S(2)}) copy-start(f32[128,2]{0,1:T(2,128)} %param.9) | copy-start | bytes 3076
  6.0 5.7 %copy-start.7 = (bf16[128,2048]{1,0:T(8,128)(2,1)S(1)}, bf16[128,2048]{1,0:T(8,128)(2,1)}, u32[]{:S(2)}) copy-start(bf16[128,2048]{1,0:T(8,128)(2,1)} %grad_ref.1) | copy-start | bytes 1572868
  6.0 41.4 %all-to-all-start = ((bf16[32,40,512]{2,1,0:T(8,128)(2,1)}), bf16[32,40,512]{2,1,0:T(8,128)(2,1)S(1)}, u32[]{:S(2)}, u32[]{:S(2)}) async-start(bf16[32,40,512]{2,1,0:T(8,128)(2,1)} %bitcast.4), calls=%async_computation | async-start | bytes 2621440 | tf_op jit(solution)/shard_map/all_to_all | solution.py:332
  12.9 3.5 %collective-permute-start.1 = (bf16[4,40,1024]{2,1,0:T(8,128)(2,1)S(1)}, bf16[4,40,1024]{2,1,0:T(8,128)(2,1)S(1)}, u32[]{:S(2)}, u32[]{:S(2)}) collective-permute-start(bf16[4,40,1024]{2,1,0:T(8,128)(2,1)S(1)} %get-tuple-element.38), channel_id=1, source_target_pairs={{0,1},{1,0},{2,3},{3,2},{4,5},{5,4},{6,7},{7,6},{8,9},{9,8},{10,11... | collective-permute-start | bytes 983048 | tf_op jit(solution)/shard_map/ppermute | solution.py:285
  13.3 14.2 %collective-permute-start.2 = (bf16[4,40,1024]{2,1,0:T(8,128)(2,1)S(1)}, bf16[4,40,1024]{2,1,0:T(8,128)(2,1)S(1)}, u32[]{:S(2)}, u32[]{:S(2)}) collective-permute-start(bf16[4,40,1024]{2,1,0:T(8,128)(2,1)S(1)} %get-tuple-element.39), channel_id=1, source_target_pairs={{0,2},{1,3},{2,0},{3,1},{4,6},{5,7},{6,4},{7,5},{8,10},{9,11},{10,... | collective-permute-start | bytes 983048 | tf_op jit(solution)/shard_map/ppermute | solution.py:285
  14.5 27.8 %collective-permute-start.3 = (bf16[4,40,1024]{2,1,0:T(8,128)(2,1)S(1)}, bf16[4,40,1024]{2,1,0:T(8,128)(2,1)S(1)}, u32[]{:S(2)}, u32[]{:S(2)}) collective-permute-start(bf16[4,40,1024]{2,1,0:T(8,128)(2,1)S(1)} %get-tuple-element.40), channel_id=1, source_target_pairs={{0,3},{1,2},{2,1},{3,0},{4,7},{5,6},{6,5},{7,4},{8,11},{9,10},{10,... | collective-permute-start | bytes 983048 | tf_op jit(solution)/shard_map/ppermute | solution.py:285
  15.1 37.6 %collective-permute-start.4 = (bf16[512,768]{1,0:T(8,128)(2,1)}, bf16[512,768]{1,0:T(8,128)(2,1)}, u32[]{:S(2)}, u32[]{:S(2)}) collective-permute-start(bf16[512,768]{1,0:T(8,128)(2,1)} %get-tuple-element.46), channel_id=1, source_target_pairs={{0,16},{16,0},{1,17},{17,1},{2,18},{18,2},{3,19},{19,3},{4,20},{20... | collective-permute-start | bytes 2359304 | tf_op jit(solution)/shard_map/ppermute | solution.py:311
  43.5 15.6 %collective-permute-start.5 = (bf16[4,40,1024]{2,1,0:T(8,128)(2,1)}, bf16[4,40,1024]{2,1,0:T(8,128)(2,1)S(1)}, u32[]{:S(2)}, u32[]{:S(2)}) collective-permute-start(bf16[4,40,1024]{2,1,0:T(8,128)(2,1)} %get-tuple-element.42), channel_id=1, source_target_pairs={{0,4},{1,5},{2,6},{3,7},{4,0},{5,1},{6,2},{7,3},{8,12},{9,13},{10,... | collective-permute-start | bytes 983048 | tf_op jit(solution)/shard_map/ppermute | solution.py:285
  44.7 15.2 %collective-permute-start.6 = (bf16[4,40,1024]{2,1,0:T(8,128)(2,1)}, bf16[4,40,1024]{2,1,0:T(8,128)(2,1)S(1)}, u32[]{:S(2)}, u32[]{:S(2)}) collective-permute-start(bf16[4,40,1024]{2,1,0:T(8,128)(2,1)} %get-tuple-element.43), channel_id=1, source_target_pairs={{0,8},{1,9},{2,10},{3,11},{4,12},{5,13},{6,14},{7,15},{8,0},{9,1},... | collective-permute-start | bytes 983048 | tf_op jit(solution)/shard_map/ppermute | solution.py:285
  44.8 30.6 %collective-permute-start.7 = (bf16[4,40,1024]{2,1,0:T(8,128)(2,1)}, bf16[4,40,1024]{2,1,0:T(8,128)(2,1)}, u32[]{:S(2)}, u32[]{:S(2)}) collective-permute-start(bf16[4,40,1024]{2,1,0:T(8,128)(2,1)} %get-tuple-element.44), channel_id=1, source_target_pairs={{0,12},{1,13},{2,14},{3,15},{4,8},{5,9},{6,10},{7,11},{8,4},{9,5},... | collective-permute-start | bytes 983048 | tf_op jit(solution)/shard_map/ppermute | solution.py:285
  46.1 0.9 copy-start.5
  52.7 28.0 %collective-permute-start.8 = (bf16[2,320,768]{2,1,0:T(8,128)(2,1)S(1)}, bf16[2,320,768]{2,1,0:T(8,128)(2,1)S(1)}, u32[]{:S(2)}, u32[]{:S(2)}) collective-permute-start(bf16[2,320,768]{2,1,0:T(8,128)(2,1)S(1)} %shard_map.99), channel_id=1, source_target_pairs={{0,16},{16,0},{1,17},{17,1},{2,18},{18,2},{3,19},{19,3},{4,20},{20... | collective-permute-start | bytes 2949128 | tf_op jit(solution)/shard_map/ppermute | solution.py:385
  54.2 21.2 %copy-start.2 = (bf16[1,1024,768]{2,1,0:T(8,128)(2,1)S(1)}, bf16[1,1024,768]{2,1,0:T(8,128)(2,1)}, u32[]{:S(2)}) copy-start(bf16[1,1024,768]{2,1,0:T(8,128)(2,1)} %param.13) | copy-start | bytes 4718596
  54.2 21.2 %copy-start.6 = (bf16[512,768]{1,0:T(8,128)(2,1)S(1)}, bf16[512,768]{1,0:T(8,128)(2,1)}, u32[]{:S(2)}) copy-start(bf16[512,768]{1,0:T(8,128)(2,1)} %copy-done.5) | copy-start | bytes 2359300
  54.2 21.2 %copy-start.8 = (bf16[4,40,1024]{2,1,0:T(8,128)(2,1)S(1)}, bf16[4,40,1024]{2,1,0:T(8,128)(2,1)}, u32[]{:S(2)}) copy-start(bf16[4,40,1024]{2,1,0:T(8,128)(2,1)} %get-tuple-element.41) | copy-start | bytes 983044
  81.7 22.6 %collective-permute-start.16 = (bf16[2,320,768]{2,1,0:T(8,128)(2,1)S(1)}, bf16[2,320,768]{2,1,0:T(8,128)(2,1)S(1)}, u32[]{:S(2)}, u32[]{:S(2)}) collective-permute-start(bf16[2,320,768]{2,1,0:T(8,128)(2,1)S(1)} %get-tuple-element.51.d_ref), channel_id=1, source_target_pairs={{0,16},{16,0},{1,17},{17,1},{2,18},{18,2},{3,19},{19,3},{4,20},{20... | collective-permute-start | bytes 2949128 | tf_op jit(solution)/shard_map/ppermute | solution.py:419
  82.9 36.1 %collective-permute-start.9 = (bf16[320,1024]{1,0:T(8,128)(2,1)}, bf16[320,1024]{1,0:T(8,128)(2,1)S(1)}, u32[]{:S(2)}, u32[]{:S(2)}) collective-permute-start(bf16[320,1024]{1,0:T(8,128)(2,1)} %get-tuple-element.52), channel_id=1, source_target_pairs={{0,16},{16,0},{1,17},{17,1},{2,18},{18,2},{3,19},{19,3},{4,20},{20... | collective-permute-start | bytes 1966088 | tf_op jit(solution)/shard_map/ppermute | solution.py:421
  83.3 7.6 %copy-start = (bf16[1,1024,768]{2,1,0:T(8,128)(2,1)S(1)}, bf16[1,1024,768]{2,1,0:T(8,128)(2,1)}, u32[]{:S(2)}) copy-start(bf16[1,1024,768]{2,1,0:T(8,128)(2,1)} %param.11) | copy-start | bytes 4718596
  83.3 7.6 %copy-start.1 = (bf16[1,1024,768]{2,1,0:T(8,128)(2,1)S(1)}, bf16[1,1024,768]{2,1,0:T(8,128)(2,1)}, u32[]{:S(2)}) copy-start(bf16[1,1024,768]{2,1,0:T(8,128)(2,1)} %param.12) | copy-start | bytes 4718596
  87.5 0.7 copy-start.12
  88.3 18.7 %collective-permute-start.11 = (bf16[4,40,1024]{2,1,0:T(8,128)(2,1)S(1)}, bf16[4,40,1024]{2,1,0:T(8,128)(2,1)S(1)}, u32[]{:S(2)}, u32[]{:S(2)}) collective-permute-start(bf16[4,40,1024]{2,1,0:T(8,128)(2,1)S(1)} %get-tuple-element.56), channel_id=1, source_target_pairs={{0,8},{1,9},{2,10},{3,11},{4,12},{5,13},{6,14},{7,15},{8,0},{9,1},... | collective-permute-start | bytes 983048 | tf_op jit(solution)/shard_map/ppermute | solution.py:285
  88.3 30.7 %collective-permute-start.10 = (bf16[4,40,1024]{2,1,0:T(8,128)(2,1)}, bf16[4,40,1024]{2,1,0:T(8,128)(2,1)}, u32[]{:S(2)}, u32[]{:S(2)}) collective-permute-start(bf16[4,40,1024]{2,1,0:T(8,128)(2,1)} %get-tuple-element.55), channel_id=1, source_target_pairs={{0,4},{1,5},{2,6},{3,7},{4,0},{5,1},{6,2},{7,3},{8,12},{9,13},{10,... | collective-permute-start | bytes 983048 | tf_op jit(solution)/shard_map/ppermute | solution.py:285
  89.6 29.3 %collective-permute-start.12 = (bf16[4,40,1024]{2,1,0:T(8,128)(2,1)}, bf16[4,40,1024]{2,1,0:T(8,128)(2,1)}, u32[]{:S(2)}, u32[]{:S(2)}) collective-permute-start(bf16[4,40,1024]{2,1,0:T(8,128)(2,1)} %get-tuple-element.57), channel_id=1, source_target_pairs={{0,12},{1,13},{2,14},{3,15},{4,8},{5,9},{6,10},{7,11},{8,4},{9,5},... | collective-permute-start | bytes 983048 | tf_op jit(solution)/shard_map/ppermute | solution.py:285
  107.0 0.7 copy-start.9
  107.7 45.5 %all-to-all-start.1 = ((bf16[32,40,512]{2,1,0:T(8,128)(2,1)}), bf16[32,40,512]{2,1,0:T(8,128)(2,1)S(1)}, u32[]{:S(2)}, u32[]{:S(2)}) async-start(bf16[32,40,512]{2,1,0:T(8,128)(2,1)} %bitcast.16), calls=%async_computation.1 | async-start | bytes 2621440 | tf_op jit(solution)/shard_map/all_to_all | solution.py:455
  117.7 25.4 %collective-permute-start.17 = (bf16[320,768]{1,0:T(8,128)(2,1)S(1)}, bf16[320,768]{1,0:T(8,128)(2,1)}, u32[]{:S(2)}, u32[]{:S(2)}) collective-permute-start(bf16[320,768]{1,0:T(8,128)(2,1)S(1)} %get-tuple-element.53.hid_ref), channel_id=1, source_target_pairs={{0,16},{16,0},{1,17},{17,1},{2,18},{18,2},{3,19},{19,3},{4,20},{20... | collective-permute-start | bytes 1474568 | tf_op jit(solution)/shard_map/ppermute | solution.py:418
  119.0 1.0 copy-start.10
  119.9 1.0 copy-start.13
  123.1 24.5 %collective-permute-start.13 = (bf16[4,40,1024]{2,1,0:T(8,128)(2,1)}, bf16[4,40,1024]{2,1,0:T(8,128)(2,1)}, u32[]{:S(2)}, u32[]{:S(2)}) collective-permute-start(bf16[4,40,1024]{2,1,0:T(8,128)(2,1)} %get-tuple-element.63), channel_id=1, source_target_pairs={{0,1},{1,0},{2,3},{3,2},{4,5},{5,4},{6,7},{7,6},{8,9},{9,8},{10,11... | collective-permute-start | bytes 983048 | tf_op jit(solution)/shard_map/ppermute | solution.py:285
  124.1 23.5 %collective-permute-start.14 = (bf16[4,40,1024]{2,1,0:T(8,128)(2,1)}, bf16[4,40,1024]{2,1,0:T(8,128)(2,1)}, u32[]{:S(2)}, u32[]{:S(2)}) collective-permute-start(bf16[4,40,1024]{2,1,0:T(8,128)(2,1)} %get-tuple-element.64), channel_id=1, source_target_pairs={{0,2},{1,3},{2,0},{3,1},{4,6},{5,7},{6,4},{7,5},{8,10},{9,11},{10,... | collective-permute-start | bytes 983048 | tf_op jit(solution)/shard_map/ppermute | solution.py:285
  124.9 24.9 %collective-permute-start.15 = (bf16[4,40,1024]{2,1,0:T(8,128)(2,1)}, bf16[4,40,1024]{2,1,0:T(8,128)(2,1)}, u32[]{:S(2)}, u32[]{:S(2)}) collective-permute-start(bf16[4,40,1024]{2,1,0:T(8,128)(2,1)} %get-tuple-element.65), channel_id=1, source_target_pairs={{0,3},{1,2},{2,1},{3,0},{4,7},{5,6},{6,5},{7,4},{8,11},{9,10},{10,... | collective-permute-start | bytes 983048 | tf_op jit(solution)/shard_map/ppermute | solution.py:285
  143.1 6.7 %copy-start.11 = (bf16[4,40,1024]{2,1,0:T(8,128)(2,1)S(1)}, bf16[4,40,1024]{2,1,0:T(8,128)(2,1)}, u32[]{:S(2)}) copy-start(bf16[4,40,1024]{2,1,0:T(8,128)(2,1)} %get-tuple-element.62) | copy-start | bytes 983044

commit v6 on v5

--- a/solution.py
+++ b/solution.py
@@ -229,10 +229,14 @@
     for k, rank in enumerate(ranks_in_rows(slots, peers)):
         near, far = masks_of(slots[:, k : k + 1], expert)
         places.append((near * (peers // PLANE) + far) * (2 * cap) + rank)
+    count, top = slots.shape
+    picks = jnp.concatenate([ones_where(at == place + o * cap) for o in range(2) for place in places], axis=0)
+    found = mm(picks, came_ref[...])
     for o, g in enumerate((group, 1 - group)):
         total = None
-        for k, place in enumerate(places):
-            term = gates[:, k : k + 1] * mm(ones_where(at == place + o * cap), came_ref[...])
+        for k in range(top):
+            lo = (o * top + k) * count
+            term = gates[:, k : k + 1] * found[lo : lo + count]
             total = term if total is None else total + term
         out_ref[:, column_half(g, half)] = total.astype(BF16)
 
@@ -241,12 +245,15 @@
     slots = slots_ref[...]
     places = [slots[:, k : k + 1] * (2 * cap) + rank for k, rank in enumerate(ranks_in_rows(slots, peers))]
     _, rows, width = back_ref.shape
-    at = iota((slots.shape[0], rows), 1)
-    for h in range(2):
-        pick = sum(jnp.where(at == place + h * cap, 1.0, 0.0) for place in places).astype(BF16)
-        for part in range(2):
+    count = slots.shape[0]
+    at = iota((count, rows), 1)
+    picks = [sum(jnp.where(at == place + h * cap, 1.0, 0.0) for place in places) for h in range(2)]
+    pick = jnp.concatenate(picks, axis=0).astype(BF16)
+    for part in range(2):
+        found = mm(pick, back_ref[part]).astype(BF16)
+        for h in range(2):
             lo = (2 * part + h) * width
-            out_ref[:, lo : lo + width] = mm(pick, back_ref[part]).astype(BF16)
+            out_ref[:, lo : lo + width] = found[h * count : (h + 1) * count]
 
 
 def split_width(tokens, out_grad, route_gates, route_slot, gate_weight, up_weight, down_weight):

time: 155 us -> 155 us (level)
  no operation moved by 1% of the time
where the time goes in v6:
time: 155 us
  waiting for transfers between devices  73.3 us (47%)
  Pallas kernels  43.4 us (28%)
  starting transfers between devices  32.3 us (21%)
  local copies, waits for them, and re-layouts  4.88 us (3%)
    ppermute x12, waiting for transfers between devices, exchange(): lax.ppermute(blocks[m], 'expert', [(i, i ^ m * stride) for i in range(pee...  44.5 us
    ppermute x1, waiting for transfers between devices, split_width(): hidden_recv = lax.ppermute(hidden, 'dp', swap)  17.2 us
    ppermute x1, waiting for transfers between devices, split_width(): d_recv = lax.ppermute(d_pair, 'dp', swap)  10.9 us
    ppermute x12, starting transfers between devices, exchange(): lax.ppermute(blocks[m], 'expert', [(i, i ^ m * stride) for i in range(pee...  10.2 us
    all_to_all x1, starting transfers between devices, split_width(): lax.all_to_all(dx_send.reshape(2 * peers, 2 * cap, quarter), ('dp', 'expe...  9.97 us
    pallas_call x2, Pallas kernels, partial(): pl.pallas_call(functools.partial(partial_kernel, tile), out_shape=shape(2...  9.36 us
    all_to_all x1, starting transfers between devices, split_width(): lax.all_to_all(tok_send.reshape(2 * peers, 2 * cap, quarter), ('dp', 'exp...  5.61 us
    pallas_call x1, Pallas kernels, split_width(): call(hidden_grad_kernel, (shape(rows, ff, dtype=F32), shape(rows, half),...  5.29 us
  transfers between devices with their start and end apart: 20, of which 8 were waited for; matrix products, arithmetic and copies ran while one was open for 0% of the time, Pallas kernels for 25%

profile of v6, /device:TPU:17, one launch (start us, length us, event | category | flops | bytes accessed | tf_op | source)
XLA Modules:
  0.0 155.0 jit_solution(13388117029634395572)
XLA Ops:
  0.6 2.4 %shard_map.94 = (bf16[512,768]{1,0:T(8,128)(2,1)}, bf16[512,768]{1,0:T(8,128)(2,1)}) custom-call(bf16[1024,768]{1,0:T(8,128)(2,1)} %bitcast.30), custom_call_target="tpu_custom_call" | custom-call | bytes 3145728 | tf_op jit(solution)/shard_map/pallas_call | solution.py:309
  3.0 1.3 collective-permute-start
  4.3 1.7 %shard_map.98 = bf16[2,640,512]{2,1,0:T(8,128)(2,1)} custom-call(s32[2,128]{1,0:T(2,128)S(1)} %bitcast.33, bf16[128,2048]{1,0:T(8,128)(2,1)S(1)} %copy-done.3), custom_call_target="tpu_custom_call" | custom-call | flops 335544320 | bytes 1835008 | tf_op jit(solution)/shard_map/pallas_call | solution.py:330
  6.0 5.6 %all-to-all-start = ((bf16[32,40,512]{2,1,0:T(8,128)(2,1)}), bf16[32,40,512]{2,1,0:T(8,128)(2,1)S(1)}, u32[]{:S(2)}, u32[]{:S(2)}) async-start(bf16[32,40,512]{2,1,0:T(8,128)(2,1)} %bitcast.4), calls=%async_computation | async-start | bytes 2621440 | tf_op jit(solution)/shard_map/all_to_all | solution.py:339
  11.8 1.1 shard_map.95
  12.9 0.4 collective-permute-start.1
  13.3 1.2 collective-permute-start.2
  14.5 0.6 collective-permute-start.3
  15.1 1.2 collective-permute-start.4
  16.4 11.1 %collective-permute-done.2.refs_2_ = bf16[4,40,1024]{2,1,0:T(8,128)(2,1)S(1)} collective-permute-done((bf16[4,40,1024]{2,1,0:T(8,128)(2,1)S(1)}, bf16[4,40,1024]{2,1,0:T(8,128)(2,1)S(1)}, u32[]{:S(2)}, u32[]{:S(2)}) %collective-permute-start.2) | collective-permute-done | bytes 327712 | tf_op jit(solution)/shard_map/ppermute | solution.py:292
  27.5 14.8 %collective-permute-done.3.refs_3_ = bf16[4,40,1024]{2,1,0:T(8,128)(2,1)S(1)} collective-permute-done((bf16[4,40,1024]{2,1,0:T(8,128)(2,1)S(1)}, bf16[4,40,1024]{2,1,0:T(8,128)(2,1)S(1)}, u32[]{:S(2)}, u32[]{:S(2)}) %collective-permute-start.3) | collective-permute-done | bytes 327712 | tf_op jit(solution)/shard_map/ppermute | solution.py:292
  42.3 1.1 shard_map.96
  43.5 1.3 collective-permute-start.5
  44.8 1.4 collective-permute-start.7
  46.1 0.9 copy-done.5
  47.0 0.2 copy.16.target_ref
  47.2 0.2 shard_map.97.pick_ref
  47.4 4.6 %shard_map.99 = bf16[2,320,768]{2,1,0:T(8,128)(2,1)S(1)} custom-call(s32[1]{0:T(128)} %bitcast.group_ref, bf16[640,640]{1,0:T(8,128)(2,1)S(1)} %shard_map.97.pick_ref, bf16[2,640,512]{2,1,0:T(8,128)(2,1)S(1)} %bitcast.27, bf16[1024,768]{1,0:T(8,128)(2,1)} %bitcast.19, bf16[1024,768]{1,0:T(8,128)(2,1)} %bitcast.23), custom_call_target="tpu_custom_call" | custom-call | flops 1006632960 | bytes 3801088 | tf_op jit(solution)/shard_map/pallas_call | solution.py:359
  52.0 0.7 collective-permute-done.4.other_1_ref
  52.7 1.2 collective-permute-start.8
  54.2 4.8 %shard_map.101.mine_ref = f32[2,320,768]{2,1,0:T(8,128)S(1)} custom-call(s32[1]{0:T(128)} %bitcast.group_ref, bf16[640,640]{1,0:T(8,128)(2,1)S(1)} %shard_map.97.pick_ref, bf16[2,640,512]{2,1,0:T(8,128)(2,1)S(1)} %bitcast.28, bf16[1024,768]{1,0:T(8,128)(2,1)} %bitcast.20, bf16[1024,768]{1,0:T(8,128)(2,1)} %bitcast.24), custom_call_target="tpu_custom_call" | custom-call | flops 1006632960 | bytes 3801088 | tf_op jit(solution)/shard_map/pallas_call | solution.py:359
  59.0 1.0 collective-permute-done.6
  60.0 15.4 %collective-permute-done.7 = bf16[4,40,1024]{2,1,0:T(8,128)(2,1)} collective-permute-done((bf16[4,40,1024]{2,1,0:T(8,128)(2,1)}, bf16[4,40,1024]{2,1,0:T(8,128)(2,1)}, u32[]{:S(2)}, u32[]{:S(2)}) %collective-permute-start.7) | collective-permute-done | bytes 327712 | tf_op jit(solution)/shard_map/ppermute | solution.py:292
  75.4 5.3 %shard_map.100 = (f32[320,768]{1,0:T(8,128)S(1)}, bf16[320,1024]{1,0:T(8,128)(2,1)S(1)}, bf16[320,1024]{1,0:T(8,128)(2,1)}) custom-call(s32[640,1]{1,0:T(8,128)S(1)} %broadcast_in_dim.21.target_ref, bf16[1024,768]{1,0:T(8,128)(2,1)S(1)} %bitcast.31, bf16[512,768]{1,0:T(8,128)(2,1)S(1)} %copy-done.6, bf16[512,768]{1,0:T(8,128)(2,1)} %collective-permute-done.4.other_1_ref, ...), custom_call_target="tpu_custom_call" | custom-call | flops 9006632960 | bytes 4456448 | tf_op jit(solution)/shard_map/pallas_call | solution.py:396
  80.7 1.1 shard_map.102
  81.7 1.1 collective-permute-start.16
  82.9 0.4 collective-permute-start.9
  83.3 4.3 %shard_map.103 = (bf16[4,40,1024]{2,1,0:T(8,128)(2,1)S(1)}, bf16[4,40,1024]{2,1,0:T(8,128)(2,1)}, bf16[4,40,1024]{2,1,0:T(8,128)(2,1)S(1)}, bf16[4,40,1024]{2,1,0:T(8,128)(2,1)}) custom-call(s32[1,640]{1,0:T(1,128)S(1)} %broadcast_in_dim.18.target_ref, bf16[320,768]{1,0:T(8,128)(2,1)S(1)} %get-tuple-element.53.hid_ref, bf16[1024,768]{1,0:T(8,128)(2,1)S(1)} %bitcast.32, ...), custom_call_target="tpu_custom_call" | custom-call | flops 1006632960 | bytes 4456448 | tf_op jit(solution)/shard_map/pallas_call | solution.py:415
  87.5 0.7 copy-done.12
  88.3 1.4 collective-permute-start.10
  89.6 1.3 collective-permute-start.12
  90.9 2.6 %shard_map.106.refs_0_ = bf16[2,640,512]{2,1,0:T(8,128)(2,1)} custom-call(s32[1]{0:T(128)} %bitcast.group_ref, s32[1,640]{1,0:T(1,128)S(1)} %broadcast_in_dim.19.target_ref, bf16[2,320,768]{2,1,0:T(8,128)(2,1)S(1)} %get-tuple-element.51.d_ref, bf16[1024,768]{1,0:T(8,128)(2,1)S(1)} %bitcast.21, bf16[1024,768]{1,0:T(8,128)(2,1)S(1)} %bitcast.25), custom_call_target="tpu_custom_call" | custom-call | flops 1006632960 | bytes 3801088 | tf_op jit(solution)/shard_map/pallas_call | solution.py:433
  93.5 10.9 %collective-permute-done.16.d_ref = bf16[2,320,768]{2,1,0:T(8,128)(2,1)S(1)} collective-permute-done((bf16[2,320,768]{2,1,0:T(8,128)(2,1)S(1)}, bf16[2,320,768]{2,1,0:T(8,128)(2,1)S(1)}, u32[]{:S(2)}, u32[]{:S(2)}) %collective-permute-start.16) | collective-permute-done | bytes 983072 | tf_op jit(solution)/shard_map/ppermute | solution.py:426
  104.4 2.6 %shard_map.107 = bf16[2,640,512]{2,1,0:T(8,128)(2,1)} custom-call(s32[1]{0:T(128)} %bitcast.group_ref, s32[1,640]{1,0:T(1,128)S(1)} %broadcast_in_dim.19.target_ref, bf16[2,320,768]{2,1,0:T(8,128)(2,1)S(1)} %collective-permute-done.16.d_ref, bf16[1024,768]{1,0:T(8,128)(2,1)S(1)} %bitcast.22, ...), custom_call_target="tpu_custom_call", output_to_operand_aliasing={{}: (5, {})} | custom-call | flops 1006632960 | bytes 3801088 | tf_op jit(solution)/shard_map/pallas_call | solution.py:433
  107.0 0.7 copy-done.9
  107.7 10.0 %all-to-all-start.1 = ((bf16[32,40,512]{2,1,0:T(8,128)(2,1)}), bf16[32,40,512]{2,1,0:T(8,128)(2,1)S(1)}, u32[]{:S(2)}, u32[]{:S(2)}) async-start(bf16[32,40,512]{2,1,0:T(8,128)(2,1)} %bitcast.16), calls=%async_computation.1 | async-start | bytes 2621440 | tf_op jit(solution)/shard_map/all_to_all | solution.py:462
  117.7 1.3 collective-permute-start.17
  119.0 1.0 copy-done.10
  119.9 1.0 copy-done.13
  120.9 2.2 %shard_map.104 = (bf16[4,40,1024]{2,1,0:T(8,128)(2,1)}, bf16[4,40,1024]{2,1,0:T(8,128)(2,1)}, bf16[4,40,1024]{2,1,0:T(8,128)(2,1)}, bf16[4,40,1024]{2,1,0:T(8,128)(2,1)}) custom-call(bf16[4,40,1024]{2,1,0:T(8,128)(2,1)S(1)} %copy-done.13, bf16[4,40,1024]{2,1,0:T(8,128)(2,1)} %collective-permute-done.10.refs_1_, bf16[4,40,1024]{2,1,0:T(8,128)(2,1)S(1)} %copy-done.10, ...), custom_call_target="tpu_custom_call" | custom-call | flops 20000000000 | bytes 2621440 | tf_op jit(solution)/shard_map/pallas_call | solution.py:298
  123.1 1.1 collective-permute-start.13
  124.1 0.8 collective-permute-start.14
  124.9 0.8 collective-permute-start.15
  125.9 17.2 %collective-permute-done.17.hid_recv_ref = bf16[320,768]{1,0:T(8,128)(2,1)} collective-permute-done((bf16[320,768]{1,0:T(8,128)(2,1)S(1)}, bf16[320,768]{1,0:T(8,128)(2,1)}, u32[]{:S(2)}, u32[]{:S(2)}) %collective-permute-start.17) | collective-permute-done | bytes 491552 | tf_op jit(solution)/shard_map/ppermute | solution.py:425
  143.1 4.5 %shard_map.109 = bf16[1024,768]{1,0:T(8,128)(2,1)} custom-call(bf16[320,1024]{1,0:T(8,128)(2,1)S(1)} %get-tuple-element.68.mine_ref, bf16[320,1024]{1,0:T(8,128)(2,1)S(1)} %collective-permute-done.9.recv_ref, bf16[320,768]{1,0:T(8,128)(2,1)S(1)} %get-tuple-element.53.hid_ref, bf16[320,768]{1,0:T(8,128)(2,1)} %collective-permute-done.17.hid_recv_ref), custom_call_target="tpu_custom_call" | custom-call | flops 1006632960 | bytes 2883584 | tf_op jit(solution)/shard_map/pallas_call | solution.py:467
  147.6 2.2 %collective-permute-done.15 = bf16[4,40,1024]{2,1,0:T(8,128)(2,1)} collective-permute-done((bf16[4,40,1024]{2,1,0:T(8,128)(2,1)}, bf16[4,40,1024]{2,1,0:T(8,128)(2,1)}, u32[]{:S(2)}, u32[]{:S(2)}) %collective-permute-start.15) | collective-permute-done | bytes 327712 | tf_op jit(solution)/shard_map/ppermute | solution.py:292
  149.8 3.4 %shard_map.105 = bf16[128,2048]{1,0:T(8,128)(2,1)} custom-call(s32[1]{0:T(128)} %bitcast.group_ref, s32[1]{0:T(128)} %bitcast.1.expert_ref, s32[128,2]{1,0:T(8,128)S(1)} %copy.18.slots_ref, f32[128,2]{1,0:T(8,128)S(1)} %copy.19.gates_ref, bf16[160,1024]{1,0:T(8,128)(2,1)S(1)} %bitcast.38, bf16[160,1024]{1,0:T(8,128)(2,1)} %bitcast.13.refs_1_, ...), custom_call_target="tpu_custom_call" | custom-call | flops 671088640 | bytes 1835008 | tf_op jit(solution)/shard_map/pallas_call | solution.py:476
  153.2 1.8 %shard_map.108 = bf16[128,2048]{1,0:T(8,128)(2,1)} custom-call(s32[128,2]{1,0:T(8,128)S(1)} %copy.18.slots_ref, bf16[2,640,512]{2,1,0:T(8,128)(2,1)S(1)} %bitcast.29), custom_call_target="tpu_custom_call" | custom-call | flops 335544320 | bytes 1835008 | tf_op jit(solution)/shard_map/pallas_call | solution.py:487
  (49 shorter events, 0.7 us)
Async XLA Ops:
  0.6 3.7 %copy-start.4 = (s32[128,2]{0,1:T(2,128)S(1)}, s32[128,2]{0,1:T(2,128)}, u32[]{:S(2)}) copy-start(s32[128,2]{0,1:T(2,128)} %param.10) | copy-start | bytes 3076
  0.6 3.7 %copy-start.3 = (bf16[128,2048]{1,0:T(8,128)(2,1)S(1)}, bf16[128,2048]{1,0:T(8,128)(2,1)}, u32[]{:S(2)}) copy-start(bf16[128,2048]{1,0:T(8,128)(2,1)} %tok_ref.1) | copy-start | bytes 1572868
  3.0 43.1 %collective-permute-start = (bf16[512,768]{1,0:T(8,128)(2,1)}, bf16[512,768]{1,0:T(8,128)(2,1)S(1)}, u32[]{:S(2)}, u32[]{:S(2)}) collective-permute-start(bf16[512,768]{1,0:T(8,128)(2,1)} %get-tuple-element.36), channel_id=1, source_target_pairs={{0,16},{16,0},{1,17},{17,1},{2,18},{18,2},{3,19},{19,3},{4,20},{20... | collective-permute-start | bytes 2359304 | tf_op jit(solution)/shard_map/ppermute | solution.py:318
  6.0 5.6 %copy-start.14 = (f32[128,2]{0,1:T(2,128)S(1)}, f32[128,2]{0,1:T(2,128)}, u32[]{:S(2)}) copy-start(f32[128,2]{0,1:T(2,128)} %param.9) | copy-start | bytes 3076
  6.0 5.7 %copy-start.7 = (bf16[128,2048]{1,0:T(8,128)(2,1)S(1)}, bf16[128,2048]{1,0:T(8,128)(2,1)}, u32[]{:S(2)}) copy-start(bf16[128,2048]{1,0:T(8,128)(2,1)} %grad_ref.1) | copy-start | bytes 1572868
  6.0 41.4 %all-to-all-start = ((bf16[32,40,512]{2,1,0:T(8,128)(2,1)}), bf16[32,40,512]{2,1,0:T(8,128)(2,1)S(1)}, u32[]{:S(2)}, u32[]{:S(2)}) async-start(bf16[32,40,512]{2,1,0:T(8,128)(2,1)} %bitcast.4), calls=%async_computation | async-start | bytes 2621440 | tf_op jit(solution)/shard_map/all_to_all | solution.py:339
  12.9 3.5 %collective-permute-start.1 = (bf16[4,40,1024]{2,1,0:T(8,128)(2,1)S(1)}, bf16[4,40,1024]{2,1,0:T(8,128)(2,1)S(1)}, u32[]{:S(2)}, u32[]{:S(2)}) collective-permute-start(bf16[4,40,1024]{2,1,0:T(8,128)(2,1)S(1)} %get-tuple-element.38), channel_id=1, source_target_pairs={{0,1},{1,0},{2,3},{3,2},{4,5},{5,4},{6,7},{7,6},{8,9},{9,8},{10,11... | collective-permute-start | bytes 983048 | tf_op jit(solution)/shard_map/ppermute | solution.py:292
  13.3 14.2 %collective-permute-start.2 = (bf16[4,40,1024]{2,1,0:T(8,128)(2,1)S(1)}, bf16[4,40,1024]{2,1,0:T(8,128)(2,1)S(1)}, u32[]{:S(2)}, u32[]{:S(2)}) collective-permute-start(bf16[4,40,1024]{2,1,0:T(8,128)(2,1)S(1)} %get-tuple-element.39), channel_id=1, source_target_pairs={{0,2},{1,3},{2,0},{3,1},{4,6},{5,7},{6,4},{7,5},{8,10},{9,11},{10,... | collective-permute-start | bytes 983048 | tf_op jit(solution)/shard_map/ppermute | solution.py:292
  14.5 27.8 %collective-permute-start.3 = (bf16[4,40,1024]{2,1,0:T(8,128)(2,1)S(1)}, bf16[4,40,1024]{2,1,0:T(8,128)(2,1)S(1)}, u32[]{:S(2)}, u32[]{:S(2)}) collective-permute-start(bf16[4,40,1024]{2,1,0:T(8,128)(2,1)S(1)} %get-tuple-element.40), channel_id=1, source_target_pairs={{0,3},{1,2},{2,1},{3,0},{4,7},{5,6},{6,5},{7,4},{8,11},{9,10},{10,... | collective-permute-start | bytes 983048 | tf_op jit(solution)/shard_map/ppermute | solution.py:292
  15.1 37.6 %collective-permute-start.4 = (bf16[512,768]{1,0:T(8,128)(2,1)}, bf16[512,768]{1,0:T(8,128)(2,1)}, u32[]{:S(2)}, u32[]{:S(2)}) collective-permute-start(bf16[512,768]{1,0:T(8,128)(2,1)} %get-tuple-element.46), channel_id=1, source_target_pairs={{0,16},{16,0},{1,17},{17,1},{2,18},{18,2},{3,19},{19,3},{4,20},{20... | collective-permute-start | bytes 2359304 | tf_op jit(solution)/shard_map/ppermute | solution.py:318
  43.5 15.6 %collective-permute-start.5 = (bf16[4,40,1024]{2,1,0:T(8,128)(2,1)}, bf16[4,40,1024]{2,1,0:T(8,128)(2,1)S(1)}, u32[]{:S(2)}, u32[]{:S(2)}) collective-permute-start(bf16[4,40,1024]{2,1,0:T(8,128)(2,1)} %get-tuple-element.42), channel_id=1, source_target_pairs={{0,4},{1,5},{2,6},{3,7},{4,0},{5,1},{6,2},{7,3},{8,12},{9,13},{10,... | collective-permute-start | bytes 983048 | tf_op jit(solution)/shard_map/ppermute | solution.py:292
  44.7 15.2 %collective-permute-start.6 = (bf16[4,40,1024]{2,1,0:T(8,128)(2,1)}, bf16[4,40,1024]{2,1,0:T(8,128)(2,1)S(1)}, u32[]{:S(2)}, u32[]{:S(2)}) collective-permute-start(bf16[4,40,1024]{2,1,0:T(8,128)(2,1)} %get-tuple-element.43), channel_id=1, source_target_pairs={{0,8},{1,9},{2,10},{3,11},{4,12},{5,13},{6,14},{7,15},{8,0},{9,1},... | collective-permute-start | bytes 983048 | tf_op jit(solution)/shard_map/ppermute | solution.py:292
  44.8 30.6 %collective-permute-start.7 = (bf16[4,40,1024]{2,1,0:T(8,128)(2,1)}, bf16[4,40,1024]{2,1,0:T(8,128)(2,1)}, u32[]{:S(2)}, u32[]{:S(2)}) collective-permute-start(bf16[4,40,1024]{2,1,0:T(8,128)(2,1)} %get-tuple-element.44), channel_id=1, source_target_pairs={{0,12},{1,13},{2,14},{3,15},{4,8},{5,9},{6,10},{7,11},{8,4},{9,5},... | collective-permute-start | bytes 983048 | tf_op jit(solution)/shard_map/ppermute | solution.py:292
  46.1 0.9 copy-start.5
  52.7 28.0 %collective-permute-start.8 = (bf16[2,320,768]{2,1,0:T(8,128)(2,1)S(1)}, bf16[2,320,768]{2,1,0:T(8,128)(2,1)S(1)}, u32[]{:S(2)}, u32[]{:S(2)}) collective-permute-start(bf16[2,320,768]{2,1,0:T(8,128)(2,1)S(1)} %shard_map.99), channel_id=1, source_target_pairs={{0,16},{16,0},{1,17},{17,1},{2,18},{18,2},{3,19},{19,3},{4,20},{20... | collective-permute-start | bytes 2949128 | tf_op jit(solution)/shard_map/ppermute | solution.py:392
  54.2 21.2 %copy-start.2 = (bf16[1,1024,768]{2,1,0:T(8,128)(2,1)S(1)}, bf16[1,1024,768]{2,1,0:T(8,128)(2,1)}, u32[]{:S(2)}) copy-start(bf16[1,1024,768]{2,1,0:T(8,128)(2,1)} %param.13) | copy-start | bytes 4718596
  54.2 21.2 %copy-start.6 = (bf16[512,768]{1,0:T(8,128)(2,1)S(1)}, bf16[512,768]{1,0:T(8,128)(2,1)}, u32[]{:S(2)}) copy-start(bf16[512,768]{1,0:T(8,128)(2,1)} %copy-done.5) | copy-start | bytes 2359300
  54.2 21.2 %copy-start.8 = (bf16[4,40,1024]{2,1,0:T(8,128)(2,1)S(1)}, bf16[4,40,1024]{2,1,0:T(8,128)(2,1)}, u32[]{:S(2)}) copy-start(bf16[4,40,1024]{2,1,0:T(8,128)(2,1)} %get-tuple-element.41) | copy-start | bytes 983044
  81.7 22.6 %collective-permute-start.16 = (bf16[2,320,768]{2,1,0:T(8,128)(2,1)S(1)}, bf16[2,320,768]{2,1,0:T(8,128)(2,1)S(1)}, u32[]{:S(2)}, u32[]{:S(2)}) collective-permute-start(bf16[2,320,768]{2,1,0:T(8,128)(2,1)S(1)} %get-tuple-element.51.d_ref), channel_id=1, source_target_pairs={{0,16},{16,0},{1,17},{17,1},{2,18},{18,2},{3,19},{19,3},{4,20},{20... | collective-permute-start | bytes 2949128 | tf_op jit(solution)/shard_map/ppermute | solution.py:426
  82.9 36.1 %collective-permute-start.9 = (bf16[320,1024]{1,0:T(8,128)(2,1)}, bf16[320,1024]{1,0:T(8,128)(2,1)S(1)}, u32[]{:S(2)}, u32[]{:S(2)}) collective-permute-start(bf16[320,1024]{1,0:T(8,128)(2,1)} %get-tuple-element.52), channel_id=1, source_target_pairs={{0,16},{16,0},{1,17},{17,1},{2,18},{18,2},{3,19},{19,3},{4,20},{20... | collective-permute-start | bytes 1966088 | tf_op jit(solution)/shard_map/ppermute | solution.py:428
  83.3 7.6 %copy-start = (bf16[1,1024,768]{2,1,0:T(8,128)(2,1)S(1)}, bf16[1,1024,768]{2,1,0:T(8,128)(2,1)}, u32[]{:S(2)}) copy-start(bf16[1,1024,768]{2,1,0:T(8,128)(2,1)} %param.11) | copy-start | bytes 4718596
  83.3 7.6 %copy-start.1 = (bf16[1,1024,768]{2,1,0:T(8,128)(2,1)S(1)}, bf16[1,1024,768]{2,1,0:T(8,128)(2,1)}, u32[]{:S(2)}) copy-start(bf16[1,1024,768]{2,1,0:T(8,128)(2,1)} %param.12) | copy-start | bytes 4718596
  87.5 0.7 copy-start.12
  88.3 18.7 %collective-permute-start.11 = (bf16[4,40,1024]{2,1,0:T(8,128)(2,1)S(1)}, bf16[4,40,1024]{2,1,0:T(8,128)(2,1)S(1)}, u32[]{:S(2)}, u32[]{:S(2)}) collective-permute-start(bf16[4,40,1024]{2,1,0:T(8,128)(2,1)S(1)} %get-tuple-element.56), channel_id=1, source_target_pairs={{0,8},{1,9},{2,10},{3,11},{4,12},{5,13},{6,14},{7,15},{8,0},{9,1},... | collective-permute-start | bytes 983048 | tf_op jit(solution)/shard_map/ppermute | solution.py:292
  88.3 30.7 %collective-permute-start.10 = (bf16[4,40,1024]{2,1,0:T(8,128)(2,1)}, bf16[4,40,1024]{2,1,0:T(8,128)(2,1)}, u32[]{:S(2)}, u32[]{:S(2)}) collective-permute-start(bf16[4,40,1024]{2,1,0:T(8,128)(2,1)} %get-tuple-element.55), channel_id=1, source_target_pairs={{0,4},{1,5},{2,6},{3,7},{4,0},{5,1},{6,2},{7,3},{8,12},{9,13},{10,... | collective-permute-start | bytes 983048 | tf_op jit(solution)/shard_map/ppermute | solution.py:292
  89.6 29.3 %collective-permute-start.12 = (bf16[4,40,1024]{2,1,0:T(8,128)(2,1)}, bf16[4,40,1024]{2,1,0:T(8,128)(2,1)}, u32[]{:S(2)}, u32[]{:S(2)}) collective-permute-start(bf16[4,40,1024]{2,1,0:T(8,128)(2,1)} %get-tuple-element.57), channel_id=1, source_target_pairs={{0,12},{1,13},{2,14},{3,15},{4,8},{5,9},{6,10},{7,11},{8,4},{9,5},... | collective-permute-start | bytes 983048 | tf_op jit(solution)/shard_map/ppermute | solution.py:292
  107.0 0.7 copy-start.9
  107.7 45.5 %all-to-all-start.1 = ((bf16[32,40,512]{2,1,0:T(8,128)(2,1)}), bf16[32,40,512]{2,1,0:T(8,128)(2,1)S(1)}, u32[]{:S(2)}, u32[]{:S(2)}) async-start(bf16[32,40,512]{2,1,0:T(8,128)(2,1)} %bitcast.16), calls=%async_computation.1 | async-start | bytes 2621440 | tf_op jit(solution)/shard_map/all_to_all | solution.py:462
  117.7 25.4 %collective-permute-start.17 = (bf16[320,768]{1,0:T(8,128)(2,1)S(1)}, bf16[320,768]{1,0:T(8,128)(2,1)}, u32[]{:S(2)}, u32[]{:S(2)}) collective-permute-start(bf16[320,768]{1,0:T(8,128)(2,1)S(1)} %get-tuple-element.53.hid_ref), channel_id=1, source_target_pairs={{0,16},{16,0},{1,17},{17,1},{2,18},{18,2},{3,19},{19,3},{4,20},{20... | collective-permute-start | bytes 1474568 | tf_op jit(solution)/shard_map/ppermute | solution.py:425
  119.0 1.0 copy-start.10
  119.9 1.0 copy-start.13
  123.1 24.5 %collective-permute-start.13 = (bf16[4,40,1024]{2,1,0:T(8,128)(2,1)}, bf16[4,40,1024]{2,1,0:T(8,128)(2,1)}, u32[]{:S(2)}, u32[]{:S(2)}) collective-permute-start(bf16[4,40,1024]{2,1,0:T(8,128)(2,1)} %get-tuple-element.63), channel_id=1, source_target_pairs={{0,1},{1,0},{2,3},{3,2},{4,5},{5,4},{6,7},{7,6},{8,9},{9,8},{10,11... | collective-permute-start | bytes 983048 | tf_op jit(solution)/shard_map/ppermute | solution.py:292
  124.1 23.5 %collective-permute-start.14 = (bf16[4,40,1024]{2,1,0:T(8,128)(2,1)}, bf16[4,40,1024]{2,1,0:T(8,128)(2,1)}, u32[]{:S(2)}, u32[]{:S(2)}) collective-permute-start(bf16[4,40,1024]{2,1,0:T(8,128)(2,1)} %get-tuple-element.64), channel_id=1, source_target_pairs={{0,2},{1,3},{2,0},{3,1},{4,6},{5,7},{6,4},{7,5},{8,10},{9,11},{10,... | collective-permute-start | bytes 983048 | tf_op jit(solution)/shard_map/ppermute | solution.py:292
  124.9 24.9 %collective-permute-start.15 = (bf16[4,40,1024]{2,1,0:T(8,128)(2,1)}, bf16[4,40,1024]{2,1,0:T(8,128)(2,1)}, u32[]{:S(2)}, u32[]{:S(2)}) collective-permute-start(bf16[4,40,1024]{2,1,0:T(8,128)(2,1)} %get-tuple-element.65), channel_id=1, source_target_pairs={{0,3},{1,2},{2,1},{3,0},{4,7},{5,6},{6,5},{7,4},{8,11},{9,10},{10,... | collective-permute-start | bytes 983048 | tf_op jit(solution)/shard_map/ppermute | solution.py:292
  143.1 6.7 %copy-start.11 = (bf16[4,40,1024]{2,1,0:T(8,128)(2,1)S(1)}, bf16[4,40,1024]{2,1,0:T(8,128)(2,1)}, u32[]{:S(2)}) copy-start(bf16[4,40,1024]{2,1,0:T(8,128)(2,1)} %get-tuple-element.62) | copy-start | bytes 983044
